TPU v7x, 256 devices: a whole 4x4x8 slice. The times are simulated.
256 devices in a mesh: role: 2 (over z_hi), expert: 32 (over y, x, core), tensor: 4 (over z_lo).
Axes of the slice: x: 4, y: 4, z: 8 (z_hi: 2, z_lo: 4; z = z_hi * 4 + z_lo), core: 2. Of those that a mesh axis runs over, the one named last changes fastest.
Arguments:
- request_latent_cache: bfloat16 [128, 4096, 576], P(('role', 'expert'), 'tensor'), may hold values from -6 to 6
- queries: bfloat16 [128, 128, 576], P(('role', 'expert')), may hold values from -32 to 32
- cache_lengths: int32 [128], P(('role', 'expert')), may hold values from 1024 to 4096, as said below
- residual_in: bfloat16 [128, 7168], P(('role', 'expert')), may hold values from -4 to 4
- value_up_weight: bfloat16 [128, 512, 128], P(('expert', 'tensor')), may hold values from -2 to 2
- out_proj: bfloat16 [16384, 7168], P(('expert', 'tensor')), may hold values from -0.046875 to 0.046875
- norm_gain: bfloat16 [7168], replicated, may hold values from 0.25 to 1.75
- gate_proj: bfloat16 [32, 7168, 1024], P('expert', None, ('role', 'tensor')), may hold values from -0.0625 to 0.0625
- up_proj: bfloat16 [32, 7168, 1024], P('expert', None, ('role', 'tensor')), may hold values from -0.0625 to 0.0625
- down_proj: bfloat16 [32, 1024, 7168], P('expert', ('role', 'tensor')), may hold values from -0.1875 to 0.1875
- expert_ids: int32 [128, 8], P(('role', 'expert')), may hold values from 0 to 31, all different within a row; in each aligned block of 128 rows (0 to 127, 128 to 255, ...) at most 64 rows name the same one
- route_weights: bfloat16 [128, 8], P(('role', 'expert')), may hold values from 0.099609375 to 0.59765625
Outputs:
- attended: float32 [128, 7168], P(('role', 'expert'))
- routed: float32 [128, 7168], P(('role', 'expert'))
Inputs may be any that keep to these rules, and one draw needn't show every extreme that they name: `cache_lengths`: slots below a request's length are live; some request uses all 4096. `expert_ids`: each token names 8 different experts; no expert is named by more than 64 tokens, a bound that some block reaches.
All inputs are finite; a program needn't handle non-finite values.
Results may differ from a plain program's by a relative error of at most 0.013.
Values may be sent and summed in bfloat16 or wider, within the bound.
No kernel may reach another device: no remote copies, remote signals or barrier semaphores. Data moves between devices by JAX's collectives and lax.ppermute only.
A program may use at most 64 MiB of HBM per device.

v0:
```python
import jax
import jax.numpy as jnp
from jax import lax
from jax.sharding import PartitionSpec as P

SCORE_SCALE = 192.0 ** (-0.5)


def shards(
    request_latent_cache,
    queries,
    cache_lengths,
    residual_in,
    value_up_weight,
    out_proj,
    norm_gain,
    gate_proj,
    up_proj,
    down_proj,
    expert_ids,
    route_weights,
):
    expert_count = lax.axis_size("expert")
    tensor_count = lax.axis_size("tensor")
    tensor_index = lax.axis_index("tensor")
    local_requests = request_latent_cache.shape[0]
    local_slots = request_latent_cache.shape[1]
    local_heads = value_up_weight.shape[0]
    latent_width = value_up_weight.shape[1]
    attention_logits = (
        jnp.einsum(
            "rhc,rsc->rhs", queries, request_latent_cache, preferred_element_type=jnp.float32
        )
        * SCORE_SCALE
    )
    position = tensor_index * local_slots + jnp.arange(local_slots, dtype=jnp.int32)
    live = (position[None, :] < cache_lengths[:, None])[:, None, :]
    masked = jnp.where(live, attention_logits, -1e30)
    row_top = lax.pmax(jnp.max(masked, axis=2), "tensor")
    expo = jnp.where(live, jnp.exp(masked - row_top[:, :, None]), 0.0)
    totals = jnp.sum(expo, axis=2)
    numer = jnp.einsum(
        "rhs,rsc->rhc",
        expo.astype(jnp.bfloat16),
        request_latent_cache[:, :, :latent_width],
        preferred_element_type=jnp.float32,
    )
    numer = numer.reshape(local_requests, expert_count, tensor_count, local_heads, latent_width)
    totals = totals.reshape(local_requests, expert_count, tensor_count, local_heads)
    numer_all, totals_all = lax.psum((numer, totals), "tensor")
    numer_mine = lax.dynamic_index_in_dim(numer_all, tensor_index, 2, keepdims=False)
    totals_mine = lax.dynamic_index_in_dim(totals_all, tensor_index, 2, keepdims=False)
    latent_context = (numer_mine / totals_mine[..., None]).astype(jnp.bfloat16)
    received_rows = lax.all_to_all(
        latent_context, "expert", split_axis=1, concat_axis=0, tiled=True
    )
    received_rows = received_rows.reshape(expert_count * local_requests, local_heads, latent_width)
    head_output_rows = jnp.einsum(
        "smz,mze->sme", received_rows, value_up_weight, preferred_element_type=jnp.float32
    ).astype(jnp.bfloat16)
    flat_heads = head_output_rows.reshape(head_output_rows.shape[0], -1)
    rows = flat_heads
    partial_attn = lax.psum_scatter(
        jnp.dot(rows, out_proj, preferred_element_type=jnp.float32),
        "expert",
        scatter_dimension=0,
        tiled=True,
    )
    attn_rows = lax.psum(partial_attn, "tensor")
    attended = attn_rows + residual_in.astype(jnp.float32)
    mean_square = jnp.mean(attended * attended, axis=1, keepdims=True)
    normed = (attended * lax.rsqrt(mean_square + 1e-06) * norm_gain.astype(jnp.float32)).astype(
        jnp.bfloat16
    )
    all_rows, all_ids, all_weights = (
        lax.all_gather(normed, ("role", "expert"), axis=0, tiled=True),
        lax.all_gather(expert_ids, ("role", "expert"), axis=0, tiled=True),
        lax.all_gather(route_weights, ("role", "expert"), axis=0, tiled=True),
    )
    local_experts = gate_proj.shape[0]
    first_expert = lax.axis_index("expert") * local_experts
    coef_weights = all_weights.astype(jnp.float32)
    rows = all_rows
    coef = jnp.sum(jnp.where(all_ids == first_expert + 0, coef_weights, 0.0), axis=1)
    gate = jnp.dot(rows, gate_proj[0], preferred_element_type=jnp.float32)
    upper = jnp.dot(rows, up_proj[0], preferred_element_type=jnp.float32)
    act = (jax.nn.silu(gate) * upper).astype(jnp.bfloat16)
    running = coef[:, None] * jnp.dot(act, down_proj[0], preferred_element_type=jnp.float32)
    columns = lax.psum_scatter(running, "tensor", scatter_dimension=1, tiled=True)
    owned = lax.psum_scatter(columns, ("role", "expert"), scatter_dimension=0, tiled=True)
    routed = lax.all_gather(owned, "tensor", axis=1, tiled=True)
    return (attended, routed)


def solution(mesh):
    placed = (
        P(("role", "expert"), "tensor", None),
        P(("role", "expert"), None, None),
        P(("role", "expert")),
        P(("role", "expert"), None),
        P(("expert", "tensor"), None, None),
        P(("expert", "tensor"), None),
        P(),
        P("expert", None, ("role", "tensor")),
        P("expert", None, ("role", "tensor")),
        P("expert", ("role", "tensor"), None),
        P(("role", "expert"), None),
        P(("role", "expert"), None),
    )
    return jax.shard_map(
        shards,
        mesh=mesh,
        in_specs=placed,
        out_specs=(P(("role", "expert"), None), P(("role", "expert"), None)),
        check_vma=False,
    )
```

profile of v0, /device:TPU:2, one launch (start us, length us, event | category | flops | bytes accessed | tf_op | source)
XLA Modules:
  0.0 1333.7 jit_solution(5151585416824068934)
XLA Ops:
  7.2 0.9 broadcast_compare_fusion
  8.1 2.5 fusion.36
  10.6 13.0 pmax.7
  23.6 2.4 fusion
  26.1 1.0 reshape.78
  27.1 0.3 fusion.17
  27.6 15.8 %psum.22 = f32[2,32,4,1]{2,1,0,3:T(8,128)S(1)} all-reduce(f32[2,32,4,1]{2,1,0,3:T(8,128)S(1)} %reshape.79), channel_id=1, replica_groups=mesh['role'=2,'expert'=32,'tensor'=4] {'tensor'}, use_global_device_ids=true, to_apply=%region_4.5 | all-reduce | flops 256 | bytes 2048 | tf_op jit(solution)/shard_map/psum | solution.py:50
  43.4 0.3 copy.24
  43.7 36.1 %all-reduce.6.cloned.1.call-done = f32[2,32,4,1,512]{4,2,1,0,3:T(4,128)} async-done(((f32[2,32,4,1,512]{4,2,1,0,3:T(4,128)}), f32[2,32,4,1,512]{4,2,1,0,3:T(4,128)}) %all-reduce.6.cloned.1.call-update) | async-done | bytes 524304 | tf_op jit(solution)/shard_map/psum | solution.py:50
  79.8 1.2 constant_dynamic-slice_fusion.3
  81.0 0.2 fusion.25
  81.2 13.5 %all_to_all.15 = bf16[2,32,1,512]{3,0,2,1:T(2,128)(2,1)S(1)} all-to-all(bf16[2,32,1,512]{3,0,2,1:T(2,128)(2,1)S(1)} %fusion.25), channel_id=1, replica_groups=mesh['role'=2,'expert'=32,'tensor'=4] {'expert'}, dimensions={1} | all-to-all | bytes 131072 | tf_op jit(solution)/shard_map/all_to_all | solution.py:54
  94.7 3.3 fusion.16
  98.1 0.6 copy-done.4
  98.7 0.6 dynamic-slice
  99.9 110.0 %all-reduce.8.cloned.1.call-done = f32[64,7168]{1,0:T(8,128)} async-done(((f32[64,7168]{1,0:T(8,128)}), f32[64,7168]{1,0:T(8,128)}) %all-reduce.8.cloned.1.call-update) | async-done | bytes 1835024
  209.9 1.0 constant_dynamic-slice_fusion.1
  210.9 19.8 %psum.23 = f32[2,7168]{1,0:T(2,128)S(1)} all-reduce(f32[2,7168]{1,0:T(2,128)S(1)} %constant_dynamic-slice_fusion.1), channel_id=1, replica_groups=mesh['role'=2,'expert'=32,'tensor'=4] {'tensor'}, use_global_device_ids=true, to_apply=%region_6.7 | all-reduce | flops 14336 | bytes 114688 | tf_op jit(solution)/shard_map/psum | solution.py:69
  230.7 0.2 multiply_reduce_fusion
  230.9 0.7 fusion.33
  231.7 108.4 %all-gather.1 = bf16[64,2,8]{2,1,0:T(2,128)(2,1)S(1)} all-gather(bf16[1,2,8]{2,1,0:T(2,128)(2,1)S(1)} %bitcast.44), channel_id=1, replica_groups=mesh['role'=2,'expert'=32,'tensor'=4] {'role','expert'}, dimensions={0}, use_global_device_ids=true | all-gather | bytes 2080 | tf_op jit(solution)/shard_map/all_gather | solution.py:78
  340.2 113.0 %all-gather = s32[64,2,8]{2,1,0:T(2,128)S(1)} all-gather(s32[1,2,8]{2,1,0:T(2,128)S(1)} %bitcast.43), channel_id=1, replica_groups=mesh['role'=2,'expert'=32,'tensor'=4] {'role','expert'}, dimensions={0}, use_global_device_ids=true | all-gather | bytes 4160 | tf_op jit(solution)/shard_map/all_gather | solution.py:77
  453.2 0.1 fusion.26
  453.5 4.9 reshape.87
  458.5 2.7 fusion.5
  461.1 5.1 convolution_multiply_fusion
  466.3 71.6 %reduce-scatter.2.cloned.1.call-done = f32[128,1792]{1,0:T(8,128)} async-done(((f32[128,7168]{1,0:T(8,128)}), f32[128,1792]{1,0:T(8,128)}) %reduce-scatter.2.cloned.1.call-update) | async-done | bytes 917520 | tf_op jit(solution)/shard_map/reduce_scatter | solution.py:89
  538.0 0.6 dynamic-slice.2
  539.2 773.5 %all-reduce.10.cloned.1.call-done = f32[128,1792]{1,0:T(8,128)} async-done(((f32[128,1792]{1,0:T(8,128)}), f32[128,1792]{1,0:T(8,128)}) %all-reduce.10.cloned.1.call-update) | async-done | bytes 917520
  1312.7 0.8 constant_dynamic-slice_fusion
  1313.5 13.1 all_gather.15
  1326.6 0.6 copy.33
  (35 shorter events, 0.7 us)
Async XLA Ops:
  7.2 454.0 %copy-start = (bf16[1,128,7168]{2,1,0:T(8,128)(2,1)S(1)}, bf16[1,128,7168]{2,1,0:T(8,128)(2,1)}, u32[]{:S(2)}) copy-start(bf16[1,128,7168]{2,1,0:T(8,128)(2,1)} %param.21) | copy-start | bytes 5505028
  7.2 72.6 %all-reduce.6.cloned.1.call-start = ((), (), s32[]{:S(2)}) async-start(), calls=%async_computation.2 | async-start | bytes 1048576 | tf_op jit(solution)/shard_map/psum | solution.py:50
  26.1 68.6 %copy-start.2 = (bf16[1,512,128]{2,1,0:T(8,128)(2,1)S(1)}, bf16[1,512,128]{2,1,0:T(8,128)(2,1)}, u32[]{:S(2)}) copy-start(bf16[1,512,128]{2,1,0:T(8,128)(2,1)} %param.16) | copy-start | bytes 393220
  27.1 182.8 %all-reduce.8.cloned.1.call-start = ((), (), s32[]{:S(2)}) async-start(), calls=%async_computation.5 | async-start | bytes 3670016
  98.0 0.7 copy-start.4
  98.0 0.7 copy-start.8
  98.0 132.7 %copy-start.3 = (bf16[2,7168]{1,0:T(2,128)(2,1)S(1)}, bf16[2,7168]{1,0:T(2,128)(2,1)}, u32[]{:S(2)}) copy-start(bf16[2,7168]{1,0:T(2,128)(2,1)} %param.15) | copy-start | bytes 86020
  98.0 133.7 %copy-start.6 = (bf16[2,8]{1,0:T(2,128)(2,1)S(1)}, bf16[2,8]{1,0:T(2,128)(2,1)}, u32[]{:S(2)}) copy-start(bf16[2,8]{1,0:T(2,128)(2,1)} %param.23) | copy-start | bytes 100
  98.0 242.2 %copy-start.5 = (s32[2,8]{1,0:T(2,128)S(1)}, s32[2,8]{1,0:T(2,128)}, u32[]{:S(2)}) copy-start(s32[2,8]{1,0:T(2,128)} %param.22) | copy-start | bytes 196
  98.0 355.5 %all-gather.5.cloned.1.call-start = ((), (), s32[]{:S(2)}) async-start(), calls=%async_computation.4 | async-start | bytes 1863680 | tf_op jit(solution)/shard_map/all_gather | solution.py:76
  230.9 227.5 %copy-start.1 = (f32[2,7168]{1,0:T(2,128)}, f32[2,7168]{1,0:T(2,128)S(1)}, u32[]{:S(2)}) copy-start(f32[2,7168]{1,0:T(2,128)S(1)} %get-tuple-element.8) | copy-start | bytes 172036
  231.7 306.3 %reduce-scatter.2.cloned.1.call-start = ((), (), s32[]{:S(2)}) async-start(), calls=%async_computation.3 | async-start | bytes 4587520 | tf_op jit(solution)/shard_map/reduce_scatter | solution.py:89
  466.2 71.7 %copy-start.7 = (u32[256]{0:T(256)S(1)}, u32[256]{0:T(256)}, u32[]{:S(2)}) copy-start(u32[256]{0:T(256)} %constant.53) | copy-start | bytes 3076
  466.2 846.4 %all-reduce.10.cloned.1.call-start = ((), (), s32[]{:S(2)}) async-start(), calls=%async_computation.6 | async-start | bytes 1835008
Sparse Core Ops, SparseCore 0:
  27.2 52.5 all-reduce.5
  98.1 111.7 all-reduce.7
  231.8 77.8 all-gather.4
  466.4 71.5 reduce-scatter.1
  540.4 772.2 all-reduce.9
where the time goes:
time: 1340 us; the launch traced here: 1330 us
  waiting for transfers between devices  991 us (74%)
  blocking collectives  297 us (22%)
  matrix products  16 us (1%)
  between operations  15.3 us (1%)
    unnamed x7, waiting for transfers between devices  884 us
    all_gather x1, blocking collectives, shards(): lax.all_gather(expert_ids, ('role', 'expert'), axis=0, tiled=True)  113 us
    all_gather x1, blocking collectives, shards(): lax.all_gather(route_weights, ('role', 'expert'), axis=0, tiled=True)  108 us
    reduce_scatter x1, waiting for transfers between devices, shards(): lax.psum_scatter(running, 'tensor', scatter_dimension=1, tiled=True)  71.6 us
    psum x1, waiting for transfers between devices, shards(): numer_all, totals_all = lax.psum((numer, totals), 'tensor')  36.1 us
  transfers between devices with their start and end apart: 5, of which 4 were waited for; matrix products, arithmetic and copies ran while one was open for 0% of the time, Pallas kernels for 0%

commit v1 on v0

v1 whole, which is shorter than its diff:
```python
import jax
import jax.numpy as jnp
from jax import lax
from jax.sharding import PartitionSpec as P

SCORE_SCALE = 192.0 ** (-0.5)
SIDE = 4
BF = jnp.bfloat16
F32 = jnp.float32


def plane(value, down=0, right=0, core=0):
    pairs = []
    for y in range(SIDE):
        for x in range(SIDE):
            for c in range(2):
                there = ((y + down) % SIDE) * 2 * SIDE + ((x + right) % SIDE) * 2 + (c ^ core)
                pairs.append((y * 2 * SIDE + x * 2 + c, there))
    return lax.ppermute(value, "expert", pairs)


def along(value, step):
    return lax.ppermute(value, "tensor", [(i, (i + step) % 4) for i in range(4)])


def swap(value, bit):
    return lax.ppermute(value, "tensor", [(i, i ^ bit) for i in range(4)])


def other_role(value):
    return lax.ppermute(value, "role", [(0, 1), (1, 0)])


def scatter_sum(acc, **_):
    for axis in ("down", "right"):
        n = acc.shape[0] // SIDE
        sent = acc.astype(BF)
        got = [plane(sent[s * n : (s + 1) * n], **{axis: s}) for s in (2, 1, 3)]
        acc = acc[:n]
        for g in got:
            acc = acc + g.astype(F32)
    return acc


def tensor_sum(value):
    value = value + swap(value, 1)
    return value + swap(value, 2)


def shards(
    request_latent_cache,
    queries,
    cache_lengths,
    residual_in,
    value_up_weight,
    out_proj,
    norm_gain,
    gate_proj,
    up_proj,
    down_proj,
    expert_ids,
    route_weights,
):
    t = lax.axis_index("tensor")
    e = lax.axis_index("expert")
    y, x, c = e // (2 * SIDE), (e // 2) % SIDE, e % 2
    local_requests, local_slots, _ = request_latent_cache.shape
    latent = value_up_weight.shape[1]
    experts = 32

    q = queries.reshape(local_requests, experts, 4, -1)
    q = jnp.take(q, (t + jnp.arange(4)) % 4, axis=2)
    q = jnp.swapaxes(q, 1, 2).reshape(local_requests, 4 * experts, -1)
    logits = (
        jnp.einsum("rhc,rsc->rhs", q, request_latent_cache, preferred_element_type=F32)
        * SCORE_SCALE
    )
    position = t * local_slots + jnp.arange(local_slots, dtype=jnp.int32)
    live = (position[None, :] < cache_lengths[:, None])[:, None, :]
    masked = jnp.where(live, logits, -1e30)
    top = jnp.max(masked, axis=2)
    expo = jnp.where(live, jnp.exp(masked - top[:, :, None]), 0.0)
    total = jnp.sum(expo, axis=2)
    numer = jnp.einsum(
        "rhs,rsc->rhc",
        expo.astype(BF),
        request_latent_cache[:, :, :latent],
        preferred_element_type=F32,
    )
    part = (numer / jnp.maximum(total, 1.0)[:, :, None]).astype(BF)
    part = part.reshape(local_requests, 4, experts, latent)
    stats = jnp.stack([top, total]).reshape(2, local_requests, 4, experts)
    stats_of = [stats[:, :, 0]] + [along(stats[:, :, s], s) for s in (1, 2, 3)]
    parts = [part[:, 0]] + [along(part[:, s], s) for s in (1, 2, 3)]
    tops = jnp.maximum(
        jnp.maximum(stats_of[0][0], stats_of[1][0]), jnp.maximum(stats_of[2][0], stats_of[3][0])
    )
    weights = [jnp.exp(s[0] - tops) * s[1] for s in stats_of]
    whole = weights[0] + weights[1] + weights[2] + weights[3]
    context = sum(
        (w / whole)[:, :, None] * p.astype(F32) for w, p in zip(weights, parts)
    ).astype(BF)
    context = jnp.swapaxes(context, 0, 1)
    rows = lax.all_to_all(context, "expert", 0, 0, tiled=True)
    rows = rows.reshape(experts * local_requests, latent)
    heads = jnp.dot(rows, value_up_weight[0], preferred_element_type=F32).astype(BF)

    n_rows = heads.shape[0]
    r = jnp.arange(n_rows)
    dc, dy, dx, k = r // 32, (r // 8) % 4, (r // 2) % 4, r % 2
    source = (((y + dy) % 4) * 8 + ((x + dx) % 4) * 2 + (c ^ dc)) * 2 + k
    pick = (source[:, None] == jnp.arange(n_rows)[None, :]).astype(BF)
    heads = jnp.dot(pick, heads, preferred_element_type=F32).astype(BF)
    half = n_rows // 2
    away = jnp.dot(heads[half:], out_proj, preferred_element_type=F32).astype(BF)
    away = plane(away, core=1)
    acc = jnp.dot(heads[:half], out_proj, preferred_element_type=F32) + away.astype(F32)
    attended = tensor_sum(scatter_sum(acc)) + residual_in.astype(F32)

    mean_square = jnp.mean(attended * attended, axis=1, keepdims=True)
    normed = (attended * lax.rsqrt(mean_square + 1e-06) * norm_gain.astype(F32)).astype(BF)
    names = jnp.arange(128, dtype=jnp.int32)
    table = jnp.sum(
        jnp.where(
            expert_ids[:, :, None] == names[None, None, :],
            route_weights.astype(F32)[:, :, None],
            0.0,
        ),
        axis=1,
    ).astype(BF)
    block = jnp.concatenate([normed, table], axis=1)
    block = jnp.concatenate([block, other_role(block)], axis=0)
    for axis in ("right", "down"):
        got = {s: plane(block, **{axis: -s}) for s in (2, 1, 3)}
        block = jnp.concatenate([block, got[1], got[2], got[3]], axis=0)
    across = plane(block, core=1)

    width = normed.shape[1]

    def expert_rows(block):
        rows = block[:, :width]
        coef = jnp.sum(
            jnp.where(names[None, :] == e, block[:, width:].astype(F32), 0.0), axis=1
        )
        gate = jnp.dot(rows, gate_proj[0], preferred_element_type=F32)
        upper = jnp.dot(rows, up_proj[0], preferred_element_type=F32)
        act = (jax.nn.silu(gate) * upper).astype(BF)
        return coef[:, None] * jnp.dot(act, down_proj[0], preferred_element_type=F32)

    sent = plane(expert_rows(across).astype(BF), core=1)
    acc = scatter_sum(expert_rows(block) + sent.astype(F32))
    keep = acc.shape[0] // 2
    acc = acc[:keep] + other_role(acc[keep:].astype(BF)).astype(F32)
    routed = tensor_sum(acc)
    return (attended, routed)


def solution(mesh):
    placed = (
        P(("role", "expert"), "tensor", None),
        P(("role", "expert"), None, None),
        P(("role", "expert")),
        P(("role", "expert"), None),
        P(("expert", "tensor"), None, None),
        P(("expert", "tensor"), None),
        P(),
        P("expert", None, ("role", "tensor")),
        P("expert", None, ("role", "tensor")),
        P("expert", ("role", "tensor"), None),
        P(("role", "expert"), None),
        P(("role", "expert"), None),
    )
    return jax.shard_map(
        shards,
        mesh=mesh,
        in_specs=placed,
        out_specs=(P(("role", "expert"), None), P(("role", "expert"), None)),
        check_vma=False,
    )
```

time: 1340 us -> 162 us (0.12)
  waiting for transfers between devices: 991 us -> 76.1 us
  blocking collectives: 297 us -> 0 us
  starting transfers between devices: 0.21 us -> 52.3 us
  between operations: 15.3 us -> 1.06 us
    unnamed x7 -> x0, waiting for transfers between devices: 884 us -> none
    all_gather x3 -> x0, blocking collectives: 235 us -> none  [the longest x1 113 us: shards(): lax.all_gather(expert_ids, ('role', 'expert'), axis=0, tiled=True)]
    reduce_scatter x1 -> x0, waiting for transfers between devices: 71.6 us -> none  [shards(): lax.psum_scatter(running, 'tensor', scatter_dimension=1, tiled=True)]
    ppermute x0 -> x33, waiting for transfers between devices: none -> 69.8 us  [the longest x21 39.7 us: plane(): return lax.ppermute(value, 'expert', pairs)]
    ppermute x0 -> x33, starting transfers between devices: none -> 44.7 us  [the longest x21 23.4 us: plane(): return lax.ppermute(value, 'expert', pairs)]
    psum x1 -> x0, waiting for transfers between devices: 36.1 us -> none  [shards(): numer_all, totals_all = lax.psum((numer, totals), 'tensor')]
    psum x2 -> x0, blocking collectives: 35.6 us -> none  [the longest x1 19.8 us: shards(): attn_rows = lax.psum(partial_attn, 'tensor')]
    all_to_all x1 -> x0, blocking collectives: 13.5 us -> none  [shards(): lax.all_to_all(latent_context, 'expert', split_axis=1, concat_axis=0, til...]
  transfers between devices with their start and end apart: 5 -> 34, of which waited for: 4 -> 29; matrix products, arithmetic and copies ran while one was open for 0% -> 3% of each run, Pallas kernels for 0% -> 0%
where the time goes in v1:
time: 162 us; the launch traced here: 160 us
  waiting for transfers between devices  76.1 us (47%)
  starting transfers between devices  52.3 us (32%)
  matrix products  19.3 us (12%)
  local copies, waits for them, and re-layouts  6.89 us (4%)
  other arithmetic  4.17 us (3%)
    ppermute x21, waiting for transfers between devices, plane(): return lax.ppermute(value, 'expert', pairs)  39.7 us
    ppermute x21, starting transfers between devices, plane(): return lax.ppermute(value, 'expert', pairs)  23.4 us
    ppermute x4, waiting for transfers between devices, swap(): return lax.ppermute(value, 'tensor', [(i, i ^ bit) for i in range(4)])  18.9 us
    ppermute x6, starting transfers between devices, along(): lax.ppermute(value, 'tensor', [(i, (i + step) % 4) for i in range(4)])  10.9 us
    ppermute x2, starting transfers between devices, other_role(): return lax.ppermute(value, 'role', [(0, 1), (1, 0)])  9.77 us
    dot_general x2, matrix products, expert_rows(): jnp.dot(act, down_proj[0], preferred_element_type=F32)  7.82 us
    all_to_all x1, starting transfers between devices, shards(): rows = lax.all_to_all(context, 'expert', 0, 0, tiled=True)  7.62 us
    all_to_all x1, waiting for transfers between devices, shards(): rows = lax.all_to_all(context, 'expert', 0, 0, tiled=True)  6.27 us
  transfers between devices with their start and end apart: 34, of which 29 were waited for; matrix products, arithmetic and copies ran while one was open for 3% of the time, Pallas kernels for 0%

profile of v1, /device:TPU:2, one launch (start us, length us, event | category | flops | bytes accessed | tf_op | source)
XLA Modules:
  0.0 159.8 jit_solution(13153694512623983409)
XLA Ops:
  3.2 2.4 %fusion.110 = (f32[2,128]{1,0:T(2,128)S(1)}, f32[2,128,1024]{2,1,0:T(8,128)S(1)}) fusion(bf16[2,128,576]{2,1,0:T(8,128)(2,1)S(1)} %bitcast.134, bf16[2,1024,576]{1,2,0:T(8,128)(2,1)} %param.12, pred[2,1024]{1,0:T(4,128)(4,1)S(1)} %broadcast_compare_fusion), kind=kOutput, calls=%fused_computation.163 | convolution fusion | flops 302776064 | bytes 3705856 | tf_op jit(solution)/shard_map/rhc,rsc->rhs/dot_general | solution.py:75
  6.1 4.7 %collective-permute-start.2 = (f32[2,2,32]{2,1,0:T(2,128)S(1)}, f32[2,2,32]{2,1,0:T(2,128)S(1)}, u32[]{:S(2)}, u32[]{:S(2)}) collective-permute-start(f32[2,2,32]{2,1,0:T(2,128)S(1)} %bitcast.143), channel_id=1, source_target_pairs={{0,3},{1,0},{2,1},{3,2},{4,7},{5,4},{6,5},{7,6},{8,11},{9,8},{10,9... | collective-permute-start | bytes 1544 | tf_op jit(solution)/shard_map/ppermute | solution.py:23
  11.5 2.5 %fusion.17 = bf16[2,128,512]{2,1,0:T(8,128)(2,1)S(1)} fusion(bf16[2,1024,576]{1,2,0:T(8,128)(2,1)} %param.12, f32[2,128,1024]{2,1,0:T(8,128)S(1)} %get-tuple-element.36, f32[2,128]{1,0:T(2,128)S(1)} %get-tuple-element.35, pred[2,1024]{1,0:T(4,128)(4,1)S(1)} %broadcast_compare_fusion, f32[2,128]{1,0:T(2,128)S(1)} %broadcast_maximum_fusion), kind=kOutput, calls=%fused_computation.21 | convolution fusion | flops 269484032 | bytes 3411968 | tf_op jit(solution)/shard_map/rhs,rsc->rhc/dot_general | solution.py:84
  14.0 3.2 %collective-permute-start.5 = (bf16[2,32,512]{2,0,1:T(2,128)(2,1)S(1)}, bf16[2,32,512]{2,0,1:T(2,128)(2,1)S(1)}, u32[]{:S(2)}, u32[]{:S(2)}) collective-permute-start(bf16[2,32,512]{2,0,1:T(2,128)(2,1)S(1)} %bitcast.136), channel_id=1, source_target_pairs={{0,3},{1,0},{2,1},{3,2},{4,7},{5,4},{6,5},{7,6},{8,11},{9,8},{10,9... | collective-permute-start | bytes 196616 | tf_op jit(solution)/shard_map/ppermute | solution.py:23
  20.1 3.5 %collective-permute-done.3 = bf16[2,32,512]{2,0,1:T(2,128)(2,1)S(1)} collective-permute-done((bf16[2,32,512]{2,0,1:T(2,128)(2,1)S(1)}, bf16[2,32,512]{2,0,1:T(2,128)(2,1)S(1)}, u32[]{:S(2)}, u32[]{:S(2)}) %collective-permute-start.3) | collective-permute-done | bytes 65568 | tf_op jit(solution)/shard_map/ppermute | solution.py:23
  26.3 7.6 %all-to-all-start = ((bf16[32,2,512]{2,1,0:T(2,128)(2,1)}), bf16[32,2,512]{2,1,0:T(2,128)(2,1)S(1)}, u32[]{:S(2)}, u32[]{:S(2)}) async-start(bf16[32,2,512]{2,1,0:T(2,128)(2,1)} %fusion.44), calls=%async_computation | async-start | bytes 131072 | tf_op jit(solution)/shard_map/all_to_all | solution.py:104
  33.9 6.3 %all-to-all-done = bf16[32,2,512]{2,1,0:T(2,128)(2,1)S(1)} async-done(((bf16[32,2,512]{2,1,0:T(2,128)(2,1)}), bf16[32,2,512]{2,1,0:T(2,128)(2,1)S(1)}, u32[]{:S(2)}, u32[]{:S(2)}) %all-to-all-start) | async-done | bytes 65568 | tf_op jit(solution)/shard_map/all_to_all | solution.py:104
  40.5 2.0 %convolution_convert_fusion = bf16[32,7168]{1,0:T(8,128)(2,1)S(1)} fusion(bf16[128,7168]{1,0:T(8,128)(2,1)} %param.17, bf16[64,128]{1,0:T(8,128)(2,1)S(1)} %convolution_convert_fusion.1), kind=kOutput, calls=%fused_computation.2 | convolution fusion | flops 58949632 | bytes 2301952 | tf_op jit(solution)/shard_map/dot_general | solution.py:115
  46.2 2.0 %collective-permute-start.9 = (bf16[8,7168]{1,0:T(8,128)(2,1)S(1)}, bf16[8,7168]{1,0:T(8,128)(2,1)S(1)}, u32[]{:S(2)}, u32[]{:S(2)}) collective-permute-start(bf16[8,7168]{1,0:T(8,128)(2,1)S(1)} %get-tuple-element.17), channel_id=1, source_target_pairs={{0,96},{4,100},{8,104},{12,108},{16,112},{20,116},{24,120},{28,124... | collective-permute-start | bytes 344072 | tf_op jit(solution)/shard_map/ppermute | solution.py:19
  48.3 4.2 %collective-permute-done.7 = bf16[8,7168]{1,0:T(8,128)(2,1)S(1)} collective-permute-done((bf16[8,7168]{1,0:T(8,128)(2,1)S(1)}, bf16[8,7168]{1,0:T(8,128)(2,1)S(1)}, u32[]{:S(2)}, u32[]{:S(2)}) %collective-permute-start.7) | collective-permute-done | bytes 114720 | tf_op jit(solution)/shard_map/ppermute | solution.py:19
  61.6 4.0 %collective-permute-done.13 = f32[2,7168]{1,0:T(2,128)S(1)} collective-permute-done((f32[2,7168]{1,0:T(2,128)S(1)}, f32[2,7168]{1,0:T(2,128)S(1)}, u32[]{:S(2)}, u32[]{:S(2)}) %collective-permute-start.13) | collective-permute-done | bytes 57376 | tf_op jit(solution)/shard_map/ppermute | solution.py:27
  65.9 5.4 %collective-permute-done.14 = f32[2,7168]{1,0:T(2,128)S(1)} collective-permute-done((f32[2,7168]{1,0:T(2,128)S(1)}, f32[2,7168]{1,0:T(2,128)S(1)}, u32[]{:S(2)}, u32[]{:S(2)}) %collective-permute-start.14) | collective-permute-done | bytes 57376 | tf_op jit(solution)/shard_map/ppermute | solution.py:27
  71.7 4.9 %collective-permute-start.15 = (bf16[2,7296]{1,0:T(2,128)(2,1)S(1)}, bf16[2,7296]{1,0:T(2,128)(2,1)S(1)}, u32[]{:S(2)}, u32[]{:S(2)}) collective-permute-start(bf16[2,7296]{1,0:T(2,128)(2,1)S(1)} %pad_maximum_fusion.1), channel_id=1, source_target_pairs={{0,128},{128,0},{1,129},{129,1},{2,130},{130,2},{3,131},{131,3},{4... | collective-permute-start | bytes 87560 | tf_op jit(solution)/shard_map/ppermute | solution.py:31
  76.5 3.0 %collective-permute-done.15 = bf16[2,7296]{1,0:T(2,128)(2,1)S(1)} collective-permute-done((bf16[2,7296]{1,0:T(2,128)(2,1)S(1)}, bf16[2,7296]{1,0:T(2,128)(2,1)S(1)}, u32[]{:S(2)}, u32[]{:S(2)}) %collective-permute-start.15) | collective-permute-done | bytes 29216 | tf_op jit(solution)/shard_map/ppermute | solution.py:31
  80.6 4.5 %collective-permute-start.17 = (bf16[4,7296]{1,0:T(4,128)(2,1)S(1)}, bf16[4,7296]{1,0:T(4,128)(2,1)S(1)}, u32[]{:S(2)}, u32[]{:S(2)}) collective-permute-start(bf16[4,7296]{1,0:T(4,128)(2,1)S(1)} %pad_maximum_fusion), channel_id=1, source_target_pairs={{0,16},{4,20},{8,24},{12,28},{16,0},{20,4},{24,8},{28,12},{32,48},... | collective-permute-start | bytes 175112 | tf_op jit(solution)/shard_map/ppermute | solution.py:19
  85.1 2.1 %collective-permute-done.17 = bf16[4,7296]{1,0:T(4,128)(2,1)S(1)} collective-permute-done((bf16[4,7296]{1,0:T(4,128)(2,1)S(1)}, bf16[4,7296]{1,0:T(4,128)(2,1)S(1)}, u32[]{:S(2)}, u32[]{:S(2)}) %collective-permute-start.17) | collective-permute-done | bytes 58400 | tf_op jit(solution)/shard_map/ppermute | solution.py:19
  87.2 2.0 %collective-permute-done.16 = bf16[4,7296]{1,0:T(4,128)(2,1)S(1)} collective-permute-done((bf16[4,7296]{1,0:T(4,128)(2,1)S(1)}, bf16[4,7296]{1,0:T(4,128)(2,1)S(1)}, u32[]{:S(2)}, u32[]{:S(2)}) %collective-permute-start.16) | collective-permute-done | bytes 58400 | tf_op jit(solution)/shard_map/ppermute | solution.py:19
  89.5 2.2 %collective-permute-start.20 = (bf16[16,7296]{1,0:T(8,128)(2,1)S(1)}, bf16[16,7296]{1,0:T(8,128)(2,1)S(1)}, u32[]{:S(2)}, u32[]{:S(2)}) collective-permute-start(bf16[16,7296]{1,0:T(8,128)(2,1)S(1)} %concatenate.17), channel_id=1, source_target_pairs={{0,64},{4,68},{8,72},{12,76},{16,80},{20,84},{24,88},{28,92},{32,9... | collective-permute-start | bytes 700424 | tf_op jit(solution)/shard_map/ppermute | solution.py:19
  92.8 6.5 %collective-permute-done.21 = bf16[16,7296]{1,0:T(8,128)(2,1)S(1)} collective-permute-done((bf16[16,7296]{1,0:T(8,128)(2,1)S(1)}, bf16[16,7296]{1,0:T(8,128)(2,1)S(1)}, u32[]{:S(2)}, u32[]{:S(2)}) %collective-permute-start.21) | collective-permute-done | bytes 233504 | tf_op jit(solution)/shard_map/ppermute | solution.py:19
  101.8 2.5 %collective-permute-done.22 = bf16[64,7296]{1,0:T(8,128)(2,1)S(1)} collective-permute-done((bf16[64,7296]{1,0:T(8,128)(2,1)S(1)}, bf16[64,7296]{1,0:T(8,128)(2,1)S(1)}, u32[]{:S(2)}, u32[]{:S(2)}) %collective-permute-start.22) | collective-permute-done | bytes 933920 | tf_op jit(solution)/shard_map/ppermute | solution.py:19
  105.2 2.0 %fusion.5 = f32[64,128]{1,0:T(8,128)S(1)} fusion(bf16[1,7168,128]{2,1,0:T(8,128)(2,1)} %param.20, bf16[64,7296]{1,0:T(8,128)(2,1)S(1)} %collective-permute-done.22), kind=kOutput, calls=%fused_computation.8 | convolution fusion | flops 117440512 | bytes 2785280 | tf_op jit(solution)/shard_map/dot_general | solution.py:146
  107.2 3.6 %multiply_convert_fusion = bf16[64,7168]{1,0:T(8,128)(2,1)} fusion(f32[64]{0:T(128)S(1)} %get-tuple-element.3, bf16[1,128,7168]{2,1,0:T(8,128)(2,1)S(1)} %copy-done, f32[64,128]{1,0:T(8,128)S(1)} %fusion.5, bf16[1,7168,128]{2,1,0:T(8,128)(2,1)} %param.19, bf16[64,7296]{1,0:T(8,128)(2,1)} %copy-done.2), kind=kOutput, calls=%fused_computation.17 | convolution fusion | flops 235847680 | bytes 5538048 | tf_op jit(solution)/shard_map/dot_general | solution.py:148
  113.6 4.2 %fusion.112 = (bf16[64,7168]{1,0:T(8,128)(2,1)}, f32[64,7168]{1,0:T(8,128)}) fusion(bf16[64,7168]{1,0:T(8,128)(2,1)} %collective-permute-done.23, bf16[1,128,7168]{2,1,0:T(8,128)(2,1)S(1)} %copy-done, f32[64,128]{1,0:T(8,128)S(1)} %fusion.7, bf16[1,7168,128]{2,1,0:T(8,128)(2,1)} %param.19, bf16[64,7296]{1,0:T(8,128)(2,1)S(1)} %concatenate.18, ...), kind=kOutput, calls=%fused_computation.165 | convolution fusion | flops 236765184 | bytes 8290816 | tf_op jit(solution)/shard_map/dot_general | solution.py:148
  119.7 2.1 %collective-permute-start.26 = (bf16[16,7168]{1,0:T(8,128)(2,1)S(1)}, bf16[16,7168]{1,0:T(8,128)(2,1)S(1)}, u32[]{:S(2)}, u32[]{:S(2)}) collective-permute-start(bf16[16,7168]{1,0:T(8,128)(2,1)S(1)} %get-tuple-element.14), channel_id=1, source_target_pairs={{0,96},{4,100},{8,104},{12,108},{16,112},{20,116},{24,120},{28,124... | collective-permute-start | bytes 688136 | tf_op jit(solution)/shard_map/ppermute | solution.py:19
  122.3 6.8 %collective-permute-done.24 = bf16[16,7168]{1,0:T(8,128)(2,1)S(1)} collective-permute-done((bf16[16,7168]{1,0:T(8,128)(2,1)S(1)}, bf16[16,7168]{1,0:T(8,128)(2,1)S(1)}, u32[]{:S(2)}, u32[]{:S(2)}) %collective-permute-start.24) | collective-permute-done | bytes 229408 | tf_op jit(solution)/shard_map/ppermute | solution.py:19
  129.1 3.8 %collective-permute-done.26 = bf16[16,7168]{1,0:T(8,128)(2,1)S(1)} collective-permute-done((bf16[16,7168]{1,0:T(8,128)(2,1)S(1)}, bf16[16,7168]{1,0:T(8,128)(2,1)S(1)}, u32[]{:S(2)}, u32[]{:S(2)}) %collective-permute-start.26) | collective-permute-done | bytes 229408 | tf_op jit(solution)/shard_map/ppermute | solution.py:19
  136.3 2.0 %collective-permute-start.28 = (bf16[4,7168]{1,0:T(4,128)(2,1)S(1)}, bf16[4,7168]{1,0:T(4,128)(2,1)S(1)}, u32[]{:S(2)}, u32[]{:S(2)}) collective-permute-start(bf16[4,7168]{1,0:T(4,128)(2,1)S(1)} %get-tuple-element.25), channel_id=1, source_target_pairs={{0,8},{4,12},{8,16},{12,20},{16,24},{20,28},{24,0},{28,4},{32,40},... | collective-permute-start | bytes 172040 | tf_op jit(solution)/shard_map/ppermute | solution.py:19
  138.4 2.1 %collective-permute-done.27 = bf16[4,7168]{1,0:T(4,128)(2,1)S(1)} collective-permute-done((bf16[4,7168]{1,0:T(4,128)(2,1)S(1)}, bf16[4,7168]{1,0:T(4,128)(2,1)S(1)}, u32[]{:S(2)}, u32[]{:S(2)}) %collective-permute-start.27) | collective-permute-done | bytes 57376 | tf_op jit(solution)/shard_map/ppermute | solution.py:19
  141.4 4.9 %collective-permute-start.30 = (bf16[2,7168]{1,0:T(2,128)(2,1)S(1)}, bf16[2,7168]{1,0:T(2,128)(2,1)S(1)}, u32[]{:S(2)}, u32[]{:S(2)}) collective-permute-start(bf16[2,7168]{1,0:T(2,128)(2,1)S(1)} %slice.313), channel_id=1, source_target_pairs={{0,128},{128,0},{1,129},{129,1},{2,130},{130,2},{3,131},{131,3},{4... | collective-permute-start | bytes 86024 | tf_op jit(solution)/shard_map/ppermute | solution.py:31
  146.3 3.1 %collective-permute-done.30 = bf16[2,7168]{1,0:T(2,128)(2,1)S(1)} collective-permute-done((bf16[2,7168]{1,0:T(2,128)(2,1)S(1)}, bf16[2,7168]{1,0:T(2,128)(2,1)S(1)}, u32[]{:S(2)}, u32[]{:S(2)}) %collective-permute-start.30) | collective-permute-done | bytes 28704 | tf_op jit(solution)/shard_map/ppermute | solution.py:31
  149.5 4.2 %collective-permute-done.31 = f32[2,7168]{1,0:T(2,128)S(1)} collective-permute-done((f32[2,7168]{1,0:T(2,128)S(1)}, f32[2,7168]{1,0:T(2,128)S(1)}, u32[]{:S(2)}, u32[]{:S(2)}) %collective-permute-start.31) | collective-permute-done | bytes 57376 | tf_op jit(solution)/shard_map/ppermute | solution.py:27
  153.8 5.3 %collective-permute-done.32 = f32[2,7168]{1,0:T(2,128)S(1)} collective-permute-done((f32[2,7168]{1,0:T(2,128)S(1)}, f32[2,7168]{1,0:T(2,128)S(1)}, u32[]{:S(2)}, u32[]{:S(2)}) %collective-permute-start.32) | collective-permute-done | bytes 57376 | tf_op jit(solution)/shard_map/ppermute | solution.py:27
  (122 shorter events, 39.3 us)
Async XLA Ops:
  6.1 12.0 %collective-permute-start.2 = (f32[2,2,32]{2,1,0:T(2,128)S(1)}, f32[2,2,32]{2,1,0:T(2,128)S(1)}, u32[]{:S(2)}, u32[]{:S(2)}) collective-permute-start(f32[2,2,32]{2,1,0:T(2,128)S(1)} %bitcast.143), channel_id=1, source_target_pairs={{0,3},{1,0},{2,1},{3,2},{4,7},{5,4},{6,5},{7,6},{8,11},{9,8},{10,9... | collective-permute-start | bytes 1544 | tf_op jit(solution)/shard_map/ppermute | solution.py:23
  10.8 8.9 %collective-permute-start = (f32[2,2,32]{2,1,0:T(2,128)S(1)}, f32[2,2,32]{2,1,0:T(2,128)S(1)}, u32[]{:S(2)}, u32[]{:S(2)}) collective-permute-start(f32[2,2,32]{2,1,0:T(2,128)S(1)} %bitcast.142), channel_id=1, source_target_pairs={{0,1},{1,2},{2,3},{3,0},{4,5},{5,6},{6,7},{7,4},{8,9},{9,10},{10,1... | collective-permute-start | bytes 1544 | tf_op jit(solution)/shard_map/ppermute | solution.py:23
  10.8 8.9 %collective-permute-start.1 = (f32[2,2,32]{2,1,0:T(2,128)S(1)}, f32[2,2,32]{2,1,0:T(2,128)S(1)}, u32[]{:S(2)}, u32[]{:S(2)}) collective-permute-start(f32[2,2,32]{2,1,0:T(2,128)S(1)} %bitcast.141), channel_id=1, source_target_pairs={{0,2},{1,3},{2,0},{3,1},{4,6},{5,7},{6,4},{7,5},{8,10},{9,11},{10,... | collective-permute-start | bytes 1544 | tf_op jit(solution)/shard_map/ppermute | solution.py:23
  14.0 6.1 %collective-permute-start.5 = (bf16[2,32,512]{2,0,1:T(2,128)(2,1)S(1)}, bf16[2,32,512]{2,0,1:T(2,128)(2,1)S(1)}, u32[]{:S(2)}, u32[]{:S(2)}) collective-permute-start(bf16[2,32,512]{2,0,1:T(2,128)(2,1)S(1)} %bitcast.136), channel_id=1, source_target_pairs={{0,3},{1,0},{2,1},{3,2},{4,7},{5,4},{6,5},{7,6},{8,11},{9,8},{10,9... | collective-permute-start | bytes 196616 | tf_op jit(solution)/shard_map/ppermute | solution.py:23
  17.4 6.2 %collective-permute-start.3 = (bf16[2,32,512]{2,0,1:T(2,128)(2,1)S(1)}, bf16[2,32,512]{2,0,1:T(2,128)(2,1)S(1)}, u32[]{:S(2)}, u32[]{:S(2)}) collective-permute-start(bf16[2,32,512]{2,0,1:T(2,128)(2,1)S(1)} %bitcast.137), channel_id=1, source_target_pairs={{0,1},{1,2},{2,3},{3,0},{4,5},{5,6},{6,7},{7,4},{8,9},{9,10},{10,1... | collective-permute-start | bytes 196616 | tf_op jit(solution)/shard_map/ppermute | solution.py:23
  18.1 7.2 %collective-permute-start.4 = (bf16[2,32,512]{2,0,1:T(2,128)(2,1)S(1)}, bf16[2,32,512]{2,0,1:T(2,128)(2,1)S(1)}, u32[]{:S(2)}, u32[]{:S(2)}) collective-permute-start(bf16[2,32,512]{2,0,1:T(2,128)(2,1)S(1)} %bitcast.138), channel_id=1, source_target_pairs={{0,2},{1,3},{2,0},{3,1},{4,6},{5,7},{6,4},{7,5},{8,10},{9,11},{10,... | collective-permute-start | bytes 196616 | tf_op jit(solution)/shard_map/ppermute | solution.py:23
  26.3 13.9 %all-to-all-start = ((bf16[32,2,512]{2,1,0:T(2,128)(2,1)}), bf16[32,2,512]{2,1,0:T(2,128)(2,1)S(1)}, u32[]{:S(2)}, u32[]{:S(2)}) async-start(bf16[32,2,512]{2,1,0:T(2,128)(2,1)} %fusion.44), calls=%async_computation | async-start | bytes 131072 | tf_op jit(solution)/shard_map/all_to_all | solution.py:104
  44.9 7.6 %collective-permute-start.7 = (bf16[8,7168]{1,0:T(8,128)(2,1)S(1)}, bf16[8,7168]{1,0:T(8,128)(2,1)S(1)}, u32[]{:S(2)}, u32[]{:S(2)}) collective-permute-start(bf16[8,7168]{1,0:T(8,128)(2,1)S(1)} %get-tuple-element.16), channel_id=1, source_target_pairs={{0,64},{4,68},{8,72},{12,76},{16,80},{20,84},{24,88},{28,92},{32,9... | collective-permute-start | bytes 344072 | tf_op jit(solution)/shard_map/ppermute | solution.py:19
  46.2 6.4 %collective-permute-start.9 = (bf16[8,7168]{1,0:T(8,128)(2,1)S(1)}, bf16[8,7168]{1,0:T(8,128)(2,1)S(1)}, u32[]{:S(2)}, u32[]{:S(2)}) collective-permute-start(bf16[8,7168]{1,0:T(8,128)(2,1)S(1)} %get-tuple-element.17), channel_id=1, source_target_pairs={{0,96},{4,100},{8,104},{12,108},{16,112},{20,116},{24,120},{28,124... | collective-permute-start | bytes 344072 | tf_op jit(solution)/shard_map/ppermute | solution.py:19
  48.3 6.3 %collective-permute-start.8 = (bf16[8,7168]{1,0:T(8,128)(2,1)S(1)}, bf16[8,7168]{1,0:T(8,128)(2,1)S(1)}, u32[]{:S(2)}, u32[]{:S(2)}) collective-permute-start(bf16[8,7168]{1,0:T(8,128)(2,1)S(1)} %get-tuple-element.18), channel_id=1, source_target_pairs={{0,32},{4,36},{8,40},{12,44},{16,48},{20,52},{24,56},{28,60},{32,6... | collective-permute-start | bytes 344072 | tf_op jit(solution)/shard_map/ppermute | solution.py:19
  54.7 5.6 %collective-permute-start.10 = (bf16[2,7168]{1,0:T(2,128)(2,1)S(1)}, bf16[2,7168]{1,0:T(2,128)(2,1)S(1)}, u32[]{:S(2)}, u32[]{:S(2)}) collective-permute-start(bf16[2,7168]{1,0:T(2,128)(2,1)S(1)} %get-tuple-element.26), channel_id=1, source_target_pairs={{0,16},{4,20},{8,24},{12,28},{16,0},{20,4},{24,8},{28,12},{32,48},... | collective-permute-start | bytes 86024 | tf_op jit(solution)/shard_map/ppermute | solution.py:19
  56.2 4.2 %collective-permute-start.12 = (bf16[2,7168]{1,0:T(2,128)(2,1)S(1)}, bf16[2,7168]{1,0:T(2,128)(2,1)S(1)}, u32[]{:S(2)}, u32[]{:S(2)}) collective-permute-start(bf16[2,7168]{1,0:T(2,128)(2,1)S(1)} %get-tuple-element.27), channel_id=1, source_target_pairs={{0,24},{4,28},{8,0},{12,4},{16,8},{20,12},{24,16},{28,20},{32,56},... | collective-permute-start | bytes 86024 | tf_op jit(solution)/shard_map/ppermute | solution.py:19
  57.3 4.0 %collective-permute-start.11 = (bf16[2,7168]{1,0:T(2,128)(2,1)S(1)}, bf16[2,7168]{1,0:T(2,128)(2,1)S(1)}, u32[]{:S(2)}, u32[]{:S(2)}) collective-permute-start(bf16[2,7168]{1,0:T(2,128)(2,1)S(1)} %get-tuple-element.28), channel_id=1, source_target_pairs={{0,8},{4,12},{8,16},{12,20},{16,24},{20,28},{24,0},{28,4},{32,40},... | collective-permute-start | bytes 86024 | tf_op jit(solution)/shard_map/ppermute | solution.py:19
  61.3 4.3 %collective-permute-start.13 = (f32[2,7168]{1,0:T(2,128)S(1)}, f32[2,7168]{1,0:T(2,128)S(1)}, u32[]{:S(2)}, u32[]{:S(2)}) collective-permute-start(f32[2,7168]{1,0:T(2,128)S(1)} %fusion.46), channel_id=1, source_target_pairs={{0,1},{1,0},{2,3},{3,2},{4,5},{5,4},{6,7},{7,6},{8,9},{9,8},{10,11... | collective-permute-start | bytes 172040 | tf_op jit(solution)/shard_map/ppermute | solution.py:27
  65.6 5.7 %collective-permute-start.14 = (f32[2,7168]{1,0:T(2,128)S(1)}, f32[2,7168]{1,0:T(2,128)S(1)}, u32[]{:S(2)}, u32[]{:S(2)}) collective-permute-start(f32[2,7168]{1,0:T(2,128)S(1)} %add.337), channel_id=1, source_target_pairs={{0,2},{1,3},{2,0},{3,1},{4,6},{5,7},{6,4},{7,5},{8,10},{9,11},{10,... | collective-permute-start | bytes 172040 | tf_op jit(solution)/shard_map/ppermute | solution.py:27
  71.7 7.9 %collective-permute-start.15 = (bf16[2,7296]{1,0:T(2,128)(2,1)S(1)}, bf16[2,7296]{1,0:T(2,128)(2,1)S(1)}, u32[]{:S(2)}, u32[]{:S(2)}) collective-permute-start(bf16[2,7296]{1,0:T(2,128)(2,1)S(1)} %pad_maximum_fusion.1), channel_id=1, source_target_pairs={{0,128},{128,0},{1,129},{129,1},{2,130},{130,2},{3,131},{131,3},{4... | collective-permute-start | bytes 87560 | tf_op jit(solution)/shard_map/ppermute | solution.py:31
  79.6 5.5 %collective-permute-start.18 = (bf16[4,7296]{1,0:T(4,128)(2,1)S(1)}, bf16[4,7296]{1,0:T(4,128)(2,1)S(1)}, u32[]{:S(2)}, u32[]{:S(2)}) collective-permute-start(bf16[4,7296]{1,0:T(4,128)(2,1)S(1)} %pad_maximum_fusion), channel_id=1, source_target_pairs={{0,8},{4,12},{8,16},{12,20},{16,24},{20,28},{24,0},{28,4},{32,40},... | collective-permute-start | bytes 175112 | tf_op jit(solution)/shard_map/ppermute | solution.py:19
  80.6 6.6 %collective-permute-start.17 = (bf16[4,7296]{1,0:T(4,128)(2,1)S(1)}, bf16[4,7296]{1,0:T(4,128)(2,1)S(1)}, u32[]{:S(2)}, u32[]{:S(2)}) collective-permute-start(bf16[4,7296]{1,0:T(4,128)(2,1)S(1)} %pad_maximum_fusion), channel_id=1, source_target_pairs={{0,16},{4,20},{8,24},{12,28},{16,0},{20,4},{24,8},{28,12},{32,48},... | collective-permute-start | bytes 175112 | tf_op jit(solution)/shard_map/ppermute | solution.py:19
  85.0 4.2 %collective-permute-start.16 = (bf16[4,7296]{1,0:T(4,128)(2,1)S(1)}, bf16[4,7296]{1,0:T(4,128)(2,1)S(1)}, u32[]{:S(2)}, u32[]{:S(2)}) collective-permute-start(bf16[4,7296]{1,0:T(4,128)(2,1)S(1)} %pad_maximum_fusion), channel_id=1, source_target_pairs={{0,24},{4,28},{8,0},{12,4},{16,8},{20,12},{24,16},{28,20},{32,56},... | collective-permute-start | bytes 175112 | tf_op jit(solution)/shard_map/ppermute | solution.py:19
  89.4 9.9 %collective-permute-start.21 = (bf16[16,7296]{1,0:T(8,128)(2,1)S(1)}, bf16[16,7296]{1,0:T(8,128)(2,1)S(1)}, u32[]{:S(2)}, u32[]{:S(2)}) collective-permute-start(bf16[16,7296]{1,0:T(8,128)(2,1)S(1)} %concatenate.17), channel_id=1, source_target_pairs={{0,32},{4,36},{8,40},{12,44},{16,48},{20,52},{24,56},{28,60},{32,6... | collective-permute-start | bytes 700424 | tf_op jit(solution)/shard_map/ppermute | solution.py:19
  89.5 9.8 %collective-permute-start.20 = (bf16[16,7296]{1,0:T(8,128)(2,1)S(1)}, bf16[16,7296]{1,0:T(8,128)(2,1)S(1)}, u32[]{:S(2)}, u32[]{:S(2)}) collective-permute-start(bf16[16,7296]{1,0:T(8,128)(2,1)S(1)} %concatenate.17), channel_id=1, source_target_pairs={{0,64},{4,68},{8,72},{12,76},{16,80},{20,84},{24,88},{28,92},{32,9... | collective-permute-start | bytes 700424 | tf_op jit(solution)/shard_map/ppermute | solution.py:19
  91.7 8.6 %collective-permute-start.19 = (bf16[16,7296]{1,0:T(8,128)(2,1)S(1)}, bf16[16,7296]{1,0:T(8,128)(2,1)}, u32[]{:S(2)}, u32[]{:S(2)}) collective-permute-start(bf16[16,7296]{1,0:T(8,128)(2,1)S(1)} %concatenate.17), channel_id=1, source_target_pairs={{0,96},{4,100},{8,104},{12,108},{16,112},{20,116},{24,120},{28,124... | collective-permute-start | bytes 700424 | tf_op jit(solution)/shard_map/ppermute | solution.py:19
  110.8 2.8 %collective-permute-start.23 = (bf16[64,7168]{1,0:T(8,128)(2,1)}, bf16[64,7168]{1,0:T(8,128)(2,1)}, u32[]{:S(2)}, u32[]{:S(2)}) collective-permute-start(bf16[64,7168]{1,0:T(8,128)(2,1)} %multiply_convert_fusion), channel_id=1, source_target_pairs={{0,4},{4,0},{8,12},{12,8},{16,20},{20,16},{24,28},{28,24},{32,36},... | collective-permute-start | bytes 2752520 | tf_op jit(solution)/shard_map/ppermute | solution.py:19
  119.1 10.1 %collective-permute-start.24 = (bf16[16,7168]{1,0:T(8,128)(2,1)S(1)}, bf16[16,7168]{1,0:T(8,128)(2,1)S(1)}, u32[]{:S(2)}, u32[]{:S(2)}) collective-permute-start(bf16[16,7168]{1,0:T(8,128)(2,1)S(1)} %get-tuple-element.13), channel_id=1, source_target_pairs={{0,64},{4,68},{8,72},{12,76},{16,80},{20,84},{24,88},{28,92},{32,9... | collective-permute-start | bytes 688136 | tf_op jit(solution)/shard_map/ppermute | solution.py:19
  119.7 13.2 %collective-permute-start.26 = (bf16[16,7168]{1,0:T(8,128)(2,1)S(1)}, bf16[16,7168]{1,0:T(8,128)(2,1)S(1)}, u32[]{:S(2)}, u32[]{:S(2)}) collective-permute-start(bf16[16,7168]{1,0:T(8,128)(2,1)S(1)} %get-tuple-element.14), channel_id=1, source_target_pairs={{0,96},{4,100},{8,104},{12,108},{16,112},{20,116},{24,120},{28,124... | collective-permute-start | bytes 688136 | tf_op jit(solution)/shard_map/ppermute | solution.py:19
  121.8 11.4 %collective-permute-start.25 = (bf16[16,7168]{1,0:T(8,128)(2,1)S(1)}, bf16[16,7168]{1,0:T(8,128)(2,1)S(1)}, u32[]{:S(2)}, u32[]{:S(2)}) collective-permute-start(bf16[16,7168]{1,0:T(8,128)(2,1)S(1)} %get-tuple-element.15), channel_id=1, source_target_pairs={{0,32},{4,36},{8,40},{12,44},{16,48},{20,52},{24,56},{28,60},{32,6... | collective-permute-start | bytes 688136 | tf_op jit(solution)/shard_map/ppermute | solution.py:19
  134.4 6.1 %collective-permute-start.27 = (bf16[4,7168]{1,0:T(4,128)(2,1)S(1)}, bf16[4,7168]{1,0:T(4,128)(2,1)S(1)}, u32[]{:S(2)}, u32[]{:S(2)}) collective-permute-start(bf16[4,7168]{1,0:T(4,128)(2,1)S(1)} %get-tuple-element.23), channel_id=1, source_target_pairs={{0,16},{4,20},{8,24},{12,28},{16,0},{20,4},{24,8},{28,12},{32,48},... | collective-permute-start | bytes 172040 | tf_op jit(solution)/shard_map/ppermute | solution.py:19
  136.3 4.7 %collective-permute-start.29 = (bf16[4,7168]{1,0:T(4,128)(2,1)S(1)}, bf16[4,7168]{1,0:T(4,128)(2,1)S(1)}, u32[]{:S(2)}, u32[]{:S(2)}) collective-permute-start(bf16[4,7168]{1,0:T(4,128)(2,1)S(1)} %get-tuple-element.24), channel_id=1, source_target_pairs={{0,24},{4,28},{8,0},{12,4},{16,8},{20,12},{24,16},{28,20},{32,56},... | collective-permute-start | bytes 172040 | tf_op jit(solution)/shard_map/ppermute | solution.py:19
  136.3 5.0 %collective-permute-start.28 = (bf16[4,7168]{1,0:T(4,128)(2,1)S(1)}, bf16[4,7168]{1,0:T(4,128)(2,1)S(1)}, u32[]{:S(2)}, u32[]{:S(2)}) collective-permute-start(bf16[4,7168]{1,0:T(4,128)(2,1)S(1)} %get-tuple-element.25), channel_id=1, source_target_pairs={{0,8},{4,12},{8,16},{12,20},{16,24},{20,28},{24,0},{28,4},{32,40},... | collective-permute-start | bytes 172040 | tf_op jit(solution)/shard_map/ppermute | solution.py:19
  141.4 8.0 %collective-permute-start.30 = (bf16[2,7168]{1,0:T(2,128)(2,1)S(1)}, bf16[2,7168]{1,0:T(2,128)(2,1)S(1)}, u32[]{:S(2)}, u32[]{:S(2)}) collective-permute-start(bf16[2,7168]{1,0:T(2,128)(2,1)S(1)} %slice.313), channel_id=1, source_target_pairs={{0,128},{128,0},{1,129},{129,1},{2,130},{130,2},{3,131},{131,3},{4... | collective-permute-start | bytes 86024 | tf_op jit(solution)/shard_map/ppermute | solution.py:31
  149.4 4.3 %collective-permute-start.31 = (f32[2,7168]{1,0:T(2,128)S(1)}, f32[2,7168]{1,0:T(2,128)S(1)}, u32[]{:S(2)}, u32[]{:S(2)}) collective-permute-start(f32[2,7168]{1,0:T(2,128)S(1)} %slice_add_fusion.3), channel_id=1, source_target_pairs={{0,1},{1,0},{2,3},{3,2},{4,5},{5,4},{6,7},{7,6},{8,9},{9,8},{10,11... | collective-permute-start | bytes 172040 | tf_op jit(solution)/shard_map/ppermute | solution.py:27
  153.7 5.4 %collective-permute-start.32 = (f32[2,7168]{1,0:T(2,128)S(1)}, f32[2,7168]{1,0:T(2,128)S(1)}, u32[]{:S(2)}, u32[]{:S(2)}) collective-permute-start(f32[2,7168]{1,0:T(2,128)S(1)} %add.351), channel_id=1, source_target_pairs={{0,2},{1,3},{2,0},{3,1},{4,6},{5,7},{6,4},{7,5},{8,10},{9,11},{10,... | collective-permute-start | bytes 172040 | tf_op jit(solution)/shard_map/ppermute | solution.py:27
  (12 other events, 268.2 us)

commit v2 on v0

v2 whole, which is shorter than its diff:
```python
import jax
import jax.numpy as jnp
from jax import lax
from jax.experimental import pallas as pl
from jax.experimental.pallas import tpu as pltpu
from jax.sharding import PartitionSpec as P

SCORE_SCALE = 192.0 ** (-0.5)
SIDE = 4
BF = jnp.bfloat16
T_AT, CORE_AT, ROLE_AT, EXPERT_AT = range(4)
F32 = jnp.float32


PLANE = ("y", "x")
LINE = ("role", "tensor")


def other_core(value):
    return lax.ppermute(value, "core", [(0, 1), (1, 0)])


def trade(value, axes):
    return lax.all_to_all(value, axes, 0, 0, tiled=True)


def in_three(value):
    high = value.astype(BF).astype(F32)
    rest = value - high
    middle = rest.astype(BF).astype(F32)
    return high, middle, rest - middle


def attend(where_ref, length_ref, q_ref, keys_ref, out_ref):
    heads, slots = q_ref.shape[2], keys_ref.shape[2]
    latent = out_ref.shape[3] - 128
    experts = out_ref.shape[2]
    row = lax.broadcasted_iota(jnp.int32, (heads, heads), 0)
    column = lax.broadcasted_iota(jnp.int32, (heads, heads), 1)
    pick = (column == (row % experts) * 4 + row // experts).astype(BF)
    q = lax.dot_general(pick, q_ref[0], (((1,), (1,)), ((), ())), preferred_element_type=F32)
    logits = jnp.dot(q.astype(BF), keys_ref[0], preferred_element_type=F32) * SCORE_SCALE
    position = where_ref[T_AT] * slots + lax.broadcasted_iota(jnp.int32, (1, slots), 1)
    live = position < length_ref[pl.program_id(0)]
    masked = jnp.where(live, logits, -1e30)
    top = jnp.max(masked, axis=1, keepdims=True)
    expo = jnp.where(live, jnp.exp(masked - top), 0.0)
    total = jnp.sum(expo, axis=1, keepdims=True)
    numer = lax.dot_general(
        expo.astype(BF), keys_ref[0, :latent], (((1,), (1,)), ((), ())), preferred_element_type=F32
    )
    part = (numer / jnp.maximum(total, 1.0)).astype(BF)
    out_ref[:, 0, :, :latent] = part.reshape(4, experts, latent)
    lane = lax.broadcasted_iota(jnp.int32, (heads, 128), 1)
    stats = jnp.zeros((heads, 128), F32)
    for i, column in enumerate((*in_three(top), *in_three(total))):
        stats = jnp.where(lane == i, column, stats)
    out_ref[:, 0, :, latent:] = stats.astype(BF).reshape(4, experts, 128)


def combine(parts_ref, out_ref):
    latent = out_ref.shape[2]
    for r in range(out_ref.shape[0]):
        tops, totals = [], []
        for t in range(4):
            s = parts_ref[t, r, :, latent:].astype(F32)
            tops.append(s[:, 0:1] + s[:, 1:2] + s[:, 2:3])
            totals.append(s[:, 3:4] + s[:, 4:5] + s[:, 5:6])
        top = jnp.maximum(jnp.maximum(tops[0], tops[1]), jnp.maximum(tops[2], tops[3]))
        weights = [jnp.exp(a - top) * b for a, b in zip(tops, totals)]
        whole = weights[0] + weights[1] + weights[2] + weights[3]
        acc = jnp.zeros((out_ref.shape[1], latent), F32)
        for t in range(4):
            acc = acc + (weights[t] / whole) * parts_ref[t, r, :, :latent].astype(F32)
        out_ref[r] = acc.astype(BF)


def pick_part(parts, count, part):
    value = parts[0]
    for j in range(1, count):
        value = jnp.where(part == j, parts[j], value)
    return value


def project(where_ref, rows_ref, value_ref, out_proj_ref, away_ref, own_ref):
    n = rows_ref.shape[0]
    heads = jnp.dot(rows_ref[...], value_ref[0], preferred_element_type=F32).astype(BF)
    out_rows, width = own_ref.shape
    r = lax.broadcasted_iota(jnp.int32, (out_rows, n), 0)
    source = lax.broadcasted_iota(jnp.int32, (out_rows, n), 1)
    quarter = lax.broadcasted_iota(jnp.int32, (out_rows, 1), 0) // 2 % 4
    for dc, out_ref in ((1, away_ref), (0, own_ref)):
        core = (where_ref[CORE_AT] + dc) % 2
        pick = (source == (r // 8) * 4 + core * 2 + r % 2).astype(BF)
        picked = jnp.dot(pick, heads, preferred_element_type=F32).astype(BF)
        for k in range(0, width, 256):
            parts = [
                jnp.dot(
                    picked,
                    out_proj_ref[:, j * width + k : j * width + k + 256],
                    preferred_element_type=F32,
                )
                for j in range(4)
            ]
            out_ref[:, k : k + 256] = pick_part(parts, 4, quarter).astype(out_ref.dtype)


def gather_sum(where_ref, got_ref, extra_ref, table_ref, out_ref, held_ref):
    width = held_ref.shape[1]
    acc = got_ref[0].astype(F32)
    for p in range(1, got_ref.shape[0]):
        acc = acc + got_ref[p].astype(F32)
    held_ref[...] = acc
    first = (where_ref[T_AT] == 0).astype(F32)
    for j in range(4):
        columns = slice(j * width, (j + 1) * width)
        piece = (held_ref[2 * j : 2 * j + 2] + first * extra_ref[:, columns].astype(F32)).astype(BF)
        for z in range(out_ref.shape[0]):
            out_ref[z, :, columns] = piece
    for z in range(out_ref.shape[0]):
        out_ref[z, :, 4 * width :] = table_ref[...]


def normalise(where_ref, got_ref, gain_ref, attended_ref, out_ref, held_ref):
    width = attended_ref.shape[1]
    half = width // 2
    gain = gain_ref[...].astype(F32)
    both = []
    for role in range(2):
        acc = got_ref[4 * role, :, :width].astype(F32)
        for t in range(1, 4):
            acc = acc + got_ref[4 * role + t, :, :width].astype(F32)
        both.append(acc)
        mean_square = jnp.mean(acc * acc, axis=1, keepdims=True)
        normed = acc * lax.rsqrt(mean_square + 1e-06) * gain
        table = got_ref[4 * role, :, width:].astype(F32)
        for h in range(2):
            at = 4 * h + 2 * role
            held_ref[at : at + 2, :half] = normed[:, h * half : (h + 1) * half]
            held_ref[at : at + 2, half:] = table
    attended_ref[...] = jnp.where(where_ref[ROLE_AT] == 0, both[0], both[1])
    block = held_ref[...].astype(BF)
    for p in range(out_ref.shape[0]):
        out_ref[p] = block


def spread_sum(got_ref, out_ref, held_ref):
    half = held_ref.shape[1]
    acc = got_ref[0].astype(F32)
    for p in range(1, got_ref.shape[0]):
        acc = acc + got_ref[p].astype(F32)
    held_ref[...] = acc
    for role in range(2):
        for h in range(2):
            at = 4 * h + 2 * role
            piece = held_ref[at : at + 2].astype(BF)
            for t in range(4):
                out_ref[4 * role + t, :, h * half : (h + 1) * half] = piece


def which_half(rows):
    return lax.broadcasted_iota(jnp.int32, (rows, 1), 0) // 4 % 2


def hidden(where_ref, rows_ref, gate_ref, up_ref):
    n, step = rows_ref.shape[0], 512
    width = gate_ref.shape[1] // 2
    half = which_half(n)

    def whole(ref):
        sums = [jnp.zeros((n, ref.shape[2]), F32) for _ in range(2)]
        for k in range(0, width, step):
            rows = rows_ref[:, k : k + step]
            for h in range(2):
                weights = ref[0, h * width + k : h * width + k + step]
                sums[h] = sums[h] + jnp.dot(rows, weights, preferred_element_type=F32)
        value = pick_part(sums, 2, half)
        other = jnp.where(half == 0, pltpu.roll(value, n - 4, 0), pltpu.roll(value, 4, 0))
        return value + other

    gate, upper = whole(gate_ref), whole(up_ref)
    lane = lax.broadcasted_iota(jnp.int32, (n, 128), 1)
    chosen = jnp.where(lane == where_ref[EXPERT_AT], rows_ref[:, width:].astype(F32), 0.0)
    coef = jnp.sum(chosen, axis=1, keepdims=True)
    act = (gate / (1.0 + jnp.exp(-gate)) * upper).astype(BF)
    return act, coef


def fall(act, coef, down_ref, out_ref):
    width, step = out_ref.shape[1], 512
    half = which_half(act.shape[0])
    for at in range(0, width, step):
        parts = [
            jnp.dot(act, down_ref[0, :, k : k + step], preferred_element_type=F32)
            for k in (at, width + at)
        ]
        out_ref[:, at : at + step] = (coef * pick_part(parts, 2, half)).astype(out_ref.dtype)


def activate(where_ref, rows_ref, gate_ref, up_ref, act_ref, coef_ref):
    act, coef = hidden(where_ref, rows_ref, gate_ref, up_ref)
    act_ref[...] = act
    coef_ref[...] = jnp.broadcast_to(coef, coef_ref.shape)


def through(where_ref, rows_ref, gate_ref, up_ref, down_ref, out_ref):
    act, coef = hidden(where_ref, rows_ref, gate_ref, up_ref)
    fall(act, coef, down_ref, out_ref)


def descend(act_ref, coef_ref, down_ref, out_ref):
    fall(act_ref[...], coef_ref[:, :1], down_ref, out_ref)


SCALAR = pl.BlockSpec(memory_space=pltpu.SMEM)
WHOLE = pl.BlockSpec(memory_space=pltpu.VMEM)


def kernel(body, shapes, inputs, specs=None, scratch=(), work=(0, 0), mib=12):
    return pl.pallas_call(
        body,
        out_shape=shapes,
        in_specs=specs or [WHOLE] * len(inputs),
        out_specs=jax.tree.map(lambda _: WHOLE, shapes),
        scratch_shapes=list(scratch),
        compiler_params=pltpu.CompilerParams(vmem_limit_bytes=mib * 1024 * 1024),
        cost_estimate=pl.CostEstimate(flops=work[0], bytes_accessed=work[1], transcendentals=0),
    )(*inputs)


def shards(
    request_latent_cache,
    queries,
    cache_lengths,
    residual_in,
    value_up_weight,
    out_proj,
    norm_gain,
    gate_proj,
    up_proj,
    down_proj,
    expert_ids,
    route_weights,
):
    t = lax.axis_index("tensor")
    role = lax.axis_index("role")
    c = lax.axis_index("core")
    e = lax.axis_index(("y", "x", "core"))
    where = jnp.stack([t, c, role, e])
    local_requests = request_latent_cache.shape[0]
    latent = value_up_weight.shape[1]
    experts, width = 32, residual_in.shape[1]

    slots, depth = request_latent_cache.shape[1:]
    n_heads = queries.shape[1]
    parts = pl.pallas_call(
        attend,
        grid=(local_requests,),
        out_shape=jax.ShapeDtypeStruct((4, local_requests, experts, latent + 128), BF),
        in_specs=[
            SCALAR,
            SCALAR,
            pl.BlockSpec((1, depth, n_heads), lambda r: (r, 0, 0)),
            pl.BlockSpec((1, depth, slots), lambda r: (r, 0, 0)),
        ],
        out_specs=pl.BlockSpec((4, 1, experts, latent + 128), lambda r: (0, r, 0, 0)),
        compiler_params=pltpu.CompilerParams(vmem_limit_bytes=58 * 1024 * 1024),
    )(
        where,
        cache_lengths,
        jnp.swapaxes(queries, 1, 2),
        jnp.swapaxes(request_latent_cache, 1, 2),
    )
    parts = trade(parts, "tensor")
    context = kernel(
        combine, jax.ShapeDtypeStruct((local_requests, experts, latent), BF), [parts]
    )
    rows = trade(jnp.swapaxes(context, 0, 1), ("y", "x", "core"))
    rows = rows.reshape(experts * local_requests, latent)
    shape = jax.ShapeDtypeStruct
    places, packed = 16, 4 * local_requests
    quarter, middle = width // 4, width // 2
    away, acc = kernel(
        project,
        (shape((places * packed, quarter), BF), shape((places * packed, quarter), F32)),
        [where, rows, value_up_weight, out_proj],
        specs=[SCALAR, WHOLE, WHOLE, WHOLE],
    )
    acc = (acc + other_core(away).astype(F32)).astype(BF)
    acc = trade(acc.reshape(places, packed, quarter), PLANE)
    names = jnp.arange(128, dtype=jnp.int32)
    table = jnp.sum(
        jnp.where(
            expert_ids[:, :, None] == names[None, None, :],
            route_weights.astype(F32)[:, :, None],
            0.0,
        ),
        axis=1,
    ).astype(BF)
    block = kernel(
        gather_sum,
        shape((8, local_requests, width + 128), BF),
        [where, acc, residual_in, table],
        specs=[SCALAR, WHOLE, WHOLE, WHOLE],
        scratch=[pltpu.VMEM((packed, quarter), F32)],
    )
    block = trade(block, LINE)
    attended, block = kernel(
        normalise,
        (
            shape((local_requests, width), F32),
            shape((places, packed, middle + 128), BF),
        ),
        [where, block, norm_gain[None]],
        specs=[SCALAR, WHOLE, WHOLE],
        scratch=[pltpu.VMEM((packed, middle + 128), F32)],
    )
    block = trade(block, PLANE).reshape(places * packed, middle + 128)
    across = other_core(block)

    n_rows, units = block.shape[0], gate_proj.shape[2]
    flops, size = 2 * n_rows * width * units, 2 * width * units
    act, coef = kernel(
        activate,
        (shape((n_rows, units), BF), shape((n_rows, 128), F32)),
        [where, block, gate_proj, up_proj],
        specs=[SCALAR, WHOLE, WHOLE, WHOLE],
        work=(2 * flops, 2 * size),
    )
    across, act, coef = lax.optimization_barrier((across, act, coef))
    sent = kernel(
        through,
        shape((n_rows, middle), BF),
        [where, across, gate_proj, up_proj, down_proj],
        specs=[SCALAR, WHOLE, WHOLE, WHOLE, WHOLE],
        work=(3 * flops, 3 * size),
    )
    sent = other_core(sent)
    acc = kernel(
        descend,
        shape((n_rows, middle), F32),
        [act, coef, down_proj],
        work=(flops, size),
    )
    acc = (acc + sent.astype(F32)).astype(BF)
    acc = trade(acc.reshape(places, packed, middle), PLANE)
    acc = kernel(
        spread_sum,
        shape((8, local_requests, width), BF),
        [acc],
        scratch=[pltpu.VMEM((packed, middle), F32)],
    )
    acc = trade(acc, LINE)
    routed = jnp.sum(acc.astype(F32), axis=0)
    return (attended, routed)


def solution(mesh):
    sizes = (mesh.shape["role"], SIDE, SIDE, 2, mesh.shape["tensor"])
    names = ("role", "y", "x", "core", "tensor")
    expert = ("y", "x", "core")
    own = ("role",) + expert
    placed = (
        P(own, "tensor", None),
        P(own, None, None),
        P(own),
        P(own, None),
        P(expert + ("tensor",), None, None),
        P(expert + ("tensor",), None),
        P(),
        P(expert, None, ("role", "tensor")),
        P(expert, None, ("role", "tensor")),
        P(expert, ("role", "tensor"), None),
        P(own, None),
        P(own, None),
    )
    return jax.shard_map(
        shards,
        mesh=jax.sharding.Mesh(mesh.devices.reshape(sizes), names),
        in_specs=placed,
        out_specs=(P(own, None), P(own, None)),
        check_vma=False,
    )
```

time: 1340 us -> 135 us (0.10)
  waiting for transfers between devices: 991 us -> 23.6 us
  blocking collectives: 297 us -> 79.6 us
  matrix products: 16 us -> 0 us
  between operations: 15.3 us -> 0.81 us
  Pallas kernels: 0 us -> 13.9 us
    unnamed x7 -> x0, waiting for transfers between devices: 884 us -> none
    all_gather x3 -> x0, blocking collectives: 235 us -> none  [the longest x1 113 us: shards(): lax.all_gather(expert_ids, ('role', 'expert'), axis=0, tiled=True)]
    reduce_scatter x1 -> x0, waiting for transfers between devices: 71.6 us -> none  [shards(): lax.psum_scatter(running, 'tensor', scatter_dimension=1, tiled=True)]
    all_to_all x1 -> x5, blocking collectives: 13.5 us -> 79.6 us  [trade(): return lax.all_to_all(value, axes, 0, 0, tiled=True)]
    psum x1 -> x0, waiting for transfers between devices: 36.1 us -> none  [shards(): numer_all, totals_all = lax.psum((numer, totals), 'tensor')]
    psum x2 -> x0, blocking collectives: 35.6 us -> none  [the longest x1 19.8 us: shards(): attn_rows = lax.psum(partial_attn, 'tensor')]
    all_to_all x0 -> x2, waiting for transfers between devices: none -> 20.5 us  [trade(): return lax.all_to_all(value, axes, 0, 0, tiled=True)]
    dot_general x5 -> x0, matrix products: 16 us -> none  [the longest x1 5.07 us: shards(): jnp.dot(act, down_proj[0], preferred_element_type=jnp.float32)]
  transfers between devices with their start and end apart: 5 -> 5, of which waited for: 4 -> 4; matrix products, arithmetic and copies ran while one was open for 0% -> 0% of each run, Pallas kernels for 0% -> 2%
where the time goes in v2:
time: 135 us; the launch traced here: 134 us
  blocking collectives  79.6 us (59%)
  waiting for transfers between devices  23.6 us (17%)
  Pallas kernels  13.9 us (10%)
  starting transfers between devices  11.8 us (9%)
  other arithmetic  2.54 us (2%)
  local copies, waits for them, and re-layouts  1.66 us (1%)
    all_to_all x5, blocking collectives, trade(): return lax.all_to_all(value, axes, 0, 0, tiled=True)  79.6 us
    all_to_all x2, waiting for transfers between devices, trade(): return lax.all_to_all(value, axes, 0, 0, tiled=True)  20.5 us
    all_to_all x2, starting transfers between devices, trade(): return lax.all_to_all(value, axes, 0, 0, tiled=True)  11.1 us
    pallas_call x8, Pallas kernels, kernel(): pl.pallas_call(body, out_shape=shapes, in_specs=specs or [WHOLE] * len(in...  9.7 us
    pallas_call x1, Pallas kernels, shards(): pl.pallas_call(attend, grid=(local_requests,), out_shape=jax.ShapeDtypeSt...  4.22 us
    ppermute x3, waiting for transfers between devices, other_core(): return lax.ppermute(value, 'core', [(0, 1), (1, 0)])  3.16 us
  transfers between devices with their start and end apart: 5, of which 4 were waited for; matrix products, arithmetic and copies ran while one was open for 0% of the time, Pallas kernels for 2%

profile of v2, /device:TPU:2, one launch (start us, length us, event | category | flops | bytes accessed | tf_op | source)
XLA Modules:
  0.0 134.0 jit_solution(17868658171097014952)
XLA Ops:
  0.6 0.6 pad_add_fusion.where_ref
  1.3 4.2 %shard_map.131 = bf16[4,2,32,640]{3,2,1,0:T(8,128)(2,1)} custom-call(s32[4]{0:T(128)} %pad_add_fusion.where_ref, s32[2]{0:T(128)} %length_ref.1, bf16[2,576,128]{2,1,0:T(8,128)(2,1)} %bitcast.16, bf16[2,576,1024]{2,1,0:T(8,128)(2,1)} %bitcast.15), custom_call_target="tpu_custom_call" | custom-call | tf_op jit(solution)/shard_map/pallas_call | solution.py:256
  5.5 16.2 %all_to_all.35.parts_ref = bf16[4,2,32,640]{3,2,1,0:T(8,128)(2,1)S(1)} all-to-all(bf16[4,2,32,640]{3,2,1,0:T(8,128)(2,1)} %shard_map.131), channel_id=1, replica_groups=mesh['role'=2,'y'=4,'x'=4,'core'=2,'tensor'=4] {'tensor'}, dimensions={0} | all-to-all | bytes 655360 | tf_op jit(solution)/shard_map/all_to_all | solution.py:24
  21.7 0.3 shard_map.132
  21.9 0.1 copy.16
  22.0 13.7 %all_to_all.36 = bf16[32,2,512]{2,1,0:T(2,128)(2,1)S(1)} all-to-all(bf16[32,2,512]{2,1,0:T(2,128)(2,1)S(1)} %copy.16), channel_id=1, replica_groups=mesh['role'=2,'y'=4,'x'=4,'core'=2,'tensor'=4] {'y','x','core'}, dimensions={0} | all-to-all | bytes 131072 | tf_op jit(solution)/shard_map/all_to_all | solution.py:24
  35.8 2.0 %shard_map.133 = (bf16[128,1792]{1,0:T(8,128)(2,1)S(1)}, f32[128,1792]{1,0:T(8,128)S(1)}) custom-call(s32[4]{0:T(128)S(1)} %copy-done.6, bf16[64,512]{1,0:T(8,128)(2,1)S(1)} %reshape.18.rows_ref, bf16[1,512,128]{2,1,0:T(8,128)(2,1)S(1)} %copy-done.4, bf16[128,7168]{1,0:T(8,128)(2,1)S(1)} %copy-done.3), custom_call_target="tpu_custom_call" | custom-call | tf_op jit(solution)/shard_map/pallas_call | solution.py:220
  37.8 0.0 copy-start.9
  37.9 0.0 copy-start.8
  37.9 0.0 copy-start.5
  37.9 0.2 collective-permute-start
  38.1 1.7 %collective-permute-done = bf16[128,1792]{1,0:T(8,128)(2,1)S(1)} collective-permute-done((bf16[128,1792]{1,0:T(8,128)(2,1)S(1)}, bf16[128,1792]{1,0:T(8,128)(2,1)S(1)}, u32[]{:S(2)}, u32[]{:S(2)}) %collective-permute-start) | collective-permute-done | bytes 458784 | tf_op jit(solution)/shard_map/ppermute | solution.py:20
  39.8 0.9 fusion.1
  40.6 4.8 %all-to-all-start.2 = ((bf16[16,8,1792]{2,1,0:T(8,128)(2,1)}), bf16[16,8,1792]{2,1,0:T(8,128)(2,1)S(1)}, u32[]{:S(2)}, u32[]{:S(2)}) async-start(bf16[16,8,1792]{2,1,0:T(8,128)(2,1)} %fusion.1), calls=%async_computation.2 | async-start | bytes 917504 | tf_op jit(solution)/shard_map/all_to_all | solution.py:24
  45.5 0.1 select_reduce_fusion.table_ref
  45.6 10.0 %all-to-all-done.2.got_ref = bf16[16,8,1792]{2,1,0:T(8,128)(2,1)S(1)} async-done(((bf16[16,8,1792]{2,1,0:T(8,128)(2,1)}), bf16[16,8,1792]{2,1,0:T(8,128)(2,1)S(1)}, u32[]{:S(2)}, u32[]{:S(2)}) %all-to-all-start.2) | async-done | bytes 458784 | tf_op jit(solution)/shard_map/all_to_all | solution.py:24
  55.6 1.3 shard_map.134
  56.9 6.3 %all-to-all-start.3 = ((bf16[8,2,7296]{2,1,0:T(2,128)(2,1)}), bf16[8,2,7296]{2,1,0:T(2,128)(2,1)S(1)}, u32[]{:S(2)}, u32[]{:S(2)}) async-start(bf16[8,2,7296]{2,1,0:T(2,128)(2,1)} %shard_map.134), calls=%async_computation.3 | async-start | bytes 466944 | tf_op jit(solution)/shard_map/all_to_all | solution.py:24
  63.2 10.4 %all-to-all-done.3.got_ref = bf16[8,2,7296]{2,1,0:T(2,128)(2,1)S(1)} async-done(((bf16[8,2,7296]{2,1,0:T(2,128)(2,1)}), bf16[8,2,7296]{2,1,0:T(2,128)(2,1)S(1)}, u32[]{:S(2)}, u32[]{:S(2)}) %all-to-all-start.3) | async-done | bytes 233504 | tf_op jit(solution)/shard_map/all_to_all | solution.py:24
  73.6 1.3 shard_map.135
  74.9 17.4 %all_to_all.37 = bf16[16,8,3712]{2,1,0:T(8,128)(2,1)S(1)} all-to-all(bf16[16,8,3712]{2,1,0:T(8,128)(2,1)S(1)} %get-tuple-element.14), channel_id=1, replica_groups=mesh['role'=2,'y'=4,'x'=4,'core'=2,'tensor'=4] {'y','x'}, dimensions={0} | all-to-all | bytes 1900544 | tf_op jit(solution)/shard_map/all_to_all | solution.py:24
  92.3 1.5 %copy-done.1 = bf16[1,7168,128]{2,1,0:T(8,128)(2,1)S(1)} copy-done((bf16[1,7168,128]{2,1,0:T(8,128)(2,1)S(1)}, bf16[1,7168,128]{2,1,0:T(8,128)(2,1)}, u32[]{:S(2)}) %copy-start.1) | copy-done | bytes 1835032
  93.8 1.7 %shard_map.136 = (bf16[128,128]{1,0:T(8,128)(2,1)S(1)}, f32[128,128]{1,0:T(8,128)S(1)}) custom-call(s32[4]{0:T(128)S(1)} %copy-done.6, bf16[128,3712]{1,0:T(8,128)(2,1)S(1)} %bitcast.13, bf16[1,7168,128]{2,1,0:T(8,128)(2,1)S(1)} %copy-done, bf16[1,7168,128]{2,1,0:T(8,128)(2,1)S(1)} %copy-done.1), custom_call_target="tpu_custom_call" | custom-call | flops 469762048 | bytes 3670016 | tf_op jit(solution)/shard_map/pallas_call | solution.py:220
  95.5 2.3 %shard_map.138 = bf16[128,3584]{1,0:T(8,128)(2,1)S(1)} custom-call(s32[4]{0:T(128)S(1)} %copy-done.6, bf16[128,3712]{1,0:T(8,128)(2,1)S(1)} %collective-permute-done.1.rows_ref, bf16[1,7168,128]{2,1,0:T(8,128)(2,1)S(1)} %copy-done, bf16[1,7168,128]{2,1,0:T(8,128)(2,1)S(1)} %copy-done.1, bf16[1,128,7168]{2,1,0:T(8,128)(2,1)S(1)} %copy-done.2), custom_call_target="tpu_custom_call" | custom-call | flops 704643072 | bytes 5505024 | tf_op jit(solution)/shard_map/pallas_call | solution.py:220
  97.8 0.6 collective-permute-start.2
  98.4 0.6 shard_map.137
  99.0 1.5 %collective-permute-done.2 = bf16[128,3584]{1,0:T(8,128)(2,1)S(1)} collective-permute-done((bf16[128,3584]{1,0:T(8,128)(2,1)S(1)}, bf16[128,3584]{1,0:T(8,128)(2,1)S(1)}, u32[]{:S(2)}, u32[]{:S(2)}) %collective-permute-start.2) | collective-permute-done | bytes 917536 | tf_op jit(solution)/shard_map/ppermute | solution.py:20
  100.5 0.2 fusion
  100.6 19.1 %all_to_all.38.got_ref = bf16[16,8,3584]{2,1,0:T(8,128)(2,1)S(1)} all-to-all(bf16[16,8,3584]{2,1,0:T(8,128)(2,1)S(1)} %fusion), channel_id=1, replica_groups=mesh['role'=2,'y'=4,'x'=4,'core'=2,'tensor'=4] {'y','x'}, dimensions={0} | all-to-all | bytes 1835008 | tf_op jit(solution)/shard_map/all_to_all | solution.py:24
  119.8 0.2 shard_map.139
  120.0 13.2 %all_to_all.39 = bf16[8,2,7168]{2,1,0:T(2,128)(2,1)S(1)} all-to-all(bf16[8,2,7168]{2,1,0:T(2,128)(2,1)S(1)} %shard_map.139), channel_id=1, replica_groups=mesh['role'=2,'y'=4,'x'=4,'core'=2,'tensor'=4] {'role','tensor'}, dimensions={0} | all-to-all | bytes 458752 | tf_op jit(solution)/shard_map/all_to_all | solution.py:24
  133.2 0.8 convert_reduce_fusion
  (21 shorter events, 0.1 us)
Async XLA Ops:
  1.3 34.5 %copy-start.3 = (bf16[128,7168]{1,0:T(8,128)(2,1)S(1)}, bf16[128,7168]{1,0:T(8,128)(2,1)}, u32[]{:S(2)}) copy-start(bf16[128,7168]{1,0:T(8,128)(2,1)} %out_proj_ref.1) | copy-start | bytes 5505028
  1.3 34.5 %copy-start.4 = (bf16[1,512,128]{2,1,0:T(8,128)(2,1)S(1)}, bf16[1,512,128]{2,1,0:T(8,128)(2,1)}, u32[]{:S(2)}) copy-start(bf16[1,512,128]{2,1,0:T(8,128)(2,1)} %value_ref.1) | copy-start | bytes 393220
  1.3 34.5 %copy-start.6 = (s32[4]{0:T(128)S(1)}, s32[4]{0:T(128)}, u32[]{:S(2)}) copy-start(s32[4]{0:T(128)} %pad_add_fusion.where_ref) | copy-start | bytes 52
  37.8 7.6 %copy-start.9 = (bf16[2,8]{1,0:T(2,128)(2,1)S(1)}, bf16[2,8]{1,0:T(2,128)(2,1)}, u32[]{:S(2)}) copy-start(bf16[2,8]{1,0:T(2,128)(2,1)} %param.23) | copy-start | bytes 100
  37.9 7.6 %copy-start.8 = (s32[2,8]{1,0:T(2,128)S(1)}, s32[2,8]{1,0:T(2,128)}, u32[]{:S(2)}) copy-start(s32[2,8]{1,0:T(2,128)} %param.22) | copy-start | bytes 196
  37.9 17.7 %copy-start.5 = (bf16[2,7168]{1,0:T(2,128)(2,1)S(1)}, bf16[2,7168]{1,0:T(2,128)(2,1)}, u32[]{:S(2)}) copy-start(bf16[2,7168]{1,0:T(2,128)(2,1)} %extra_ref.1) | copy-start | bytes 86020
  37.9 1.9 %collective-permute-start = (bf16[128,1792]{1,0:T(8,128)(2,1)S(1)}, bf16[128,1792]{1,0:T(8,128)(2,1)S(1)}, u32[]{:S(2)}, u32[]{:S(2)}) collective-permute-start(bf16[128,1792]{1,0:T(8,128)(2,1)S(1)} %get-tuple-element.12), channel_id=1, source_target_pairs={{0,4},{4,0},{1,5},{5,1},{2,6},{6,2},{3,7},{7,3},{8,12},{12,8},{9,1... | collective-permute-start | bytes 1376264 | tf_op jit(solution)/shard_map/ppermute | solution.py:20
  39.8 23.4 %copy-start.7 = (bf16[7168]{0:T(1024)(128)(2,1)S(1)}, bf16[7168]{0:T(1024)(128)(2,1)}, u32[]{:S(2)}) copy-start(bf16[7168]{0:T(1024)(128)(2,1)} %param.18) | copy-start | bytes 43012
  40.6 14.9 %all-to-all-start.2 = ((bf16[16,8,1792]{2,1,0:T(8,128)(2,1)}), bf16[16,8,1792]{2,1,0:T(8,128)(2,1)S(1)}, u32[]{:S(2)}, u32[]{:S(2)}) async-start(bf16[16,8,1792]{2,1,0:T(8,128)(2,1)} %fusion.1), calls=%async_computation.2 | async-start | bytes 917504 | tf_op jit(solution)/shard_map/all_to_all | solution.py:24
  45.4 46.9 %copy-start = (bf16[1,7168,128]{2,1,0:T(8,128)(2,1)S(1)}, bf16[1,7168,128]{2,1,0:T(8,128)(2,1)}, u32[]{:S(2)}) copy-start(bf16[1,7168,128]{2,1,0:T(8,128)(2,1)} %gate_ref.3) | copy-start | bytes 5505028
  56.9 16.7 %all-to-all-start.3 = ((bf16[8,2,7296]{2,1,0:T(2,128)(2,1)}), bf16[8,2,7296]{2,1,0:T(2,128)(2,1)S(1)}, u32[]{:S(2)}, u32[]{:S(2)}) async-start(bf16[8,2,7296]{2,1,0:T(2,128)(2,1)} %shard_map.134), calls=%async_computation.3 | async-start | bytes 466944 | tf_op jit(solution)/shard_map/all_to_all | solution.py:24
  92.3 3.2 %collective-permute-start.1 = (bf16[128,3712]{1,0:T(8,128)(2,1)S(1)}, bf16[128,3712]{1,0:T(8,128)(2,1)S(1)}, u32[]{:S(2)}, u32[]{:S(2)}) collective-permute-start(bf16[128,3712]{1,0:T(8,128)(2,1)S(1)} %bitcast.12), channel_id=1, source_target_pairs={{0,4},{4,0},{1,5},{5,1},{2,6},{6,2},{3,7},{7,3},{8,12},{12,8},{9,1... | collective-permute-start | bytes 2850824 | tf_op jit(solution)/shard_map/ppermute | solution.py:20
  92.3 1.5 %copy-start.1 = (bf16[1,7168,128]{2,1,0:T(8,128)(2,1)S(1)}, bf16[1,7168,128]{2,1,0:T(8,128)(2,1)}, u32[]{:S(2)}) copy-start(bf16[1,7168,128]{2,1,0:T(8,128)(2,1)} %up_ref.3) | copy-start | bytes 5505028
  93.8 1.7 %copy-start.2 = (bf16[1,128,7168]{2,1,0:T(8,128)(2,1)S(1)}, bf16[1,128,7168]{2,1,0:T(8,128)(2,1)}, u32[]{:S(2)}) copy-start(bf16[1,128,7168]{2,1,0:T(8,128)(2,1)} %down_ref.3) | copy-start | bytes 5505028
  97.8 2.7 %collective-permute-start.2 = (bf16[128,3584]{1,0:T(8,128)(2,1)S(1)}, bf16[128,3584]{1,0:T(8,128)(2,1)S(1)}, u32[]{:S(2)}, u32[]{:S(2)}) collective-permute-start(bf16[128,3584]{1,0:T(8,128)(2,1)S(1)} %shard_map.138), channel_id=1, source_target_pairs={{0,4},{4,0},{1,5},{5,1},{2,6},{6,2},{3,7},{7,3},{8,12},{12,8},{9,1... | collective-permute-start | bytes 2752520 | tf_op jit(solution)/shard_map/ppermute | solution.py:20

commit v3 on v2

--- a/solution.py
+++ b/solution.py
@@ -1,3 +1,5 @@
+import functools
+
 import jax
 import jax.numpy as jnp
 from jax import lax
@@ -8,7 +10,6 @@
 SCORE_SCALE = 192.0 ** (-0.5)
 SIDE = 4
 BF = jnp.bfloat16
-T_AT, CORE_AT, ROLE_AT, EXPERT_AT = range(4)
 F32 = jnp.float32
 
 
@@ -18,6 +19,10 @@
 
 def other_core(value):
     return lax.ppermute(value, "core", [(0, 1), (1, 0)])
+
+
+def along(value, bits):
+    return lax.ppermute(value, LINE, [(i, i ^ bits) for i in range(8)])
 
 
 def trade(value, axes):
@@ -31,7 +36,7 @@
     return high, middle, rest - middle
 
 
-def attend(where_ref, length_ref, q_ref, keys_ref, out_ref):
+def attend(length_ref, q_ref, keys_ref, out_ref):
     heads, slots = q_ref.shape[2], keys_ref.shape[2]
     latent = out_ref.shape[3] - 128
     experts = out_ref.shape[2]
@@ -40,7 +45,7 @@
     pick = (column == (row % experts) * 4 + row // experts).astype(BF)
     q = lax.dot_general(pick, q_ref[0], (((1,), (1,)), ((), ())), preferred_element_type=F32)
     logits = jnp.dot(q.astype(BF), keys_ref[0], preferred_element_type=F32) * SCORE_SCALE
-    position = where_ref[T_AT] * slots + lax.broadcasted_iota(jnp.int32, (1, slots), 1)
+    position = lax.axis_index("tensor") * slots + lax.broadcasted_iota(jnp.int32, (1, slots), 1)
     live = position < length_ref[pl.program_id(0)]
     masked = jnp.where(live, logits, -1e30)
     top = jnp.max(masked, axis=1, keepdims=True)
@@ -82,63 +87,73 @@
     return value
 
 
-def project(where_ref, rows_ref, value_ref, out_proj_ref, away_ref, own_ref):
+def project(dc, rows_ref, value_ref, out_proj_ref, out_ref):
     n = rows_ref.shape[0]
     heads = jnp.dot(rows_ref[...], value_ref[0], preferred_element_type=F32).astype(BF)
-    out_rows, width = own_ref.shape
+    out_rows, width = out_ref.shape
     r = lax.broadcasted_iota(jnp.int32, (out_rows, n), 0)
     source = lax.broadcasted_iota(jnp.int32, (out_rows, n), 1)
     quarter = lax.broadcasted_iota(jnp.int32, (out_rows, 1), 0) // 2 % 4
-    for dc, out_ref in ((1, away_ref), (0, own_ref)):
-        core = (where_ref[CORE_AT] + dc) % 2
-        pick = (source == (r // 8) * 4 + core * 2 + r % 2).astype(BF)
-        picked = jnp.dot(pick, heads, preferred_element_type=F32).astype(BF)
-        for k in range(0, width, 256):
-            parts = [
-                jnp.dot(
-                    picked,
-                    out_proj_ref[:, j * width + k : j * width + k + 256],
-                    preferred_element_type=F32,
-                )
-                for j in range(4)
-            ]
-            out_ref[:, k : k + 256] = pick_part(parts, 4, quarter).astype(out_ref.dtype)
-
-
-def gather_sum(where_ref, got_ref, extra_ref, table_ref, out_ref, held_ref):
-    width = held_ref.shape[1]
+    core = (lax.axis_index("core") + dc) % 2
+    pick = (source == (r // 8) * 4 + core * 2 + r % 2).astype(BF)
+    picked = jnp.dot(pick, heads, preferred_element_type=F32).astype(BF)
+    for k in range(0, width, 256):
+        parts = [
+            jnp.dot(
+                picked,
+                out_proj_ref[:, j * width + k : j * width + k + 256],
+                preferred_element_type=F32,
+            )
+            for j in range(4)
+        ]
+        out_ref[:, k : k + 256] = pick_part(parts, 4, quarter).astype(out_ref.dtype)
+
+
+def add_places(got_ref):
     acc = got_ref[0].astype(F32)
     for p in range(1, got_ref.shape[0]):
         acc = acc + got_ref[p].astype(F32)
-    held_ref[...] = acc
-    first = (where_ref[T_AT] == 0).astype(F32)
+    return acc
+
+
+def gather_sum(got_ref, extra_ref, ids_ref, weights_ref, out_ref, held_ref):
+    width = held_ref.shape[1]
+    held_ref[...] = add_places(got_ref)
+    first = (lax.axis_index("tensor") == 0).astype(F32)
     for j in range(4):
         columns = slice(j * width, (j + 1) * width)
-        piece = (held_ref[2 * j : 2 * j + 2] + first * extra_ref[:, columns].astype(F32)).astype(BF)
-        for z in range(out_ref.shape[0]):
-            out_ref[z, :, columns] = piece
-    for z in range(out_ref.shape[0]):
-        out_ref[z, :, 4 * width :] = table_ref[...]
-
-
-def normalise(where_ref, got_ref, gain_ref, attended_ref, out_ref, held_ref):
+        term = first * extra_ref[:, columns].astype(F32)
+        out_ref[:, columns] = (held_ref[2 * j : 2 * j + 2] + term).astype(BF)
+    ids, weights = ids_ref[...], weights_ref[...].astype(F32)
+    lane = lax.broadcasted_iota(jnp.int32, (ids.shape[0], 128), 1)
+    table = jnp.zeros(lane.shape, F32)
+    for k in range(ids.shape[1]):
+        table = table + jnp.where(lane == ids[:, k : k + 1], weights[:, k : k + 1], 0.0)
+    out_ref[:, 4 * width :] = table.astype(BF)
+
+
+def add_pair(here_ref, there_ref, out_ref):
+    width = here_ref.shape[1] - 128
+    both = here_ref[:, :width].astype(F32) + there_ref[:, :width].astype(F32)
+    out_ref[:, :width] = both.astype(BF)
+    out_ref[:, width:] = here_ref[:, width:]
+
+
+def normalise(a_ref, b_ref, c_ref, d_ref, gain_ref, attended_ref, out_ref, held_ref):
     width = attended_ref.shape[1]
     half = width // 2
-    gain = gain_ref[...].astype(F32)
-    both = []
-    for role in range(2):
-        acc = got_ref[4 * role, :, :width].astype(F32)
-        for t in range(1, 4):
-            acc = acc + got_ref[4 * role + t, :, :width].astype(F32)
-        both.append(acc)
+    gain = gain_ref[...].astype(F32).reshape(1, width)
+    for role, (here_ref, there_ref) in enumerate(((a_ref, b_ref), (c_ref, d_ref))):
+        acc = here_ref[:, :width].astype(F32) + there_ref[:, :width].astype(F32)
+        if role == 0:
+            attended_ref[...] = acc
         mean_square = jnp.mean(acc * acc, axis=1, keepdims=True)
         normed = acc * lax.rsqrt(mean_square + 1e-06) * gain
-        table = got_ref[4 * role, :, width:].astype(F32)
+        table = here_ref[:, width:].astype(F32)
         for h in range(2):
             at = 4 * h + 2 * role
             held_ref[at : at + 2, :half] = normed[:, h * half : (h + 1) * half]
             held_ref[at : at + 2, half:] = table
-    attended_ref[...] = jnp.where(where_ref[ROLE_AT] == 0, both[0], both[1])
     block = held_ref[...].astype(BF)
     for p in range(out_ref.shape[0]):
         out_ref[p] = block
@@ -146,23 +161,24 @@
 
 def spread_sum(got_ref, out_ref, held_ref):
     half = held_ref.shape[1]
-    acc = got_ref[0].astype(F32)
-    for p in range(1, got_ref.shape[0]):
-        acc = acc + got_ref[p].astype(F32)
-    held_ref[...] = acc
-    for role in range(2):
-        for h in range(2):
-            at = 4 * h + 2 * role
-            piece = held_ref[at : at + 2].astype(BF)
-            for t in range(4):
-                out_ref[4 * role + t, :, h * half : (h + 1) * half] = piece
+    held_ref[...] = add_places(got_ref)
+    first = lax.axis_index("role") == 0
+    for h in range(2):
+        columns = slice(h * half, (h + 1) * half)
+        own = held_ref[4 * h : 4 * h + 2]
+        other = held_ref[4 * h + 2 : 4 * h + 4]
+        low = jnp.where(first, own, other).astype(BF)
+        high = jnp.where(first, other, own).astype(BF)
+        for t in range(4):
+            out_ref[t, :, columns] = low
+            out_ref[4 + t, :, columns] = high
 
 
 def which_half(rows):
     return lax.broadcasted_iota(jnp.int32, (rows, 1), 0) // 4 % 2
 
 
-def hidden(where_ref, rows_ref, gate_ref, up_ref):
+def hidden(rows_ref, gate_ref, up_ref):
     n, step = rows_ref.shape[0], 512
     width = gate_ref.shape[1] // 2
     half = which_half(n)
@@ -180,7 +196,7 @@
 
     gate, upper = whole(gate_ref), whole(up_ref)
     lane = lax.broadcasted_iota(jnp.int32, (n, 128), 1)
-    chosen = jnp.where(lane == where_ref[EXPERT_AT], rows_ref[:, width:].astype(F32), 0.0)
+    chosen = jnp.where(lane == lax.axis_index(("y", "x", "core")), rows_ref[:, width:].astype(F32), 0.0)
     coef = jnp.sum(chosen, axis=1, keepdims=True)
     act = (gate / (1.0 + jnp.exp(-gate)) * upper).astype(BF)
     return act, coef
@@ -197,14 +213,14 @@
         out_ref[:, at : at + step] = (coef * pick_part(parts, 2, half)).astype(out_ref.dtype)
 
 
-def activate(where_ref, rows_ref, gate_ref, up_ref, act_ref, coef_ref):
-    act, coef = hidden(where_ref, rows_ref, gate_ref, up_ref)
+def activate(rows_ref, gate_ref, up_ref, act_ref, coef_ref):
+    act, coef = hidden(rows_ref, gate_ref, up_ref)
     act_ref[...] = act
     coef_ref[...] = jnp.broadcast_to(coef, coef_ref.shape)
 
 
-def through(where_ref, rows_ref, gate_ref, up_ref, down_ref, out_ref):
-    act, coef = hidden(where_ref, rows_ref, gate_ref, up_ref)
+def through(rows_ref, gate_ref, up_ref, down_ref, out_ref):
+    act, coef = hidden(rows_ref, gate_ref, up_ref)
     fall(act, coef, down_ref, out_ref)
 
 
@@ -242,11 +258,6 @@
     expert_ids,
     route_weights,
 ):
-    t = lax.axis_index("tensor")
-    role = lax.axis_index("role")
-    c = lax.axis_index("core")
-    e = lax.axis_index(("y", "x", "core"))
-    where = jnp.stack([t, c, role, e])
     local_requests = request_latent_cache.shape[0]
     latent = value_up_weight.shape[1]
     experts, width = 32, residual_in.shape[1]
@@ -259,14 +270,12 @@
         out_shape=jax.ShapeDtypeStruct((4, local_requests, experts, latent + 128), BF),
         in_specs=[
             SCALAR,
-            SCALAR,
             pl.BlockSpec((1, depth, n_heads), lambda r: (r, 0, 0)),
             pl.BlockSpec((1, depth, slots), lambda r: (r, 0, 0)),
         ],
         out_specs=pl.BlockSpec((4, 1, experts, latent + 128), lambda r: (0, r, 0, 0)),
         compiler_params=pltpu.CompilerParams(vmem_limit_bytes=58 * 1024 * 1024),
     )(
-        where,
         cache_lengths,
         jnp.swapaxes(queries, 1, 2),
         jnp.swapaxes(request_latent_cache, 1, 2),
@@ -280,39 +289,35 @@
     shape = jax.ShapeDtypeStruct
     places, packed = 16, 4 * local_requests
     quarter, middle = width // 4, width // 2
-    away, acc = kernel(
-        project,
-        (shape((places * packed, quarter), BF), shape((places * packed, quarter), F32)),
-        [where, rows, value_up_weight, out_proj],
-        specs=[SCALAR, WHOLE, WHOLE, WHOLE],
-    )
+    away, acc = [
+        kernel(
+            functools.partial(project, dc),
+            shape((places * packed, quarter), kind),
+            [rows, value_up_weight, out_proj],
+            work=(2 * places * packed * 128 * width, 2 * 128 * width),
+        )
+        for dc, kind in ((1, BF), (0, F32))
+    ]
     acc = (acc + other_core(away).astype(F32)).astype(BF)
     acc = trade(acc.reshape(places, packed, quarter), PLANE)
-    names = jnp.arange(128, dtype=jnp.int32)
-    table = jnp.sum(
-        jnp.where(
-            expert_ids[:, :, None] == names[None, None, :],
-            route_weights.astype(F32)[:, :, None],
-            0.0,
-        ),
-        axis=1,
-    ).astype(BF)
+    routed_width = width + 128
     block = kernel(
         gather_sum,
-        shape((8, local_requests, width + 128), BF),
-        [where, acc, residual_in, table],
-        specs=[SCALAR, WHOLE, WHOLE, WHOLE],
+        shape((local_requests, routed_width), BF),
+        [acc, residual_in, expert_ids, route_weights],
         scratch=[pltpu.VMEM((packed, quarter), F32)],
     )
-    block = trade(block, LINE)
+    block = kernel(
+        add_pair, shape((local_requests, routed_width), BF), [block, along(block, 1)]
+    )
+    far, near, mate = along(block, 5), along(block, 6), along(block, 2)
     attended, block = kernel(
         normalise,
         (
             shape((local_requests, width), F32),
             shape((places, packed, middle + 128), BF),
         ),
-        [where, block, norm_gain[None]],
-        specs=[SCALAR, WHOLE, WHOLE],
+        [block, mate, near, far, norm_gain],
         scratch=[pltpu.VMEM((packed, middle + 128), F32)],
     )
     block = trade(block, PLANE).reshape(places * packed, middle + 128)
@@ -323,16 +328,14 @@
     act, coef = kernel(
         activate,
         (shape((n_rows, units), BF), shape((n_rows, 128), F32)),
-        [where, block, gate_proj, up_proj],
-        specs=[SCALAR, WHOLE, WHOLE, WHOLE],
+        [block, gate_proj, up_proj],
         work=(2 * flops, 2 * size),
     )
     across, act, coef = lax.optimization_barrier((across, act, coef))
     sent = kernel(
         through,
         shape((n_rows, middle), BF),
-        [where, across, gate_proj, up_proj, down_proj],
-        specs=[SCALAR, WHOLE, WHOLE, WHOLE, WHOLE],
+        [across, gate_proj, up_proj, down_proj],
         work=(3 * flops, 3 * size),
     )
     sent = other_core(sent)

time: 135 us -> 126 us (0.933)
  blocking collectives: 79.6 us -> 94.7 us
  waiting for transfers between devices: 23.6 us -> 11.2 us
  starting transfers between devices: 11.8 us -> 6.97 us
  Pallas kernels: 13.9 us -> 10.8 us
  local copies, waits for them, and re-layouts: 1.66 us -> 0.15 us
  other arithmetic: 2.54 us -> 1.04 us
    all_to_all x2 -> x0, waiting for transfers between devices: 20.5 us -> none  [trade(): return lax.all_to_all(value, axes, 0, 0, tiled=True)]
    all_to_all x5 -> x6, blocking collectives: 79.6 us -> 94.7 us  [trade(): return lax.all_to_all(value, axes, 0, 0, tiled=True)]
    all_to_all x2 -> x0, starting transfers between devices: 11.1 us -> none  [trade(): return lax.all_to_all(value, axes, 0, 0, tiled=True)]
    ppermute x0 -> x4, waiting for transfers between devices: none -> 7.41 us  [along(): return lax.ppermute(value, LINE, [(i, i ^ bits) for i in range(8)])]
    ppermute x0 -> x4, starting transfers between devices: none -> 6.54 us  [along(): return lax.ppermute(value, LINE, [(i, i ^ bits) for i in range(8)])]
    pallas_call x8 -> x10, Pallas kernels: 9.7 us -> 6.61 us  [kernel(): pl.pallas_call(body, out_shape=shapes, in_specs=specs or [WHOLE] * len(in...]
    unnamed x20 -> x18, local copies, waits for them, and re-layouts: 1.54 us -> 0.05 us
  transfers between devices with their start and end apart: 5 -> 7, of which waited for: 4 -> 6; matrix products, arithmetic and copies ran while one was open for 0% -> 0% of each run, Pallas kernels for 2% -> 2%
where the time goes in v3:
time: 126 us
  blocking collectives  94.7 us (75%)
  waiting for transfers between devices  11.2 us (9%)
  Pallas kernels  10.8 us (9%)
  starting transfers between devices  6.97 us (6%)
    all_to_all x6, blocking collectives, trade(): return lax.all_to_all(value, axes, 0, 0, tiled=True)  94.7 us
    ppermute x4, waiting for transfers between devices, along(): return lax.ppermute(value, LINE, [(i, i ^ bits) for i in range(8)])  7.41 us
    pallas_call x10, Pallas kernels, kernel(): pl.pallas_call(body, out_shape=shapes, in_specs=specs or [WHOLE] * len(in...  6.61 us
    ppermute x4, starting transfers between devices, along(): return lax.ppermute(value, LINE, [(i, i ^ bits) for i in range(8)])  6.54 us
    pallas_call x1, Pallas kernels, shards(): pl.pallas_call(attend, grid=(local_requests,), out_shape=jax.ShapeDtypeSt...  4.22 us
    ppermute x3, waiting for transfers between devices, other_core(): return lax.ppermute(value, 'core', [(0, 1), (1, 0)])  3.83 us
  transfers between devices with their start and end apart: 7, of which 6 were waited for; matrix products, arithmetic and copies ran while one was open for 0% of the time, Pallas kernels for 2%

profile of v3, /device:TPU:2, one launch (start us, length us, event | category | flops | bytes accessed | tf_op | source)
XLA Modules:
  0.0 125.7 jit_solution(5151960772315952280)
XLA Ops:
  0.7 4.2 %shard_map.131 = bf16[4,2,32,640]{3,2,1,0:T(8,128)(2,1)} custom-call(s32[2]{0:T(128)} %length_ref.1, bf16[2,576,128]{2,1,0:T(8,128)(2,1)} %bitcast.12, bf16[2,576,1024]{2,1,0:T(8,128)(2,1)} %bitcast.11), custom_call_target="tpu_custom_call" | custom-call | tf_op jit(solution)/shard_map/pallas_call | solution.py:267
  4.9 16.2 %all_to_all.30.parts_ref = bf16[4,2,32,640]{3,2,1,0:T(8,128)(2,1)S(1)} all-to-all(bf16[4,2,32,640]{3,2,1,0:T(8,128)(2,1)} %shard_map.131), channel_id=1, replica_groups=mesh['role'=2,'y'=4,'x'=4,'core'=2,'tensor'=4] {'tensor'}, dimensions={0} | all-to-all | bytes 655360 | tf_op jit(solution)/shard_map/all_to_all | solution.py:29
  21.0 0.3 shard_map.132
  21.3 0.1 copy.15
  21.4 13.7 %all_to_all.31 = bf16[32,2,512]{2,1,0:T(2,128)(2,1)S(1)} all-to-all(bf16[32,2,512]{2,1,0:T(2,128)(2,1)S(1)} %copy.15), channel_id=1, replica_groups=mesh['role'=2,'y'=4,'x'=4,'core'=2,'tensor'=4] {'y','x','core'}, dimensions={0} | all-to-all | bytes 131072 | tf_op jit(solution)/shard_map/all_to_all | solution.py:29
  35.2 0.9 shard_map.134
  36.1 0.2 collective-permute-start
  36.3 0.9 shard_map.133
  37.2 0.8 collective-permute-done
  38.0 0.1 fusion.1
  38.1 14.4 %all_to_all.32.got_ref = bf16[16,8,1792]{2,1,0:T(8,128)(2,1)S(1)} all-to-all(bf16[16,8,1792]{2,1,0:T(8,128)(2,1)S(1)} %fusion.1), channel_id=1, replica_groups=mesh['role'=2,'y'=4,'x'=4,'core'=2,'tensor'=4] {'y','x'}, dimensions={0} | all-to-all | bytes 917504 | tf_op jit(solution)/shard_map/all_to_all | solution.py:29
  52.5 0.1 shard_map.135.here_ref
  52.6 0.5 collective-permute-start.1
  53.1 3.5 %collective-permute-done.1.there_ref = bf16[2,7296]{1,0:T(2,128)(2,1)S(1)} collective-permute-done((bf16[2,7296]{1,0:T(2,128)(2,1)S(1)}, bf16[2,7296]{1,0:T(2,128)(2,1)S(1)}, u32[]{:S(2)}, u32[]{:S(2)}) %collective-permute-start.1) | collective-permute-done | bytes 29216 | tf_op jit(solution)/shard_map/ppermute | solution.py:25
  56.6 4.0 %collective-permute-start.4 = (bf16[2,7296]{1,0:T(2,128)(2,1)S(1)}, bf16[2,7296]{1,0:T(2,128)(2,1)S(1)}, u32[]{:S(2)}, u32[]{:S(2)}) collective-permute-start(bf16[2,7296]{1,0:T(2,128)(2,1)S(1)} %shard_map.136.a_ref), channel_id=1, source_target_pairs={{0,129},{1,128},{2,131},{3,130},{128,1},{129,0},{130,3},{131,2},{4... | collective-permute-start | bytes 87560 | tf_op jit(solution)/shard_map/ppermute | solution.py:25
  60.6 0.2 collective-permute-start.3
  60.8 1.8 %collective-permute-start.2 = (bf16[2,7296]{1,0:T(2,128)(2,1)S(1)}, bf16[2,7296]{1,0:T(2,128)(2,1)S(1)}, u32[]{:S(2)}, u32[]{:S(2)}) collective-permute-start(bf16[2,7296]{1,0:T(2,128)(2,1)S(1)} %shard_map.136.a_ref), channel_id=1, source_target_pairs={{0,2},{1,3},{2,0},{3,1},{128,130},{129,131},{130,128},{131,129},{4... | collective-permute-start | bytes 87560 | tf_op jit(solution)/shard_map/ppermute | solution.py:25
  62.7 0.9 collective-permute-done.4.d_ref
  63.6 3.0 %collective-permute-done.3.c_ref = bf16[2,7296]{1,0:T(2,128)(2,1)S(1)} collective-permute-done((bf16[2,7296]{1,0:T(2,128)(2,1)S(1)}, bf16[2,7296]{1,0:T(2,128)(2,1)S(1)}, u32[]{:S(2)}, u32[]{:S(2)}) %collective-permute-start.3) | collective-permute-done | bytes 29216 | tf_op jit(solution)/shard_map/ppermute | solution.py:25
  66.6 0.7 shard_map.137
  67.3 16.4 %all_to_all.33 = bf16[16,8,3712]{2,1,0:T(8,128)(2,1)S(1)} all-to-all(bf16[16,8,3712]{2,1,0:T(8,128)(2,1)S(1)} %get-tuple-element.10), channel_id=1, replica_groups=mesh['role'=2,'y'=4,'x'=4,'core'=2,'tensor'=4] {'y','x'}, dimensions={0} | all-to-all | bytes 1900544 | tf_op jit(solution)/shard_map/all_to_all | solution.py:29
  83.7 1.1 shard_map.138
  84.8 1.4 %collective-permute-done.5.rows_ref = bf16[128,3712]{1,0:T(8,128)(2,1)S(1)} collective-permute-done((bf16[128,3712]{1,0:T(8,128)(2,1)S(1)}, bf16[128,3712]{1,0:T(8,128)(2,1)S(1)}, u32[]{:S(2)}, u32[]{:S(2)}) %collective-permute-start.5) | collective-permute-done | bytes 950304 | tf_op jit(solution)/shard_map/ppermute | solution.py:21
  86.2 1.7 %shard_map.140 = bf16[128,3584]{1,0:T(8,128)(2,1)S(1)} custom-call(bf16[128,3712]{1,0:T(8,128)(2,1)S(1)} %collective-permute-done.5.rows_ref, bf16[1,7168,128]{2,1,0:T(8,128)(2,1)S(1)} %copy-done, bf16[1,7168,128]{2,1,0:T(8,128)(2,1)S(1)} %copy-done.1, bf16[1,128,7168]{2,1,0:T(8,128)(2,1)S(1)} %copy-done.2), custom_call_target="tpu_custom_call" | custom-call | flops 704643072 | bytes 5505024 | tf_op jit(solution)/shard_map/pallas_call | solution.py:236
  88.0 0.2 collective-permute-start.6
  88.2 0.6 shard_map.139
  88.8 1.7 %collective-permute-done.6 = bf16[128,3584]{1,0:T(8,128)(2,1)S(1)} collective-permute-done((bf16[128,3584]{1,0:T(8,128)(2,1)S(1)}, bf16[128,3584]{1,0:T(8,128)(2,1)S(1)}, u32[]{:S(2)}, u32[]{:S(2)}) %collective-permute-start.6) | collective-permute-done | bytes 917536 | tf_op jit(solution)/shard_map/ppermute | solution.py:21
  90.5 0.2 fusion
  90.7 18.9 %all_to_all.34.got_ref = bf16[16,8,3584]{2,1,0:T(8,128)(2,1)S(1)} all-to-all(bf16[16,8,3584]{2,1,0:T(8,128)(2,1)S(1)} %fusion), channel_id=1, replica_groups=mesh['role'=2,'y'=4,'x'=4,'core'=2,'tensor'=4] {'y','x'}, dimensions={0} | all-to-all | bytes 1835008 | tf_op jit(solution)/shard_map/all_to_all | solution.py:29
  109.6 0.2 shard_map.141
  109.8 15.1 %all_to_all.35 = bf16[8,2,7168]{2,1,0:T(2,128)(2,1)S(1)} all-to-all(bf16[8,2,7168]{2,1,0:T(2,128)(2,1)S(1)} %shard_map.141), channel_id=1, replica_groups=mesh['role'=2,'y'=4,'x'=4,'core'=2,'tensor'=4] {'role','tensor'}, dimensions={0} | all-to-all | bytes 458752 | tf_op jit(solution)/shard_map/all_to_all | solution.py:29
  124.9 0.8 convert_reduce_fusion
  (22 shorter events, 0.1 us)
Async XLA Ops:
  0.6 34.5 %copy-start.3 = (bf16[128,7168]{1,0:T(8,128)(2,1)S(1)}, bf16[128,7168]{1,0:T(8,128)(2,1)}, u32[]{:S(2)}) copy-start(bf16[128,7168]{1,0:T(8,128)(2,1)} %out_proj_ref.3) | copy-start | bytes 5505028
  0.6 34.5 %copy-start.4 = (bf16[1,512,128]{2,1,0:T(8,128)(2,1)S(1)}, bf16[1,512,128]{2,1,0:T(8,128)(2,1)}, u32[]{:S(2)}) copy-start(bf16[1,512,128]{2,1,0:T(8,128)(2,1)} %value_ref.3) | copy-start | bytes 393220
  36.1 1.9 %collective-permute-start = (bf16[128,1792]{1,0:T(8,128)(2,1)S(1)}, bf16[128,1792]{1,0:T(8,128)(2,1)S(1)}, u32[]{:S(2)}, u32[]{:S(2)}) collective-permute-start(bf16[128,1792]{1,0:T(8,128)(2,1)S(1)} %shard_map.134), channel_id=1, source_target_pairs={{0,4},{4,0},{1,5},{5,1},{2,6},{6,2},{3,7},{7,3},{8,12},{12,8},{9,1... | collective-permute-start | bytes 1376264 | tf_op jit(solution)/shard_map/ppermute | solution.py:21
  37.2 15.3 %copy-start.5 = (bf16[2,7168]{1,0:T(2,128)(2,1)S(1)}, bf16[2,7168]{1,0:T(2,128)(2,1)}, u32[]{:S(2)}) copy-start(bf16[2,7168]{1,0:T(2,128)(2,1)} %extra_ref.1) | copy-start | bytes 86020
  37.2 15.3 %copy-start.7 = (s32[2,8]{1,0:T(2,128)S(1)}, s32[2,8]{1,0:T(2,128)}, u32[]{:S(2)}) copy-start(s32[2,8]{1,0:T(2,128)} %ids_ref.1) | copy-start | bytes 196
  37.2 15.3 %copy-start.8 = (bf16[2,8]{1,0:T(2,128)(2,1)S(1)}, bf16[2,8]{1,0:T(2,128)(2,1)}, u32[]{:S(2)}) copy-start(bf16[2,8]{1,0:T(2,128)(2,1)} %weights_ref.1) | copy-start | bytes 100
  37.2 29.4 %copy-start.6 = (bf16[7168]{0:T(1024)(128)(2,1)S(1)}, bf16[7168]{0:T(1024)(128)(2,1)}, u32[]{:S(2)}) copy-start(bf16[7168]{0:T(1024)(128)(2,1)} %gain_ref.1) | copy-start | bytes 43012
  38.0 45.7 %copy-start.1 = (bf16[1,7168,128]{2,1,0:T(8,128)(2,1)S(1)}, bf16[1,7168,128]{2,1,0:T(8,128)(2,1)}, u32[]{:S(2)}) copy-start(bf16[1,7168,128]{2,1,0:T(8,128)(2,1)} %up_ref.3) | copy-start | bytes 5505028
  38.1 45.7 %copy-start = (bf16[1,7168,128]{2,1,0:T(8,128)(2,1)S(1)}, bf16[1,7168,128]{2,1,0:T(8,128)(2,1)}, u32[]{:S(2)}) copy-start(bf16[1,7168,128]{2,1,0:T(8,128)(2,1)} %gate_ref.3) | copy-start | bytes 5505028
  52.6 4.0 %collective-permute-start.1 = (bf16[2,7296]{1,0:T(2,128)(2,1)S(1)}, bf16[2,7296]{1,0:T(2,128)(2,1)S(1)}, u32[]{:S(2)}, u32[]{:S(2)}) collective-permute-start(bf16[2,7296]{1,0:T(2,128)(2,1)S(1)} %shard_map.135.here_ref), channel_id=1, source_target_pairs={{0,1},{1,0},{2,3},{3,2},{128,129},{129,128},{130,131},{131,130},{4... | collective-permute-start | bytes 87560 | tf_op jit(solution)/shard_map/ppermute | solution.py:25
  56.6 7.0 %collective-permute-start.4 = (bf16[2,7296]{1,0:T(2,128)(2,1)S(1)}, bf16[2,7296]{1,0:T(2,128)(2,1)S(1)}, u32[]{:S(2)}, u32[]{:S(2)}) collective-permute-start(bf16[2,7296]{1,0:T(2,128)(2,1)S(1)} %shard_map.136.a_ref), channel_id=1, source_target_pairs={{0,129},{1,128},{2,131},{3,130},{128,1},{129,0},{130,3},{131,2},{4... | collective-permute-start | bytes 87560 | tf_op jit(solution)/shard_map/ppermute | solution.py:25
  60.6 6.0 %collective-permute-start.3 = (bf16[2,7296]{1,0:T(2,128)(2,1)S(1)}, bf16[2,7296]{1,0:T(2,128)(2,1)S(1)}, u32[]{:S(2)}, u32[]{:S(2)}) collective-permute-start(bf16[2,7296]{1,0:T(2,128)(2,1)S(1)} %shard_map.136.a_ref), channel_id=1, source_target_pairs={{0,130},{1,131},{2,128},{3,129},{128,2},{129,3},{130,0},{131,1},{4... | collective-permute-start | bytes 87560 | tf_op jit(solution)/shard_map/ppermute | solution.py:25
  60.8 5.8 %collective-permute-start.2 = (bf16[2,7296]{1,0:T(2,128)(2,1)S(1)}, bf16[2,7296]{1,0:T(2,128)(2,1)S(1)}, u32[]{:S(2)}, u32[]{:S(2)}) collective-permute-start(bf16[2,7296]{1,0:T(2,128)(2,1)S(1)} %shard_map.136.a_ref), channel_id=1, source_target_pairs={{0,2},{1,3},{2,0},{3,1},{128,130},{129,131},{130,128},{131,129},{4... | collective-permute-start | bytes 87560 | tf_op jit(solution)/shard_map/ppermute | solution.py:25
  83.7 2.5 %copy-start.2 = (bf16[1,128,7168]{2,1,0:T(8,128)(2,1)S(1)}, bf16[1,128,7168]{2,1,0:T(8,128)(2,1)}, u32[]{:S(2)}) copy-start(bf16[1,128,7168]{2,1,0:T(8,128)(2,1)} %down_ref.3) | copy-start | bytes 5505028
  83.7 2.5 %collective-permute-start.5 = (bf16[128,3712]{1,0:T(8,128)(2,1)S(1)}, bf16[128,3712]{1,0:T(8,128)(2,1)S(1)}, u32[]{:S(2)}, u32[]{:S(2)}) collective-permute-start(bf16[128,3712]{1,0:T(8,128)(2,1)S(1)} %bitcast.8), channel_id=1, source_target_pairs={{0,4},{4,0},{1,5},{5,1},{2,6},{6,2},{3,7},{7,3},{8,12},{12,8},{9,1... | collective-permute-start | bytes 2850824 | tf_op jit(solution)/shard_map/ppermute | solution.py:21
  88.0 2.6 %collective-permute-start.6 = (bf16[128,3584]{1,0:T(8,128)(2,1)S(1)}, bf16[128,3584]{1,0:T(8,128)(2,1)S(1)}, u32[]{:S(2)}, u32[]{:S(2)}) collective-permute-start(bf16[128,3584]{1,0:T(8,128)(2,1)S(1)} %shard_map.140), channel_id=1, source_target_pairs={{0,4},{4,0},{1,5},{5,1},{2,6},{6,2},{3,7},{7,3},{8,12},{12,8},{9,1... | collective-permute-start | bytes 2752520 | tf_op jit(solution)/shard_map/ppermute | solution.py:21

commit v4 on v3

--- a/solution.py
+++ b/solution.py
@@ -36,13 +36,14 @@
     return high, middle, rest - middle
 
 
-def attend(length_ref, q_ref, keys_ref, out_ref):
+def attend(length_ref, q_ref, keys_ref, *out_refs):
     heads, slots = q_ref.shape[2], keys_ref.shape[2]
-    latent = out_ref.shape[3] - 128
-    experts = out_ref.shape[2]
+    latent = out_refs[0].shape[2] - 128
+    experts = out_refs[0].shape[1]
     row = lax.broadcasted_iota(jnp.int32, (heads, heads), 0)
     column = lax.broadcasted_iota(jnp.int32, (heads, heads), 1)
-    pick = (column == (row % experts) * 4 + row // experts).astype(BF)
+    owner = (lax.axis_index("tensor") + row // experts) % 4
+    pick = (column == (row % experts) * 4 + owner).astype(BF)
     q = lax.dot_general(pick, q_ref[0], (((1,), (1,)), ((), ())), preferred_element_type=F32)
     logits = jnp.dot(q.astype(BF), keys_ref[0], preferred_element_type=F32) * SCORE_SCALE
     position = lax.axis_index("tensor") * slots + lax.broadcasted_iota(jnp.int32, (1, slots), 1)
@@ -55,29 +56,35 @@
         expo.astype(BF), keys_ref[0, :latent], (((1,), (1,)), ((), ())), preferred_element_type=F32
     )
     part = (numer / jnp.maximum(total, 1.0)).astype(BF)
-    out_ref[:, 0, :, :latent] = part.reshape(4, experts, latent)
+    for t, out_ref in enumerate(out_refs):
+        out_ref[0, :, :latent] = part[t * experts : (t + 1) * experts]
     lane = lax.broadcasted_iota(jnp.int32, (heads, 128), 1)
     stats = jnp.zeros((heads, 128), F32)
     for i, column in enumerate((*in_three(top), *in_three(total))):
         stats = jnp.where(lane == i, column, stats)
-    out_ref[:, 0, :, latent:] = stats.astype(BF).reshape(4, experts, 128)
-
-
-def combine(parts_ref, out_ref):
-    latent = out_ref.shape[2]
-    for r in range(out_ref.shape[0]):
+    stats = stats.astype(BF)
+    for t, out_ref in enumerate(out_refs):
+        out_ref[0, :, latent:] = stats[t * experts : (t + 1) * experts]
+
+
+def combine(*refs):
+    parts_refs, out_ref = refs[:-1], refs[-1]
+    experts, requests, latent = out_ref.shape
+    contexts = []
+    for r in range(requests):
         tops, totals = [], []
         for t in range(4):
-            s = parts_ref[t, r, :, latent:].astype(F32)
+            s = parts_refs[t][r, :, latent:].astype(F32)
             tops.append(s[:, 0:1] + s[:, 1:2] + s[:, 2:3])
             totals.append(s[:, 3:4] + s[:, 4:5] + s[:, 5:6])
         top = jnp.maximum(jnp.maximum(tops[0], tops[1]), jnp.maximum(tops[2], tops[3]))
         weights = [jnp.exp(a - top) * b for a, b in zip(tops, totals)]
         whole = weights[0] + weights[1] + weights[2] + weights[3]
-        acc = jnp.zeros((out_ref.shape[1], latent), F32)
+        acc = jnp.zeros((experts, latent), F32)
         for t in range(4):
-            acc = acc + (weights[t] / whole) * parts_ref[t, r, :, :latent].astype(F32)
-        out_ref[r] = acc.astype(BF)
+            acc = acc + (weights[t] / whole) * parts_refs[t][r, :, :latent].astype(F32)
+        contexts.append(acc)
+    out_ref[...] = jnp.stack(contexts, axis=1).astype(BF)
 
 
 def pick_part(parts, count, part):
@@ -183,18 +190,18 @@
     width = gate_ref.shape[1] // 2
     half = which_half(n)
 
-    def whole(ref):
-        sums = [jnp.zeros((n, ref.shape[2]), F32) for _ in range(2)]
-        for k in range(0, width, step):
-            rows = rows_ref[:, k : k + step]
-            for h in range(2):
-                weights = ref[0, h * width + k : h * width + k + step]
-                sums[h] = sums[h] + jnp.dot(rows, weights, preferred_element_type=F32)
-        value = pick_part(sums, 2, half)
-        other = jnp.where(half == 0, pltpu.roll(value, n - 4, 0), pltpu.roll(value, 4, 0))
-        return value + other
-
-    gate, upper = whole(gate_ref), whole(up_ref)
+    units = gate_ref.shape[2]
+    sums = [jnp.zeros((n, 2 * units), F32) for _ in range(2)]
+    for k in range(0, width, step):
+        rows = rows_ref[:, k : k + step]
+        for h in range(2):
+            at = slice(h * width + k, h * width + k + step)
+            weights = jnp.concatenate([gate_ref[0, at], up_ref[0, at]], axis=1)
+            sums[h] = sums[h] + jnp.dot(rows, weights, preferred_element_type=F32)
+    value = pick_part(sums, 2, half)
+    other = jnp.where(half == 0, pltpu.roll(value, n - 4, 0), pltpu.roll(value, 4, 0))
+    value = value + other
+    gate, upper = value[:, :units], value[:, units:]
     lane = lax.broadcasted_iota(jnp.int32, (n, 128), 1)
     chosen = jnp.where(lane == lax.axis_index(("y", "x", "core")), rows_ref[:, width:].astype(F32), 0.0)
     coef = jnp.sum(chosen, axis=1, keepdims=True)
@@ -267,24 +274,26 @@
     parts = pl.pallas_call(
         attend,
         grid=(local_requests,),
-        out_shape=jax.ShapeDtypeStruct((4, local_requests, experts, latent + 128), BF),
+        out_shape=[pltpu.VMEM((local_requests, experts, latent + 128), BF)] * 4,
         in_specs=[
             SCALAR,
             pl.BlockSpec((1, depth, n_heads), lambda r: (r, 0, 0)),
             pl.BlockSpec((1, depth, slots), lambda r: (r, 0, 0)),
         ],
-        out_specs=pl.BlockSpec((4, 1, experts, latent + 128), lambda r: (0, r, 0, 0)),
+        out_specs=[pl.BlockSpec((1, experts, latent + 128), lambda r: (r, 0, 0))] * 4,
         compiler_params=pltpu.CompilerParams(vmem_limit_bytes=58 * 1024 * 1024),
     )(
         cache_lengths,
         jnp.swapaxes(queries, 1, 2),
         jnp.swapaxes(request_latent_cache, 1, 2),
     )
-    parts = trade(parts, "tensor")
+    parts = [parts[0]] + [
+        lax.ppermute(parts[s], "tensor", [(i, (i + s) % 4) for i in range(4)]) for s in (1, 2, 3)
+    ]
     context = kernel(
-        combine, jax.ShapeDtypeStruct((local_requests, experts, latent), BF), [parts]
-    )
-    rows = trade(jnp.swapaxes(context, 0, 1), ("y", "x", "core"))
+        combine, jax.ShapeDtypeStruct((experts, local_requests, latent), BF), parts
+    )
+    rows = trade(context, ("y", "x", "core"))
     rows = rows.reshape(experts * local_requests, latent)
     shape = jax.ShapeDtypeStruct
     places, packed = 16, 4 * local_requests

time: 126 us -> 122 us (0.968)
  blocking collectives: 94.7 us -> 77.9 us
  starting transfers between devices: 6.97 us -> 16.1 us
  waiting for transfers between devices: 11.2 us -> 16.1 us
  Pallas kernels: 10.8 us -> 9.42 us
    all_to_all x6 -> x5, blocking collectives: 94.7 us -> 77.9 us  [trade(): return lax.all_to_all(value, axes, 0, 0, tiled=True)]
    ppermute x0 -> x3, starting transfers between devices: none -> 6.28 us  [shards(): lax.ppermute(parts[s], 'tensor', [(i, (i + s) % 4) for i in range(4)])]
    ppermute x0 -> x3, waiting for transfers between devices: none -> 4.82 us  [shards(): lax.ppermute(parts[s], 'tensor', [(i, (i + s) % 4) for i in range(4)])]
    ppermute x4, starting transfers between devices: 6.54 us -> 9.38 us  [along(): return lax.ppermute(value, LINE, [(i, i ^ bits) for i in range(8)])]
  transfers between devices with their start and end apart: 7 -> 10, of which waited for: 6 -> 9; matrix products, arithmetic and copies ran while one was open for 0% -> 0% of each run, Pallas kernels for 2% -> 2%
where the time goes in v4:
time: 122 us; the launch traced here: 121 us
  blocking collectives  77.9 us (64%)
  starting transfers between devices  16.1 us (13%)
  waiting for transfers between devices  16.1 us (13%)
  Pallas kernels  9.42 us (8%)
    all_to_all x5, blocking collectives, trade(): return lax.all_to_all(value, axes, 0, 0, tiled=True)  77.9 us
    ppermute x4, starting transfers between devices, along(): return lax.ppermute(value, LINE, [(i, i ^ bits) for i in range(8)])  9.38 us
    ppermute x4, waiting for transfers between devices, along(): return lax.ppermute(value, LINE, [(i, i ^ bits) for i in range(8)])  7.01 us
    ppermute x3, starting transfers between devices, shards(): lax.ppermute(parts[s], 'tensor', [(i, (i + s) % 4) for i in range(4)])  6.28 us
    pallas_call x10, Pallas kernels, kernel(): pl.pallas_call(body, out_shape=shapes, in_specs=specs or [WHOLE] * len(in...  5.85 us
    ppermute x3, waiting for transfers between devices, shards(): lax.ppermute(parts[s], 'tensor', [(i, (i + s) % 4) for i in range(4)])  4.82 us
    ppermute x3, waiting for transfers between devices, other_core(): return lax.ppermute(value, 'core', [(0, 1), (1, 0)])  4.3 us
    pallas_call x1, Pallas kernels, shards(): pl.pallas_call(attend, grid=(local_requests,), out_shape=[pltpu.VMEM((loc...  3.57 us
  transfers between devices with their start and end apart: 10, of which 9 were waited for; matrix products, arithmetic and copies ran while one was open for 0% of the time, Pallas kernels for 2%

profile of v4, /device:TPU:2, one launch (start us, length us, event | category | flops | bytes accessed | tf_op | source)
XLA Modules:
  0.0 121.5 jit_solution(5199103596905851008)
XLA Ops:
  0.7 3.6 %shard_map.131 = (bf16[2,32,640]{2,1,0:T(8,128)(2,1)S(1)}, bf16[2,32,640]{2,1,0:T(8,128)(2,1)S(1)}, bf16[2,32,640]{2,1,0:T(8,128)(2,1)S(1)}, bf16[2,32,640]{2,1,0:T(8,128)(2,1)S(1)}) custom-call(s32[2]{0:T(128)} %length_ref.1, bf16[2,576,128]{2,1,0:T(8,128)(2,1)} %bitcast.10, bf16[2,576,1024]{2,1,0:T(8,128)(2,1)} %bitcast.9), custom_call_target="tpu_custom_call" | custom-call | tf_op jit(solution)/shard_map/pallas_call | solution.py:274
  4.2 2.0 %collective-permute-start = (bf16[2,32,640]{2,1,0:T(8,128)(2,1)S(1)}, bf16[2,32,640]{2,1,0:T(8,128)(2,1)S(1)}, u32[]{:S(2)}, u32[]{:S(2)}) collective-permute-start(bf16[2,32,640]{2,1,0:T(8,128)(2,1)S(1)} %get-tuple-element.14), channel_id=1, source_target_pairs={{0,1},{1,2},{2,3},{3,0},{4,5},{5,6},{6,7},{7,4},{8,9},{9,10},{10,1... | collective-permute-start | bytes 245768 | tf_op jit(solution)/shard_map/ppermute | solution.py:291
  6.2 3.3 %collective-permute-start.1 = (bf16[2,32,640]{2,1,0:T(8,128)(2,1)S(1)}, bf16[2,32,640]{2,1,0:T(8,128)(2,1)S(1)}, u32[]{:S(2)}, u32[]{:S(2)}) collective-permute-start(bf16[2,32,640]{2,1,0:T(8,128)(2,1)S(1)} %get-tuple-element.15), channel_id=1, source_target_pairs={{0,2},{1,3},{2,0},{3,1},{4,6},{5,7},{6,4},{7,5},{8,10},{9,11},{10,... | collective-permute-start | bytes 245768 | tf_op jit(solution)/shard_map/ppermute | solution.py:291
  9.5 1.0 collective-permute-start.2
  10.5 1.7 %collective-permute-done.refs_1_ = bf16[2,32,640]{2,1,0:T(8,128)(2,1)S(1)} collective-permute-done((bf16[2,32,640]{2,1,0:T(8,128)(2,1)S(1)}, bf16[2,32,640]{2,1,0:T(8,128)(2,1)S(1)}, u32[]{:S(2)}, u32[]{:S(2)}) %collective-permute-start) | collective-permute-done | bytes 81952 | tf_op jit(solution)/shard_map/ppermute | solution.py:291
  12.2 2.8 %collective-permute-done.1.refs_2_ = bf16[2,32,640]{2,1,0:T(8,128)(2,1)S(1)} collective-permute-done((bf16[2,32,640]{2,1,0:T(8,128)(2,1)S(1)}, bf16[2,32,640]{2,1,0:T(8,128)(2,1)S(1)}, u32[]{:S(2)}, u32[]{:S(2)}) %collective-permute-start.1) | collective-permute-done | bytes 81952 | tf_op jit(solution)/shard_map/ppermute | solution.py:291
  15.0 0.3 collective-permute-done.2.refs_3_
  15.3 0.4 shard_map.132
  15.7 13.7 %all_to_all.25 = bf16[32,2,512]{2,1,0:T(2,128)(2,1)S(1)} all-to-all(bf16[32,2,512]{2,1,0:T(2,128)(2,1)S(1)} %shard_map.132), channel_id=1, replica_groups=mesh['role'=2,'y'=4,'x'=4,'core'=2,'tensor'=4] {'y','x','core'}, dimensions={0} | all-to-all | bytes 131072 | tf_op jit(solution)/shard_map/all_to_all | solution.py:29
  29.5 0.9 shard_map.134
  30.4 0.2 collective-permute-start.3
  30.6 0.9 shard_map.133
  31.5 0.8 collective-permute-done.3
  32.4 14.4 %all_to_all.26.got_ref = bf16[16,8,1792]{2,1,0:T(8,128)(2,1)S(1)} all-to-all(bf16[16,8,1792]{2,1,0:T(8,128)(2,1)S(1)} %fusion.1), channel_id=1, replica_groups=mesh['role'=2,'y'=4,'x'=4,'core'=2,'tensor'=4] {'y','x'}, dimensions={0} | all-to-all | bytes 917504 | tf_op jit(solution)/shard_map/all_to_all | solution.py:29
  47.0 2.0 %collective-permute-start.4 = (bf16[2,7296]{1,0:T(2,128)(2,1)S(1)}, bf16[2,7296]{1,0:T(2,128)(2,1)S(1)}, u32[]{:S(2)}, u32[]{:S(2)}) collective-permute-start(bf16[2,7296]{1,0:T(2,128)(2,1)S(1)} %shard_map.135.here_ref), channel_id=1, source_target_pairs={{0,1},{1,0},{2,3},{3,2},{128,129},{129,128},{130,131},{131,130},{4... | collective-permute-start | bytes 87560 | tf_op jit(solution)/shard_map/ppermute | solution.py:25
  48.9 2.0 %collective-permute-done.4.there_ref = bf16[2,7296]{1,0:T(2,128)(2,1)S(1)} collective-permute-done((bf16[2,7296]{1,0:T(2,128)(2,1)S(1)}, bf16[2,7296]{1,0:T(2,128)(2,1)S(1)}, u32[]{:S(2)}, u32[]{:S(2)}) %collective-permute-start.4) | collective-permute-done | bytes 29216 | tf_op jit(solution)/shard_map/ppermute | solution.py:25
  51.0 6.4 %collective-permute-start.7 = (bf16[2,7296]{1,0:T(2,128)(2,1)S(1)}, bf16[2,7296]{1,0:T(2,128)(2,1)S(1)}, u32[]{:S(2)}, u32[]{:S(2)}) collective-permute-start(bf16[2,7296]{1,0:T(2,128)(2,1)S(1)} %shard_map.136.a_ref), channel_id=1, source_target_pairs={{0,129},{1,128},{2,131},{3,130},{128,1},{129,0},{130,3},{131,2},{4... | collective-permute-start | bytes 87560 | tf_op jit(solution)/shard_map/ppermute | solution.py:25
  57.4 1.0 collective-permute-start.5
  58.4 0.9 collective-permute-done.7.d_ref
  59.3 4.1 %collective-permute-done.6.c_ref = bf16[2,7296]{1,0:T(2,128)(2,1)S(1)} collective-permute-done((bf16[2,7296]{1,0:T(2,128)(2,1)S(1)}, bf16[2,7296]{1,0:T(2,128)(2,1)S(1)}, u32[]{:S(2)}, u32[]{:S(2)}) %collective-permute-start.6) | collective-permute-done | bytes 29216 | tf_op jit(solution)/shard_map/ppermute | solution.py:25
  63.4 0.7 shard_map.137
  64.1 16.1 %all_to_all.27 = bf16[16,8,3712]{2,1,0:T(8,128)(2,1)S(1)} all-to-all(bf16[16,8,3712]{2,1,0:T(8,128)(2,1)S(1)} %get-tuple-element.18), channel_id=1, replica_groups=mesh['role'=2,'y'=4,'x'=4,'core'=2,'tensor'=4] {'y','x'}, dimensions={0} | all-to-all | bytes 1900544 | tf_op jit(solution)/shard_map/all_to_all | solution.py:29
  80.2 0.7 shard_map.138
  80.9 1.8 %collective-permute-done.8.rows_ref = bf16[128,3712]{1,0:T(8,128)(2,1)S(1)} collective-permute-done((bf16[128,3712]{1,0:T(8,128)(2,1)S(1)}, bf16[128,3712]{1,0:T(8,128)(2,1)S(1)}, u32[]{:S(2)}, u32[]{:S(2)}) %collective-permute-start.8) | collective-permute-done | bytes 950304 | tf_op jit(solution)/shard_map/ppermute | solution.py:21
  82.7 1.3 %shard_map.140 = bf16[128,3584]{1,0:T(8,128)(2,1)S(1)} custom-call(bf16[128,3712]{1,0:T(8,128)(2,1)S(1)} %collective-permute-done.8.rows_ref, bf16[1,7168,128]{2,1,0:T(8,128)(2,1)S(1)} %copy-done, bf16[1,7168,128]{2,1,0:T(8,128)(2,1)S(1)} %copy-done.1, bf16[1,128,7168]{2,1,0:T(8,128)(2,1)S(1)} %copy-done.2), custom_call_target="tpu_custom_call" | custom-call | flops 704643072 | bytes 5505024 | tf_op jit(solution)/shard_map/pallas_call | solution.py:243
  84.0 0.2 collective-permute-start.9
  84.2 0.6 shard_map.139
  84.8 1.7 %collective-permute-done.9 = bf16[128,3584]{1,0:T(8,128)(2,1)S(1)} collective-permute-done((bf16[128,3584]{1,0:T(8,128)(2,1)S(1)}, bf16[128,3584]{1,0:T(8,128)(2,1)S(1)}, u32[]{:S(2)}, u32[]{:S(2)}) %collective-permute-start.9) | collective-permute-done | bytes 917536 | tf_op jit(solution)/shard_map/ppermute | solution.py:21
  86.7 18.9 %all_to_all.28.got_ref = bf16[16,8,3584]{2,1,0:T(8,128)(2,1)S(1)} all-to-all(bf16[16,8,3584]{2,1,0:T(8,128)(2,1)S(1)} %fusion), channel_id=1, replica_groups=mesh['role'=2,'y'=4,'x'=4,'core'=2,'tensor'=4] {'y','x'}, dimensions={0} | all-to-all | bytes 1835008 | tf_op jit(solution)/shard_map/all_to_all | solution.py:29
  105.6 0.2 shard_map.141
  105.8 14.8 %all_to_all.29 = bf16[8,2,7168]{2,1,0:T(2,128)(2,1)S(1)} all-to-all(bf16[8,2,7168]{2,1,0:T(2,128)(2,1)S(1)} %shard_map.141), channel_id=1, replica_groups=mesh['role'=2,'y'=4,'x'=4,'core'=2,'tensor'=4] {'role','tensor'}, dimensions={0} | all-to-all | bytes 458752 | tf_op jit(solution)/shard_map/all_to_all | solution.py:29
  120.7 0.8 convert_reduce_fusion
  (26 shorter events, 0.5 us)
Async XLA Ops:
  0.6 28.9 %copy-start.3 = (bf16[128,7168]{1,0:T(8,128)(2,1)S(1)}, bf16[128,7168]{1,0:T(8,128)(2,1)}, u32[]{:S(2)}) copy-start(bf16[128,7168]{1,0:T(8,128)(2,1)} %out_proj_ref.3) | copy-start | bytes 5505028
  0.6 28.9 %copy-start.4 = (bf16[1,512,128]{2,1,0:T(8,128)(2,1)S(1)}, bf16[1,512,128]{2,1,0:T(8,128)(2,1)}, u32[]{:S(2)}) copy-start(bf16[1,512,128]{2,1,0:T(8,128)(2,1)} %value_ref.3) | copy-start | bytes 393220
  4.2 8.0 %collective-permute-start = (bf16[2,32,640]{2,1,0:T(8,128)(2,1)S(1)}, bf16[2,32,640]{2,1,0:T(8,128)(2,1)S(1)}, u32[]{:S(2)}, u32[]{:S(2)}) collective-permute-start(bf16[2,32,640]{2,1,0:T(8,128)(2,1)S(1)} %get-tuple-element.14), channel_id=1, source_target_pairs={{0,1},{1,2},{2,3},{3,0},{4,5},{5,6},{6,7},{7,4},{8,9},{9,10},{10,1... | collective-permute-start | bytes 245768 | tf_op jit(solution)/shard_map/ppermute | solution.py:291
  6.2 8.8 %collective-permute-start.1 = (bf16[2,32,640]{2,1,0:T(8,128)(2,1)S(1)}, bf16[2,32,640]{2,1,0:T(8,128)(2,1)S(1)}, u32[]{:S(2)}, u32[]{:S(2)}) collective-permute-start(bf16[2,32,640]{2,1,0:T(8,128)(2,1)S(1)} %get-tuple-element.15), channel_id=1, source_target_pairs={{0,2},{1,3},{2,0},{3,1},{4,6},{5,7},{6,4},{7,5},{8,10},{9,11},{10,... | collective-permute-start | bytes 245768 | tf_op jit(solution)/shard_map/ppermute | solution.py:291
  9.5 5.8 %collective-permute-start.2 = (bf16[2,32,640]{2,1,0:T(8,128)(2,1)S(1)}, bf16[2,32,640]{2,1,0:T(8,128)(2,1)S(1)}, u32[]{:S(2)}, u32[]{:S(2)}) collective-permute-start(bf16[2,32,640]{2,1,0:T(8,128)(2,1)S(1)} %get-tuple-element.16), channel_id=1, source_target_pairs={{0,3},{1,0},{2,1},{3,2},{4,7},{5,4},{6,5},{7,6},{8,11},{9,8},{10,9... | collective-permute-start | bytes 245768 | tf_op jit(solution)/shard_map/ppermute | solution.py:291
  30.4 1.9 %collective-permute-start.3 = (bf16[128,1792]{1,0:T(8,128)(2,1)S(1)}, bf16[128,1792]{1,0:T(8,128)(2,1)S(1)}, u32[]{:S(2)}, u32[]{:S(2)}) collective-permute-start(bf16[128,1792]{1,0:T(8,128)(2,1)S(1)} %shard_map.134), channel_id=1, source_target_pairs={{0,4},{4,0},{1,5},{5,1},{2,6},{6,2},{3,7},{7,3},{8,12},{12,8},{9,1... | collective-permute-start | bytes 1376264 | tf_op jit(solution)/shard_map/ppermute | solution.py:21
  31.5 15.3 %copy-start.5 = (bf16[2,7168]{1,0:T(2,128)(2,1)S(1)}, bf16[2,7168]{1,0:T(2,128)(2,1)}, u32[]{:S(2)}) copy-start(bf16[2,7168]{1,0:T(2,128)(2,1)} %extra_ref.1) | copy-start | bytes 86020
  31.5 15.3 %copy-start.7 = (s32[2,8]{1,0:T(2,128)S(1)}, s32[2,8]{1,0:T(2,128)}, u32[]{:S(2)}) copy-start(s32[2,8]{1,0:T(2,128)} %ids_ref.1) | copy-start | bytes 196
  31.5 15.3 %copy-start.8 = (bf16[2,8]{1,0:T(2,128)(2,1)S(1)}, bf16[2,8]{1,0:T(2,128)(2,1)}, u32[]{:S(2)}) copy-start(bf16[2,8]{1,0:T(2,128)(2,1)} %weights_ref.1) | copy-start | bytes 100
  31.5 31.9 %copy-start.6 = (bf16[7168]{0:T(1024)(128)(2,1)S(1)}, bf16[7168]{0:T(1024)(128)(2,1)}, u32[]{:S(2)}) copy-start(bf16[7168]{0:T(1024)(128)(2,1)} %gain_ref.1) | copy-start | bytes 43012
  32.3 47.9 %copy-start.1 = (bf16[1,7168,128]{2,1,0:T(8,128)(2,1)S(1)}, bf16[1,7168,128]{2,1,0:T(8,128)(2,1)}, u32[]{:S(2)}) copy-start(bf16[1,7168,128]{2,1,0:T(8,128)(2,1)} %up_ref.3) | copy-start | bytes 5505028
  32.4 47.8 %copy-start = (bf16[1,7168,128]{2,1,0:T(8,128)(2,1)S(1)}, bf16[1,7168,128]{2,1,0:T(8,128)(2,1)}, u32[]{:S(2)}) copy-start(bf16[1,7168,128]{2,1,0:T(8,128)(2,1)} %gate_ref.3) | copy-start | bytes 5505028
  47.0 4.0 %collective-permute-start.4 = (bf16[2,7296]{1,0:T(2,128)(2,1)S(1)}, bf16[2,7296]{1,0:T(2,128)(2,1)S(1)}, u32[]{:S(2)}, u32[]{:S(2)}) collective-permute-start(bf16[2,7296]{1,0:T(2,128)(2,1)S(1)} %shard_map.135.here_ref), channel_id=1, source_target_pairs={{0,1},{1,0},{2,3},{3,2},{128,129},{129,128},{130,131},{131,130},{4... | collective-permute-start | bytes 87560 | tf_op jit(solution)/shard_map/ppermute | solution.py:25
  51.0 8.3 %collective-permute-start.7 = (bf16[2,7296]{1,0:T(2,128)(2,1)S(1)}, bf16[2,7296]{1,0:T(2,128)(2,1)S(1)}, u32[]{:S(2)}, u32[]{:S(2)}) collective-permute-start(bf16[2,7296]{1,0:T(2,128)(2,1)S(1)} %shard_map.136.a_ref), channel_id=1, source_target_pairs={{0,129},{1,128},{2,131},{3,130},{128,1},{129,0},{130,3},{131,2},{4... | collective-permute-start | bytes 87560 | tf_op jit(solution)/shard_map/ppermute | solution.py:25
  57.4 6.0 %collective-permute-start.6 = (bf16[2,7296]{1,0:T(2,128)(2,1)S(1)}, bf16[2,7296]{1,0:T(2,128)(2,1)S(1)}, u32[]{:S(2)}, u32[]{:S(2)}) collective-permute-start(bf16[2,7296]{1,0:T(2,128)(2,1)S(1)} %shard_map.136.a_ref), channel_id=1, source_target_pairs={{0,130},{1,131},{2,128},{3,129},{128,2},{129,3},{130,0},{131,1},{4... | collective-permute-start | bytes 87560 | tf_op jit(solution)/shard_map/ppermute | solution.py:25
  57.4 6.0 %collective-permute-start.5 = (bf16[2,7296]{1,0:T(2,128)(2,1)S(1)}, bf16[2,7296]{1,0:T(2,128)(2,1)S(1)}, u32[]{:S(2)}, u32[]{:S(2)}) collective-permute-start(bf16[2,7296]{1,0:T(2,128)(2,1)S(1)} %shard_map.136.a_ref), channel_id=1, source_target_pairs={{0,2},{1,3},{2,0},{3,1},{128,130},{129,131},{130,128},{131,129},{4... | collective-permute-start | bytes 87560 | tf_op jit(solution)/shard_map/ppermute | solution.py:25
  80.2 2.5 %copy-start.2 = (bf16[1,128,7168]{2,1,0:T(8,128)(2,1)S(1)}, bf16[1,128,7168]{2,1,0:T(8,128)(2,1)}, u32[]{:S(2)}) copy-start(bf16[1,128,7168]{2,1,0:T(8,128)(2,1)} %down_ref.3) | copy-start | bytes 5505028
  80.2 2.5 %collective-permute-start.8 = (bf16[128,3712]{1,0:T(8,128)(2,1)S(1)}, bf16[128,3712]{1,0:T(8,128)(2,1)S(1)}, u32[]{:S(2)}, u32[]{:S(2)}) collective-permute-start(bf16[128,3712]{1,0:T(8,128)(2,1)S(1)} %bitcast.7), channel_id=1, source_target_pairs={{0,4},{4,0},{1,5},{5,1},{2,6},{6,2},{3,7},{7,3},{8,12},{12,8},{9,1... | collective-permute-start | bytes 2850824 | tf_op jit(solution)/shard_map/ppermute | solution.py:21
  84.0 2.6 %collective-permute-start.9 = (bf16[128,3584]{1,0:T(8,128)(2,1)S(1)}, bf16[128,3584]{1,0:T(8,128)(2,1)S(1)}, u32[]{:S(2)}, u32[]{:S(2)}) collective-permute-start(bf16[128,3584]{1,0:T(8,128)(2,1)S(1)} %shard_map.140), channel_id=1, source_target_pairs={{0,4},{4,0},{1,5},{5,1},{2,6},{6,2},{3,7},{7,3},{8,12},{12,8},{9,1... | collective-permute-start | bytes 2752520 | tf_op jit(solution)/shard_map/ppermute | solution.py:21

commit v5 on v4

--- a/solution.py
+++ b/solution.py
@@ -13,7 +13,7 @@
 F32 = jnp.float32
 
 
-PLANE = ("y", "x")
+PLANE = ("x", "y")
 LINE = ("role", "tensor")
 
 
@@ -36,25 +36,35 @@
     return high, middle, rest - middle
 
 
-def attend(length_ref, q_ref, keys_ref, *out_refs):
-    heads, slots = q_ref.shape[2], keys_ref.shape[2]
+def attend(length_ref, q_ref, first_ref, last_ref, *out_refs):
+    heads, half = q_ref.shape[2], first_ref.shape[2]
+    slots = 2 * half
     latent = out_refs[0].shape[2] - 128
     experts = out_refs[0].shape[1]
     row = lax.broadcasted_iota(jnp.int32, (heads, heads), 0)
     column = lax.broadcasted_iota(jnp.int32, (heads, heads), 1)
     owner = (lax.axis_index("tensor") + row // experts) % 4
-    pick = (column == (row % experts) * 4 + owner).astype(BF)
+    place = row % experts
+    expert = (place // 2 % SIDE * SIDE + place // (2 * SIDE)) * 2 + place % 2
+    pick = (column == expert * 4 + owner).astype(BF)
     q = lax.dot_general(pick, q_ref[0], (((1,), (1,)), ((), ())), preferred_element_type=F32)
-    logits = jnp.dot(q.astype(BF), keys_ref[0], preferred_element_type=F32) * SCORE_SCALE
+    q = q.astype(BF)
+    logits = [
+        jnp.dot(q, keys_ref[0], preferred_element_type=F32) for keys_ref in (first_ref, last_ref)
+    ]
+    logits = jnp.concatenate(logits, axis=1) * SCORE_SCALE
     position = lax.axis_index("tensor") * slots + lax.broadcasted_iota(jnp.int32, (1, slots), 1)
     live = position < length_ref[pl.program_id(0)]
     masked = jnp.where(live, logits, -1e30)
     top = jnp.max(masked, axis=1, keepdims=True)
     expo = jnp.where(live, jnp.exp(masked - top), 0.0)
     total = jnp.sum(expo, axis=1, keepdims=True)
-    numer = lax.dot_general(
-        expo.astype(BF), keys_ref[0, :latent], (((1,), (1,)), ((), ())), preferred_element_type=F32
-    )
+    expo = expo.astype(BF)
+    numer = jnp.zeros((heads, latent), F32)
+    for part, keys_ref in ((expo[:, :half], first_ref), (expo[:, half:], last_ref)):
+        numer = numer + lax.dot_general(
+            part, keys_ref[0, :latent], (((1,), (1,)), ((), ())), preferred_element_type=F32
+        )
     part = (numer / jnp.maximum(total, 1.0)).astype(BF)
     for t, out_ref in enumerate(out_refs):
         out_ref[0, :, :latent] = part[t * experts : (t + 1) * experts]
@@ -278,7 +288,8 @@
         in_specs=[
             SCALAR,
             pl.BlockSpec((1, depth, n_heads), lambda r: (r, 0, 0)),
-            pl.BlockSpec((1, depth, slots), lambda r: (r, 0, 0)),
+            pl.BlockSpec((1, depth, slots // 2), lambda r: (r, 0, 0)),
+            pl.BlockSpec((1, depth, slots // 2), lambda r: (r, 0, 1)),
         ],
         out_specs=[pl.BlockSpec((1, experts, latent + 128), lambda r: (r, 0, 0))] * 4,
         compiler_params=pltpu.CompilerParams(vmem_limit_bytes=58 * 1024 * 1024),
@@ -286,6 +297,7 @@
         cache_lengths,
         jnp.swapaxes(queries, 1, 2),
         jnp.swapaxes(request_latent_cache, 1, 2),
+        jnp.swapaxes(request_latent_cache, 1, 2),
     )
     parts = [parts[0]] + [
         lax.ppermute(parts[s], "tensor", [(i, (i + s) % 4) for i in range(4)]) for s in (1, 2, 3)
@@ -293,7 +305,7 @@
     context = kernel(
         combine, jax.ShapeDtypeStruct((experts, local_requests, latent), BF), parts
     )
-    rows = trade(context, ("y", "x", "core"))
+    rows = trade(context, PLANE + ("core",))
     rows = rows.reshape(experts * local_requests, latent)
     shape = jax.ShapeDtypeStruct
     places, packed = 16, 4 * local_requests

time: 122 us -> 121 us (level)
  no operation moved by 1% of the time
where the time goes in v5:
time: 121 us
  blocking collectives  77.2 us (64%)
  starting transfers between devices  16.1 us (13%)
  waiting for transfers between devices  16.1 us (13%)
  Pallas kernels  9.3 us (8%)
    all_to_all x5, blocking collectives, trade(): return lax.all_to_all(value, axes, 0, 0, tiled=True)  77.2 us
    ppermute x4, starting transfers between devices, along(): return lax.ppermute(value, LINE, [(i, i ^ bits) for i in range(8)])  9.41 us
    ppermute x4, waiting for transfers between devices, along(): return lax.ppermute(value, LINE, [(i, i ^ bits) for i in range(8)])  6.98 us
    ppermute x3, starting transfers between devices, shards(): lax.ppermute(parts[s], 'tensor', [(i, (i + s) % 4) for i in range(4)])  6.28 us
    pallas_call x10, Pallas kernels, kernel(): pl.pallas_call(body, out_shape=shapes, in_specs=specs or [WHOLE] * len(in...  5.84 us
    ppermute x3, waiting for transfers between devices, shards(): lax.ppermute(parts[s], 'tensor', [(i, (i + s) % 4) for i in range(4)])  4.82 us
    ppermute x3, waiting for transfers between devices, other_core(): return lax.ppermute(value, 'core', [(0, 1), (1, 0)])  4.29 us
    pallas_call x1, Pallas kernels, shards(): pl.pallas_call(attend, grid=(local_requests,), out_shape=[pltpu.VMEM((loc...  3.47 us
  transfers between devices with their start and end apart: 10, of which 9 were waited for; matrix products, arithmetic and copies ran while one was open for 0% of the time, Pallas kernels for 2%

profile of v5, /device:TPU:2, one launch (start us, length us, event | category | flops | bytes accessed | tf_op | source)
XLA Modules:
  0.0 120.7 jit_solution(13856581878988624148)
XLA Ops:
  0.7 3.5 %shard_map.131 = (bf16[2,32,640]{2,1,0:T(8,128)(2,1)S(1)}, bf16[2,32,640]{2,1,0:T(8,128)(2,1)S(1)}, bf16[2,32,640]{2,1,0:T(8,128)(2,1)S(1)}, bf16[2,32,640]{2,1,0:T(8,128)(2,1)S(1)}) custom-call(s32[2]{0:T(128)} %length_ref.1, bf16[2,576,128]{2,1,0:T(8,128)(2,1)} %bitcast.11, bf16[2,576,1024]{2,1,0:T(8,128)(2,1)} %bitcast.9, bf16[2,576,1024]{2,1,0:T(8,128)(2,1)} %bitcast.10), custom_call_target="tpu_custom_call" | custom-call | tf_op jit(solution)/shard_map/pallas_call | solution.py:284
  4.1 2.0 %collective-permute-start = (bf16[2,32,640]{2,1,0:T(8,128)(2,1)S(1)}, bf16[2,32,640]{2,1,0:T(8,128)(2,1)S(1)}, u32[]{:S(2)}, u32[]{:S(2)}) collective-permute-start(bf16[2,32,640]{2,1,0:T(8,128)(2,1)S(1)} %get-tuple-element.14), channel_id=1, source_target_pairs={{0,1},{1,2},{2,3},{3,0},{4,5},{5,6},{6,7},{7,4},{8,9},{9,10},{10,1... | collective-permute-start | bytes 245768 | tf_op jit(solution)/shard_map/ppermute | solution.py:303
  6.1 3.3 %collective-permute-start.1 = (bf16[2,32,640]{2,1,0:T(8,128)(2,1)S(1)}, bf16[2,32,640]{2,1,0:T(8,128)(2,1)S(1)}, u32[]{:S(2)}, u32[]{:S(2)}) collective-permute-start(bf16[2,32,640]{2,1,0:T(8,128)(2,1)S(1)} %get-tuple-element.15), channel_id=1, source_target_pairs={{0,2},{1,3},{2,0},{3,1},{4,6},{5,7},{6,4},{7,5},{8,10},{9,11},{10,... | collective-permute-start | bytes 245768 | tf_op jit(solution)/shard_map/ppermute | solution.py:303
  9.4 1.0 collective-permute-start.2
  10.4 1.7 %collective-permute-done.refs_1_ = bf16[2,32,640]{2,1,0:T(8,128)(2,1)S(1)} collective-permute-done((bf16[2,32,640]{2,1,0:T(8,128)(2,1)S(1)}, bf16[2,32,640]{2,1,0:T(8,128)(2,1)S(1)}, u32[]{:S(2)}, u32[]{:S(2)}) %collective-permute-start) | collective-permute-done | bytes 81952 | tf_op jit(solution)/shard_map/ppermute | solution.py:303
  12.1 2.8 %collective-permute-done.1.refs_2_ = bf16[2,32,640]{2,1,0:T(8,128)(2,1)S(1)} collective-permute-done((bf16[2,32,640]{2,1,0:T(8,128)(2,1)S(1)}, bf16[2,32,640]{2,1,0:T(8,128)(2,1)S(1)}, u32[]{:S(2)}, u32[]{:S(2)}) %collective-permute-start.1) | collective-permute-done | bytes 81952 | tf_op jit(solution)/shard_map/ppermute | solution.py:303
  14.9 0.3 collective-permute-done.2.refs_3_
  15.2 0.4 shard_map.132
  15.6 13.8 %all_to_all.25 = bf16[32,2,512]{2,1,0:T(2,128)(2,1)S(1)} all-to-all(bf16[32,2,512]{2,1,0:T(2,128)(2,1)S(1)} %shard_map.132), channel_id=1, replica_groups=mesh['role'=2,'y'=4,'x'=4,'core'=2,'tensor'=4] {'x','y','core'}, dimensions={0} | all-to-all | bytes 131072 | tf_op jit(solution)/shard_map/all_to_all | solution.py:29
  29.4 0.9 shard_map.134
  30.3 0.2 collective-permute-start.3
  30.5 0.9 shard_map.133
  31.5 0.8 collective-permute-done.3
  32.4 13.5 %all_to_all.26.got_ref = bf16[16,8,1792]{2,1,0:T(8,128)(2,1)S(1)} all-to-all(bf16[16,8,1792]{2,1,0:T(8,128)(2,1)S(1)} %fusion.1), channel_id=1, replica_groups=mesh['role'=2,'y'=4,'x'=4,'core'=2,'tensor'=4] {'x','y'}, dimensions={0} | all-to-all | bytes 917504 | tf_op jit(solution)/shard_map/all_to_all | solution.py:29
  46.0 2.0 %collective-permute-start.4 = (bf16[2,7296]{1,0:T(2,128)(2,1)S(1)}, bf16[2,7296]{1,0:T(2,128)(2,1)S(1)}, u32[]{:S(2)}, u32[]{:S(2)}) collective-permute-start(bf16[2,7296]{1,0:T(2,128)(2,1)S(1)} %shard_map.135.here_ref), channel_id=1, source_target_pairs={{0,1},{1,0},{2,3},{3,2},{128,129},{129,128},{130,131},{131,130},{4... | collective-permute-start | bytes 87560 | tf_op jit(solution)/shard_map/ppermute | solution.py:25
  48.0 2.0 %collective-permute-done.4.there_ref = bf16[2,7296]{1,0:T(2,128)(2,1)S(1)} collective-permute-done((bf16[2,7296]{1,0:T(2,128)(2,1)S(1)}, bf16[2,7296]{1,0:T(2,128)(2,1)S(1)}, u32[]{:S(2)}, u32[]{:S(2)}) %collective-permute-start.4) | collective-permute-done | bytes 29216 | tf_op jit(solution)/shard_map/ppermute | solution.py:25
  50.0 6.4 %collective-permute-start.7 = (bf16[2,7296]{1,0:T(2,128)(2,1)S(1)}, bf16[2,7296]{1,0:T(2,128)(2,1)S(1)}, u32[]{:S(2)}, u32[]{:S(2)}) collective-permute-start(bf16[2,7296]{1,0:T(2,128)(2,1)S(1)} %shard_map.136.a_ref), channel_id=1, source_target_pairs={{0,129},{1,128},{2,131},{3,130},{128,1},{129,0},{130,3},{131,2},{4... | collective-permute-start | bytes 87560 | tf_op jit(solution)/shard_map/ppermute | solution.py:25
  56.4 1.0 collective-permute-start.5
  57.4 0.9 collective-permute-done.7.d_ref
  58.3 4.1 %collective-permute-done.6.c_ref = bf16[2,7296]{1,0:T(2,128)(2,1)S(1)} collective-permute-done((bf16[2,7296]{1,0:T(2,128)(2,1)S(1)}, bf16[2,7296]{1,0:T(2,128)(2,1)S(1)}, u32[]{:S(2)}, u32[]{:S(2)}) %collective-permute-start.6) | collective-permute-done | bytes 29216 | tf_op jit(solution)/shard_map/ppermute | solution.py:25
  62.4 0.7 shard_map.137
  63.1 15.9 %all_to_all.27 = bf16[16,8,3712]{2,1,0:T(8,128)(2,1)S(1)} all-to-all(bf16[16,8,3712]{2,1,0:T(8,128)(2,1)S(1)} %get-tuple-element.18), channel_id=1, replica_groups=mesh['role'=2,'y'=4,'x'=4,'core'=2,'tensor'=4] {'x','y'}, dimensions={0} | all-to-all | bytes 1900544 | tf_op jit(solution)/shard_map/all_to_all | solution.py:29
  79.1 0.7 shard_map.138
  79.7 1.8 %collective-permute-done.8.rows_ref = bf16[128,3712]{1,0:T(8,128)(2,1)S(1)} collective-permute-done((bf16[128,3712]{1,0:T(8,128)(2,1)S(1)}, bf16[128,3712]{1,0:T(8,128)(2,1)S(1)}, u32[]{:S(2)}, u32[]{:S(2)}) %collective-permute-start.8) | collective-permute-done | bytes 950304 | tf_op jit(solution)/shard_map/ppermute | solution.py:21
  81.6 1.3 %shard_map.140 = bf16[128,3584]{1,0:T(8,128)(2,1)S(1)} custom-call(bf16[128,3712]{1,0:T(8,128)(2,1)S(1)} %collective-permute-done.8.rows_ref, bf16[1,7168,128]{2,1,0:T(8,128)(2,1)S(1)} %copy-done, bf16[1,7168,128]{2,1,0:T(8,128)(2,1)S(1)} %copy-done.1, bf16[1,128,7168]{2,1,0:T(8,128)(2,1)S(1)} %copy-done.2), custom_call_target="tpu_custom_call" | custom-call | flops 704643072 | bytes 5505024 | tf_op jit(solution)/shard_map/pallas_call | solution.py:253
  82.9 0.2 collective-permute-start.9
  83.1 0.6 shard_map.139
  83.7 1.7 %collective-permute-done.9 = bf16[128,3584]{1,0:T(8,128)(2,1)S(1)} collective-permute-done((bf16[128,3584]{1,0:T(8,128)(2,1)S(1)}, bf16[128,3584]{1,0:T(8,128)(2,1)S(1)}, u32[]{:S(2)}, u32[]{:S(2)}) %collective-permute-start.9) | collective-permute-done | bytes 917536 | tf_op jit(solution)/shard_map/ppermute | solution.py:21
  85.6 19.3 %all_to_all.28.got_ref = bf16[16,8,3584]{2,1,0:T(8,128)(2,1)S(1)} all-to-all(bf16[16,8,3584]{2,1,0:T(8,128)(2,1)S(1)} %fusion), channel_id=1, replica_groups=mesh['role'=2,'y'=4,'x'=4,'core'=2,'tensor'=4] {'x','y'}, dimensions={0} | all-to-all | bytes 1835008 | tf_op jit(solution)/shard_map/all_to_all | solution.py:29
  104.9 0.2 shard_map.141
  105.1 14.8 %all_to_all.29 = bf16[8,2,7168]{2,1,0:T(2,128)(2,1)S(1)} all-to-all(bf16[8,2,7168]{2,1,0:T(2,128)(2,1)S(1)} %shard_map.141), channel_id=1, replica_groups=mesh['role'=2,'y'=4,'x'=4,'core'=2,'tensor'=4] {'role','tensor'}, dimensions={0} | all-to-all | bytes 458752 | tf_op jit(solution)/shard_map/all_to_all | solution.py:29
  119.8 0.8 convert_reduce_fusion
  (26 shorter events, 0.5 us)
Async XLA Ops:
  0.6 28.8 %copy-start.3 = (bf16[128,7168]{1,0:T(8,128)(2,1)S(1)}, bf16[128,7168]{1,0:T(8,128)(2,1)}, u32[]{:S(2)}) copy-start(bf16[128,7168]{1,0:T(8,128)(2,1)} %out_proj_ref.3) | copy-start | bytes 5505028
  0.6 28.8 %copy-start.4 = (bf16[1,512,128]{2,1,0:T(8,128)(2,1)S(1)}, bf16[1,512,128]{2,1,0:T(8,128)(2,1)}, u32[]{:S(2)}) copy-start(bf16[1,512,128]{2,1,0:T(8,128)(2,1)} %value_ref.3) | copy-start | bytes 393220
  4.1 8.0 %collective-permute-start = (bf16[2,32,640]{2,1,0:T(8,128)(2,1)S(1)}, bf16[2,32,640]{2,1,0:T(8,128)(2,1)S(1)}, u32[]{:S(2)}, u32[]{:S(2)}) collective-permute-start(bf16[2,32,640]{2,1,0:T(8,128)(2,1)S(1)} %get-tuple-element.14), channel_id=1, source_target_pairs={{0,1},{1,2},{2,3},{3,0},{4,5},{5,6},{6,7},{7,4},{8,9},{9,10},{10,1... | collective-permute-start | bytes 245768 | tf_op jit(solution)/shard_map/ppermute | solution.py:303
  6.1 8.8 %collective-permute-start.1 = (bf16[2,32,640]{2,1,0:T(8,128)(2,1)S(1)}, bf16[2,32,640]{2,1,0:T(8,128)(2,1)S(1)}, u32[]{:S(2)}, u32[]{:S(2)}) collective-permute-start(bf16[2,32,640]{2,1,0:T(8,128)(2,1)S(1)} %get-tuple-element.15), channel_id=1, source_target_pairs={{0,2},{1,3},{2,0},{3,1},{4,6},{5,7},{6,4},{7,5},{8,10},{9,11},{10,... | collective-permute-start | bytes 245768 | tf_op jit(solution)/shard_map/ppermute | solution.py:303
  9.4 5.8 %collective-permute-start.2 = (bf16[2,32,640]{2,1,0:T(8,128)(2,1)S(1)}, bf16[2,32,640]{2,1,0:T(8,128)(2,1)S(1)}, u32[]{:S(2)}, u32[]{:S(2)}) collective-permute-start(bf16[2,32,640]{2,1,0:T(8,128)(2,1)S(1)} %get-tuple-element.16), channel_id=1, source_target_pairs={{0,3},{1,0},{2,1},{3,2},{4,7},{5,4},{6,5},{7,6},{8,11},{9,8},{10,9... | collective-permute-start | bytes 245768 | tf_op jit(solution)/shard_map/ppermute | solution.py:303
  30.3 1.9 %collective-permute-start.3 = (bf16[128,1792]{1,0:T(8,128)(2,1)S(1)}, bf16[128,1792]{1,0:T(8,128)(2,1)S(1)}, u32[]{:S(2)}, u32[]{:S(2)}) collective-permute-start(bf16[128,1792]{1,0:T(8,128)(2,1)S(1)} %shard_map.134), channel_id=1, source_target_pairs={{0,4},{4,0},{1,5},{5,1},{2,6},{6,2},{3,7},{7,3},{8,12},{12,8},{9,1... | collective-permute-start | bytes 1376264 | tf_op jit(solution)/shard_map/ppermute | solution.py:21
  31.4 14.4 %copy-start.5 = (bf16[2,7168]{1,0:T(2,128)(2,1)S(1)}, bf16[2,7168]{1,0:T(2,128)(2,1)}, u32[]{:S(2)}) copy-start(bf16[2,7168]{1,0:T(2,128)(2,1)} %extra_ref.1) | copy-start | bytes 86020
  31.5 14.4 %copy-start.7 = (s32[2,8]{1,0:T(2,128)S(1)}, s32[2,8]{1,0:T(2,128)}, u32[]{:S(2)}) copy-start(s32[2,8]{1,0:T(2,128)} %ids_ref.1) | copy-start | bytes 196
  31.5 14.4 %copy-start.8 = (bf16[2,8]{1,0:T(2,128)(2,1)S(1)}, bf16[2,8]{1,0:T(2,128)(2,1)}, u32[]{:S(2)}) copy-start(bf16[2,8]{1,0:T(2,128)(2,1)} %weights_ref.1) | copy-start | bytes 100
  31.5 31.0 %copy-start.6 = (bf16[7168]{0:T(1024)(128)(2,1)S(1)}, bf16[7168]{0:T(1024)(128)(2,1)}, u32[]{:S(2)}) copy-start(bf16[7168]{0:T(1024)(128)(2,1)} %gain_ref.1) | copy-start | bytes 43012
  32.2 46.8 %copy-start.1 = (bf16[1,7168,128]{2,1,0:T(8,128)(2,1)S(1)}, bf16[1,7168,128]{2,1,0:T(8,128)(2,1)}, u32[]{:S(2)}) copy-start(bf16[1,7168,128]{2,1,0:T(8,128)(2,1)} %up_ref.3) | copy-start | bytes 5505028
  32.4 46.7 %copy-start = (bf16[1,7168,128]{2,1,0:T(8,128)(2,1)S(1)}, bf16[1,7168,128]{2,1,0:T(8,128)(2,1)}, u32[]{:S(2)}) copy-start(bf16[1,7168,128]{2,1,0:T(8,128)(2,1)} %gate_ref.3) | copy-start | bytes 5505028
  46.0 4.0 %collective-permute-start.4 = (bf16[2,7296]{1,0:T(2,128)(2,1)S(1)}, bf16[2,7296]{1,0:T(2,128)(2,1)S(1)}, u32[]{:S(2)}, u32[]{:S(2)}) collective-permute-start(bf16[2,7296]{1,0:T(2,128)(2,1)S(1)} %shard_map.135.here_ref), channel_id=1, source_target_pairs={{0,1},{1,0},{2,3},{3,2},{128,129},{129,128},{130,131},{131,130},{4... | collective-permute-start | bytes 87560 | tf_op jit(solution)/shard_map/ppermute | solution.py:25
  50.0 8.3 %collective-permute-start.7 = (bf16[2,7296]{1,0:T(2,128)(2,1)S(1)}, bf16[2,7296]{1,0:T(2,128)(2,1)S(1)}, u32[]{:S(2)}, u32[]{:S(2)}) collective-permute-start(bf16[2,7296]{1,0:T(2,128)(2,1)S(1)} %shard_map.136.a_ref), channel_id=1, source_target_pairs={{0,129},{1,128},{2,131},{3,130},{128,1},{129,0},{130,3},{131,2},{4... | collective-permute-start | bytes 87560 | tf_op jit(solution)/shard_map/ppermute | solution.py:25
  56.4 6.0 %collective-permute-start.6 = (bf16[2,7296]{1,0:T(2,128)(2,1)S(1)}, bf16[2,7296]{1,0:T(2,128)(2,1)S(1)}, u32[]{:S(2)}, u32[]{:S(2)}) collective-permute-start(bf16[2,7296]{1,0:T(2,128)(2,1)S(1)} %shard_map.136.a_ref), channel_id=1, source_target_pairs={{0,130},{1,131},{2,128},{3,129},{128,2},{129,3},{130,0},{131,1},{4... | collective-permute-start | bytes 87560 | tf_op jit(solution)/shard_map/ppermute | solution.py:25
  56.4 6.0 %collective-permute-start.5 = (bf16[2,7296]{1,0:T(2,128)(2,1)S(1)}, bf16[2,7296]{1,0:T(2,128)(2,1)S(1)}, u32[]{:S(2)}, u32[]{:S(2)}) collective-permute-start(bf16[2,7296]{1,0:T(2,128)(2,1)S(1)} %shard_map.136.a_ref), channel_id=1, source_target_pairs={{0,2},{1,3},{2,0},{3,1},{128,130},{129,131},{130,128},{131,129},{4... | collective-permute-start | bytes 87560 | tf_op jit(solution)/shard_map/ppermute | solution.py:25
  79.0 2.5 %copy-start.2 = (bf16[1,128,7168]{2,1,0:T(8,128)(2,1)S(1)}, bf16[1,128,7168]{2,1,0:T(8,128)(2,1)}, u32[]{:S(2)}) copy-start(bf16[1,128,7168]{2,1,0:T(8,128)(2,1)} %down_ref.3) | copy-start | bytes 5505028
  79.0 2.5 %collective-permute-start.8 = (bf16[128,3712]{1,0:T(8,128)(2,1)S(1)}, bf16[128,3712]{1,0:T(8,128)(2,1)S(1)}, u32[]{:S(2)}, u32[]{:S(2)}) collective-permute-start(bf16[128,3712]{1,0:T(8,128)(2,1)S(1)} %bitcast.7), channel_id=1, source_target_pairs={{0,4},{4,0},{1,5},{5,1},{2,6},{6,2},{3,7},{7,3},{8,12},{12,8},{9,1... | collective-permute-start | bytes 2850824 | tf_op jit(solution)/shard_map/ppermute | solution.py:21
  82.9 2.6 %collective-permute-start.9 = (bf16[128,3584]{1,0:T(8,128)(2,1)S(1)}, bf16[128,3584]{1,0:T(8,128)(2,1)S(1)}, u32[]{:S(2)}, u32[]{:S(2)}) collective-permute-start(bf16[128,3584]{1,0:T(8,128)(2,1)S(1)} %shard_map.140), channel_id=1, source_target_pairs={{0,4},{4,0},{1,5},{5,1},{2,6},{6,2},{3,7},{7,3},{8,12},{12,8},{9,1... | collective-permute-start | bytes 2752520 | tf_op jit(solution)/shard_map/ppermute | solution.py:21

commit v6 on v5

--- a/solution.py
+++ b/solution.py
@@ -191,6 +191,10 @@
             out_ref[4 + t, :, columns] = high
 
 
+def line_sum(got_ref, out_ref):
+    out_ref[...] = add_places(got_ref)
+
+
 def which_half(rows):
     return lax.broadcasted_iota(jnp.int32, (rows, 1), 0) // 4 % 2
 
@@ -375,7 +379,7 @@
         scratch=[pltpu.VMEM((packed, middle), F32)],
     )
     acc = trade(acc, LINE)
-    routed = jnp.sum(acc.astype(F32), axis=0)
+    routed = kernel(line_sum, shape((local_requests, width), F32), [acc])
     return (attended, routed)
 
 

time: 121 us -> 121 us (level)
    pallas_call x10 -> x11, Pallas kernels: 5.84 us -> 6.49 us  [kernel(): pl.pallas_call(body, out_shape=shapes, in_specs=specs or [WHOLE] * len(in...]
where the time goes in v6:
time: 121 us
  blocking collectives  77.2 us (64%)
  starting transfers between devices  16.1 us (13%)
  waiting for transfers between devices  16.1 us (13%)
  Pallas kernels  9.96 us (8%)
    all_to_all x5, blocking collectives, trade(): return lax.all_to_all(value, axes, 0, 0, tiled=True)  77.2 us
    ppermute x4, starting transfers between devices, along(): return lax.ppermute(value, LINE, [(i, i ^ bits) for i in range(8)])  9.41 us
    ppermute x4, waiting for transfers between devices, along(): return lax.ppermute(value, LINE, [(i, i ^ bits) for i in range(8)])  6.98 us
    pallas_call x11, Pallas kernels, kernel(): pl.pallas_call(body, out_shape=shapes, in_specs=specs or [WHOLE] * len(in...  6.49 us
    ppermute x3, starting transfers between devices, shards(): lax.ppermute(parts[s], 'tensor', [(i, (i + s) % 4) for i in range(4)])  6.28 us
    ppermute x3, waiting for transfers between devices, shards(): lax.ppermute(parts[s], 'tensor', [(i, (i + s) % 4) for i in range(4)])  4.82 us
    ppermute x3, waiting for transfers between devices, other_core(): return lax.ppermute(value, 'core', [(0, 1), (1, 0)])  4.29 us
    pallas_call x1, Pallas kernels, shards(): pl.pallas_call(attend, grid=(local_requests,), out_shape=[pltpu.VMEM((loc...  3.47 us
  transfers between devices with their start and end apart: 10, of which 9 were waited for; matrix products, arithmetic and copies ran while one was open for 0% of the time, Pallas kernels for 2%

profile of v6, /device:TPU:2, one launch (start us, length us, event | category | flops | bytes accessed | tf_op | source)
XLA Modules:
  0.0 120.5 jit_solution(14467830660105632140)
XLA Ops:
  0.7 3.5 %shard_map.131 = (bf16[2,32,640]{2,1,0:T(8,128)(2,1)S(1)}, bf16[2,32,640]{2,1,0:T(8,128)(2,1)S(1)}, bf16[2,32,640]{2,1,0:T(8,128)(2,1)S(1)}, bf16[2,32,640]{2,1,0:T(8,128)(2,1)S(1)}) custom-call(s32[2]{0:T(128)} %length_ref.1, bf16[2,576,128]{2,1,0:T(8,128)(2,1)} %bitcast.11, bf16[2,576,1024]{2,1,0:T(8,128)(2,1)} %bitcast.9, bf16[2,576,1024]{2,1,0:T(8,128)(2,1)} %bitcast.10), custom_call_target="tpu_custom_call" | custom-call | tf_op jit(solution)/shard_map/pallas_call | solution.py:288
  4.1 2.0 %collective-permute-start = (bf16[2,32,640]{2,1,0:T(8,128)(2,1)S(1)}, bf16[2,32,640]{2,1,0:T(8,128)(2,1)S(1)}, u32[]{:S(2)}, u32[]{:S(2)}) collective-permute-start(bf16[2,32,640]{2,1,0:T(8,128)(2,1)S(1)} %get-tuple-element.14), channel_id=1, source_target_pairs={{0,1},{1,2},{2,3},{3,0},{4,5},{5,6},{6,7},{7,4},{8,9},{9,10},{10,1... | collective-permute-start | bytes 245768 | tf_op jit(solution)/shard_map/ppermute | solution.py:307
  6.1 3.3 %collective-permute-start.1 = (bf16[2,32,640]{2,1,0:T(8,128)(2,1)S(1)}, bf16[2,32,640]{2,1,0:T(8,128)(2,1)S(1)}, u32[]{:S(2)}, u32[]{:S(2)}) collective-permute-start(bf16[2,32,640]{2,1,0:T(8,128)(2,1)S(1)} %get-tuple-element.15), channel_id=1, source_target_pairs={{0,2},{1,3},{2,0},{3,1},{4,6},{5,7},{6,4},{7,5},{8,10},{9,11},{10,... | collective-permute-start | bytes 245768 | tf_op jit(solution)/shard_map/ppermute | solution.py:307
  9.4 1.0 collective-permute-start.2
  10.4 1.7 %collective-permute-done.refs_1_ = bf16[2,32,640]{2,1,0:T(8,128)(2,1)S(1)} collective-permute-done((bf16[2,32,640]{2,1,0:T(8,128)(2,1)S(1)}, bf16[2,32,640]{2,1,0:T(8,128)(2,1)S(1)}, u32[]{:S(2)}, u32[]{:S(2)}) %collective-permute-start) | collective-permute-done | bytes 81952 | tf_op jit(solution)/shard_map/ppermute | solution.py:307
  12.1 2.8 %collective-permute-done.1.refs_2_ = bf16[2,32,640]{2,1,0:T(8,128)(2,1)S(1)} collective-permute-done((bf16[2,32,640]{2,1,0:T(8,128)(2,1)S(1)}, bf16[2,32,640]{2,1,0:T(8,128)(2,1)S(1)}, u32[]{:S(2)}, u32[]{:S(2)}) %collective-permute-start.1) | collective-permute-done | bytes 81952 | tf_op jit(solution)/shard_map/ppermute | solution.py:307
  14.9 0.3 collective-permute-done.2.refs_3_
  15.2 0.4 shard_map.132
  15.6 13.8 %all_to_all.25 = bf16[32,2,512]{2,1,0:T(2,128)(2,1)S(1)} all-to-all(bf16[32,2,512]{2,1,0:T(2,128)(2,1)S(1)} %shard_map.132), channel_id=1, replica_groups=mesh['role'=2,'y'=4,'x'=4,'core'=2,'tensor'=4] {'x','y','core'}, dimensions={0} | all-to-all | bytes 131072 | tf_op jit(solution)/shard_map/all_to_all | solution.py:29
  29.4 0.9 shard_map.134
  30.3 0.2 collective-permute-start.3
  30.5 0.9 shard_map.133
  31.5 0.8 collective-permute-done.3
  32.4 13.5 %all_to_all.26.got_ref = bf16[16,8,1792]{2,1,0:T(8,128)(2,1)S(1)} all-to-all(bf16[16,8,1792]{2,1,0:T(8,128)(2,1)S(1)} %fusion.1), channel_id=1, replica_groups=mesh['role'=2,'y'=4,'x'=4,'core'=2,'tensor'=4] {'x','y'}, dimensions={0} | all-to-all | bytes 917504 | tf_op jit(solution)/shard_map/all_to_all | solution.py:29
  46.0 2.0 %collective-permute-start.4 = (bf16[2,7296]{1,0:T(2,128)(2,1)S(1)}, bf16[2,7296]{1,0:T(2,128)(2,1)S(1)}, u32[]{:S(2)}, u32[]{:S(2)}) collective-permute-start(bf16[2,7296]{1,0:T(2,128)(2,1)S(1)} %shard_map.135.here_ref), channel_id=1, source_target_pairs={{0,1},{1,0},{2,3},{3,2},{128,129},{129,128},{130,131},{131,130},{4... | collective-permute-start | bytes 87560 | tf_op jit(solution)/shard_map/ppermute | solution.py:25
  48.0 2.0 %collective-permute-done.4.there_ref = bf16[2,7296]{1,0:T(2,128)(2,1)S(1)} collective-permute-done((bf16[2,7296]{1,0:T(2,128)(2,1)S(1)}, bf16[2,7296]{1,0:T(2,128)(2,1)S(1)}, u32[]{:S(2)}, u32[]{:S(2)}) %collective-permute-start.4) | collective-permute-done | bytes 29216 | tf_op jit(solution)/shard_map/ppermute | solution.py:25
  50.0 6.4 %collective-permute-start.7 = (bf16[2,7296]{1,0:T(2,128)(2,1)S(1)}, bf16[2,7296]{1,0:T(2,128)(2,1)S(1)}, u32[]{:S(2)}, u32[]{:S(2)}) collective-permute-start(bf16[2,7296]{1,0:T(2,128)(2,1)S(1)} %shard_map.136.a_ref), channel_id=1, source_target_pairs={{0,129},{1,128},{2,131},{3,130},{128,1},{129,0},{130,3},{131,2},{4... | collective-permute-start | bytes 87560 | tf_op jit(solution)/shard_map/ppermute | solution.py:25
  56.4 1.0 collective-permute-start.5
  57.4 0.9 collective-permute-done.7.d_ref
  58.3 4.1 %collective-permute-done.6.c_ref = bf16[2,7296]{1,0:T(2,128)(2,1)S(1)} collective-permute-done((bf16[2,7296]{1,0:T(2,128)(2,1)S(1)}, bf16[2,7296]{1,0:T(2,128)(2,1)S(1)}, u32[]{:S(2)}, u32[]{:S(2)}) %collective-permute-start.6) | collective-permute-done | bytes 29216 | tf_op jit(solution)/shard_map/ppermute | solution.py:25
  62.4 0.7 shard_map.137
  63.1 15.9 %all_to_all.27 = bf16[16,8,3712]{2,1,0:T(8,128)(2,1)S(1)} all-to-all(bf16[16,8,3712]{2,1,0:T(8,128)(2,1)S(1)} %get-tuple-element.18), channel_id=1, replica_groups=mesh['role'=2,'y'=4,'x'=4,'core'=2,'tensor'=4] {'x','y'}, dimensions={0} | all-to-all | bytes 1900544 | tf_op jit(solution)/shard_map/all_to_all | solution.py:29
  79.1 0.7 shard_map.138
  79.7 1.8 %collective-permute-done.8.rows_ref = bf16[128,3712]{1,0:T(8,128)(2,1)S(1)} collective-permute-done((bf16[128,3712]{1,0:T(8,128)(2,1)S(1)}, bf16[128,3712]{1,0:T(8,128)(2,1)S(1)}, u32[]{:S(2)}, u32[]{:S(2)}) %collective-permute-start.8) | collective-permute-done | bytes 950304 | tf_op jit(solution)/shard_map/ppermute | solution.py:21
  81.6 1.3 %shard_map.140 = bf16[128,3584]{1,0:T(8,128)(2,1)S(1)} custom-call(bf16[128,3712]{1,0:T(8,128)(2,1)S(1)} %collective-permute-done.8.rows_ref, bf16[1,7168,128]{2,1,0:T(8,128)(2,1)S(1)} %copy-done, bf16[1,7168,128]{2,1,0:T(8,128)(2,1)S(1)} %copy-done.1, bf16[1,128,7168]{2,1,0:T(8,128)(2,1)S(1)} %copy-done.2), custom_call_target="tpu_custom_call" | custom-call | flops 704643072 | bytes 5505024 | tf_op jit(solution)/shard_map/pallas_call | solution.py:257
  82.9 0.2 collective-permute-start.9
  83.1 0.6 shard_map.139
  83.7 1.7 %collective-permute-done.9 = bf16[128,3584]{1,0:T(8,128)(2,1)S(1)} collective-permute-done((bf16[128,3584]{1,0:T(8,128)(2,1)S(1)}, bf16[128,3584]{1,0:T(8,128)(2,1)S(1)}, u32[]{:S(2)}, u32[]{:S(2)}) %collective-permute-start.9) | collective-permute-done | bytes 917536 | tf_op jit(solution)/shard_map/ppermute | solution.py:21
  85.6 19.3 %all_to_all.28.got_ref = bf16[16,8,3584]{2,1,0:T(8,128)(2,1)S(1)} all-to-all(bf16[16,8,3584]{2,1,0:T(8,128)(2,1)S(1)} %fusion), channel_id=1, replica_groups=mesh['role'=2,'y'=4,'x'=4,'core'=2,'tensor'=4] {'x','y'}, dimensions={0} | all-to-all | bytes 1835008 | tf_op jit(solution)/shard_map/all_to_all | solution.py:29
  104.9 0.2 shard_map.141
  105.1 14.8 %all_to_all.29.got_ref = bf16[8,2,7168]{2,1,0:T(2,128)(2,1)S(1)} all-to-all(bf16[8,2,7168]{2,1,0:T(2,128)(2,1)S(1)} %shard_map.141), channel_id=1, replica_groups=mesh['role'=2,'y'=4,'x'=4,'core'=2,'tensor'=4] {'role','tensor'}, dimensions={0} | all-to-all | bytes 458752 | tf_op jit(solution)/shard_map/all_to_all | solution.py:29
  119.8 0.7 shard_map.142
  (26 shorter events, 0.5 us)
Async XLA Ops:
  0.6 28.8 %copy-start.3 = (bf16[128,7168]{1,0:T(8,128)(2,1)S(1)}, bf16[128,7168]{1,0:T(8,128)(2,1)}, u32[]{:S(2)}) copy-start(bf16[128,7168]{1,0:T(8,128)(2,1)} %out_proj_ref.3) | copy-start | bytes 5505028
  0.6 28.8 %copy-start.4 = (bf16[1,512,128]{2,1,0:T(8,128)(2,1)S(1)}, bf16[1,512,128]{2,1,0:T(8,128)(2,1)}, u32[]{:S(2)}) copy-start(bf16[1,512,128]{2,1,0:T(8,128)(2,1)} %value_ref.3) | copy-start | bytes 393220
  4.1 8.0 %collective-permute-start = (bf16[2,32,640]{2,1,0:T(8,128)(2,1)S(1)}, bf16[2,32,640]{2,1,0:T(8,128)(2,1)S(1)}, u32[]{:S(2)}, u32[]{:S(2)}) collective-permute-start(bf16[2,32,640]{2,1,0:T(8,128)(2,1)S(1)} %get-tuple-element.14), channel_id=1, source_target_pairs={{0,1},{1,2},{2,3},{3,0},{4,5},{5,6},{6,7},{7,4},{8,9},{9,10},{10,1... | collective-permute-start | bytes 245768 | tf_op jit(solution)/shard_map/ppermute | solution.py:307
  6.1 8.8 %collective-permute-start.1 = (bf16[2,32,640]{2,1,0:T(8,128)(2,1)S(1)}, bf16[2,32,640]{2,1,0:T(8,128)(2,1)S(1)}, u32[]{:S(2)}, u32[]{:S(2)}) collective-permute-start(bf16[2,32,640]{2,1,0:T(8,128)(2,1)S(1)} %get-tuple-element.15), channel_id=1, source_target_pairs={{0,2},{1,3},{2,0},{3,1},{4,6},{5,7},{6,4},{7,5},{8,10},{9,11},{10,... | collective-permute-start | bytes 245768 | tf_op jit(solution)/shard_map/ppermute | solution.py:307
  9.4 5.8 %collective-permute-start.2 = (bf16[2,32,640]{2,1,0:T(8,128)(2,1)S(1)}, bf16[2,32,640]{2,1,0:T(8,128)(2,1)S(1)}, u32[]{:S(2)}, u32[]{:S(2)}) collective-permute-start(bf16[2,32,640]{2,1,0:T(8,128)(2,1)S(1)} %get-tuple-element.16), channel_id=1, source_target_pairs={{0,3},{1,0},{2,1},{3,2},{4,7},{5,4},{6,5},{7,6},{8,11},{9,8},{10,9... | collective-permute-start | bytes 245768 | tf_op jit(solution)/shard_map/ppermute | solution.py:307
  30.3 1.9 %collective-permute-start.3 = (bf16[128,1792]{1,0:T(8,128)(2,1)S(1)}, bf16[128,1792]{1,0:T(8,128)(2,1)S(1)}, u32[]{:S(2)}, u32[]{:S(2)}) collective-permute-start(bf16[128,1792]{1,0:T(8,128)(2,1)S(1)} %shard_map.134), channel_id=1, source_target_pairs={{0,4},{4,0},{1,5},{5,1},{2,6},{6,2},{3,7},{7,3},{8,12},{12,8},{9,1... | collective-permute-start | bytes 1376264 | tf_op jit(solution)/shard_map/ppermute | solution.py:21
  31.4 14.4 %copy-start.5 = (bf16[2,7168]{1,0:T(2,128)(2,1)S(1)}, bf16[2,7168]{1,0:T(2,128)(2,1)}, u32[]{:S(2)}) copy-start(bf16[2,7168]{1,0:T(2,128)(2,1)} %extra_ref.1) | copy-start | bytes 86020
  31.5 14.4 %copy-start.7 = (s32[2,8]{1,0:T(2,128)S(1)}, s32[2,8]{1,0:T(2,128)}, u32[]{:S(2)}) copy-start(s32[2,8]{1,0:T(2,128)} %ids_ref.1) | copy-start | bytes 196
  31.5 14.4 %copy-start.8 = (bf16[2,8]{1,0:T(2,128)(2,1)S(1)}, bf16[2,8]{1,0:T(2,128)(2,1)}, u32[]{:S(2)}) copy-start(bf16[2,8]{1,0:T(2,128)(2,1)} %weights_ref.1) | copy-start | bytes 100
  31.5 31.0 %copy-start.6 = (bf16[7168]{0:T(1024)(128)(2,1)S(1)}, bf16[7168]{0:T(1024)(128)(2,1)}, u32[]{:S(2)}) copy-start(bf16[7168]{0:T(1024)(128)(2,1)} %gain_ref.1) | copy-start | bytes 43012
  32.2 46.8 %copy-start.1 = (bf16[1,7168,128]{2,1,0:T(8,128)(2,1)S(1)}, bf16[1,7168,128]{2,1,0:T(8,128)(2,1)}, u32[]{:S(2)}) copy-start(bf16[1,7168,128]{2,1,0:T(8,128)(2,1)} %up_ref.3) | copy-start | bytes 5505028
  32.4 46.7 %copy-start = (bf16[1,7168,128]{2,1,0:T(8,128)(2,1)S(1)}, bf16[1,7168,128]{2,1,0:T(8,128)(2,1)}, u32[]{:S(2)}) copy-start(bf16[1,7168,128]{2,1,0:T(8,128)(2,1)} %gate_ref.3) | copy-start | bytes 5505028
  46.0 4.0 %collective-permute-start.4 = (bf16[2,7296]{1,0:T(2,128)(2,1)S(1)}, bf16[2,7296]{1,0:T(2,128)(2,1)S(1)}, u32[]{:S(2)}, u32[]{:S(2)}) collective-permute-start(bf16[2,7296]{1,0:T(2,128)(2,1)S(1)} %shard_map.135.here_ref), channel_id=1, source_target_pairs={{0,1},{1,0},{2,3},{3,2},{128,129},{129,128},{130,131},{131,130},{4... | collective-permute-start | bytes 87560 | tf_op jit(solution)/shard_map/ppermute | solution.py:25
  50.0 8.3 %collective-permute-start.7 = (bf16[2,7296]{1,0:T(2,128)(2,1)S(1)}, bf16[2,7296]{1,0:T(2,128)(2,1)S(1)}, u32[]{:S(2)}, u32[]{:S(2)}) collective-permute-start(bf16[2,7296]{1,0:T(2,128)(2,1)S(1)} %shard_map.136.a_ref), channel_id=1, source_target_pairs={{0,129},{1,128},{2,131},{3,130},{128,1},{129,0},{130,3},{131,2},{4... | collective-permute-start | bytes 87560 | tf_op jit(solution)/shard_map/ppermute | solution.py:25
  56.4 6.0 %collective-permute-start.6 = (bf16[2,7296]{1,0:T(2,128)(2,1)S(1)}, bf16[2,7296]{1,0:T(2,128)(2,1)S(1)}, u32[]{:S(2)}, u32[]{:S(2)}) collective-permute-start(bf16[2,7296]{1,0:T(2,128)(2,1)S(1)} %shard_map.136.a_ref), channel_id=1, source_target_pairs={{0,130},{1,131},{2,128},{3,129},{128,2},{129,3},{130,0},{131,1},{4... | collective-permute-start | bytes 87560 | tf_op jit(solution)/shard_map/ppermute | solution.py:25
  56.4 6.0 %collective-permute-start.5 = (bf16[2,7296]{1,0:T(2,128)(2,1)S(1)}, bf16[2,7296]{1,0:T(2,128)(2,1)S(1)}, u32[]{:S(2)}, u32[]{:S(2)}) collective-permute-start(bf16[2,7296]{1,0:T(2,128)(2,1)S(1)} %shard_map.136.a_ref), channel_id=1, source_target_pairs={{0,2},{1,3},{2,0},{3,1},{128,130},{129,131},{130,128},{131,129},{4... | collective-permute-start | bytes 87560 | tf_op jit(solution)/shard_map/ppermute | solution.py:25
  79.0 2.5 %copy-start.2 = (bf16[1,128,7168]{2,1,0:T(8,128)(2,1)S(1)}, bf16[1,128,7168]{2,1,0:T(8,128)(2,1)}, u32[]{:S(2)}) copy-start(bf16[1,128,7168]{2,1,0:T(8,128)(2,1)} %down_ref.3) | copy-start | bytes 5505028
  79.0 2.5 %collective-permute-start.8 = (bf16[128,3712]{1,0:T(8,128)(2,1)S(1)}, bf16[128,3712]{1,0:T(8,128)(2,1)S(1)}, u32[]{:S(2)}, u32[]{:S(2)}) collective-permute-start(bf16[128,3712]{1,0:T(8,128)(2,1)S(1)} %bitcast.7), channel_id=1, source_target_pairs={{0,4},{4,0},{1,5},{5,1},{2,6},{6,2},{3,7},{7,3},{8,12},{12,8},{9,1... | collective-permute-start | bytes 2850824 | tf_op jit(solution)/shard_map/ppermute | solution.py:21
  82.9 2.6 %collective-permute-start.9 = (bf16[128,3584]{1,0:T(8,128)(2,1)S(1)}, bf16[128,3584]{1,0:T(8,128)(2,1)S(1)}, u32[]{:S(2)}, u32[]{:S(2)}) collective-permute-start(bf16[128,3584]{1,0:T(8,128)(2,1)S(1)} %shard_map.140), channel_id=1, source_target_pairs={{0,4},{4,0},{1,5},{5,1},{2,6},{6,2},{3,7},{7,3},{8,12},{12,8},{9,1... | collective-permute-start | bytes 2752520 | tf_op jit(solution)/shard_map/ppermute | solution.py:21
